TPU v7x, 128 devices: a whole 4x4x4 slice. The times are simulated.
128 devices in a mesh: out: 8 (over x, z_lo), in: 16 (over y, z_hi, core).
Axes of the slice: x: 4, y: 4, z: 4 (z_hi: 2, z_lo: 2; z = z_hi * 2 + z_lo), core: 2. Of those that a mesh axis runs over, the one named last changes fastest.
Arguments:
- out_grads: bfloat16 [1024, 28672], P('out', 'in'), may hold values from -2 to 2
- layer_inputs: bfloat16 [1024, 8192], P('in', 'out'), may hold values from -2 to 2
- basis_out: bfloat16 [28672, 28672], P('in', 'out'), may hold values from -0.03125 to 0.03125
- basis_in: bfloat16 [8192, 8192], P('out', 'in'), may hold values from -0.0625 to 0.0625
Outputs:
- eigen_correction: float32 [28672, 8192], P('out', 'in')
All inputs are finite; a program needn't handle non-finite values.
Results may differ from a plain program's by a relative error of at most 0.0029.
Values may be sent and summed in bfloat16 or wider, within the bound.
No kernel may reach another device: no remote copies, remote signals or barrier semaphores. Data moves between devices by JAX's collectives and lax.ppermute only.
A program may use at most 128 MiB of HBM per device.

v0:
```python
import jax
import jax.numpy as jnp
from jax import lax
from jax.sharding import PartitionSpec as P

SEQ_LEN = 128


def body(out_grads, layer_inputs, basis_out, basis_in):
    tokens = out_grads.shape[0] * lax.axis_size("out")
    partial_sums = jnp.dot(
        lax.all_gather(out_grads, "out", axis=0, tiled=True),
        basis_out,
        preferred_element_type=jnp.float32,
    )
    rotated_grads = lax.psum(partial_sums, "in").astype(jnp.bfloat16)
    all_inputs = lax.all_gather(layer_inputs, "in", axis=0, tiled=True)
    own_inputs = lax.psum_scatter(
        jnp.dot(all_inputs, basis_in, preferred_element_type=jnp.float32),
        "out",
        scatter_dimension=0,
        tiled=True,
    )
    rotated_inputs = lax.all_gather(own_inputs.astype(jnp.bfloat16), "out", axis=0, tiled=True)

    def add_sequence(index, total):
        first = index * SEQ_LEN
        grad_rows = lax.dynamic_slice_in_dim(rotated_grads, first, SEQ_LEN, 0)
        input_rows = lax.dynamic_slice_in_dim(rotated_inputs, first, SEQ_LEN, 0)
        product = jnp.einsum("tk,tl->kl", grad_rows, input_rows, preferred_element_type=jnp.float32)
        return total + product * product

    shape_out = (rotated_grads.shape[1], rotated_inputs.shape[1])
    total = lax.fori_loop(0, tokens // SEQ_LEN, add_sequence, jnp.zeros(shape_out, jnp.float32))
    return total / jnp.float32(tokens // SEQ_LEN)


def solution(mesh):
    return jax.shard_map(
        body,
        mesh=mesh,
        in_specs=(P("out", "in"), P("in", "out"), P("in", "out"), P("out", "in")),
        out_specs=P("out", "in"),
        check_vma=False,
    )
```

profile of v0, /device:TPU:1, one launch (start us, length us, event | category | flops | bytes accessed | tf_op | source)
XLA Modules:
  0.0 605.5 jit_solution(8199221020892551616)
XLA Ops:
  6.5 0.7 all-gather.6.cloned.1.call-update
  7.3 0.0 all-gather.4.cloned.1.call-start
  7.3 0.7 all-gather.4.cloned.1.call-update
  8.0 0.0 reduce-scatter.2.cloned.1.call-start
  8.1 53.8 %all-gather.6.cloned.1.call-done = bf16[1024,1024]{1,0:T(8,128)(2,1)} async-done(((bf16[64,1024]{1,0:T(8,128)(2,1)}), bf16[1024,1024]{1,0:T(8,128)(2,1)}) %all-gather.6.cloned.1.call-update) | async-done | bytes 2097168 | tf_op jit(solution)/shard_map/all_gather | solution.py:17
  61.9 4.1 fusion.4
  66.0 0.0 reduce-scatter.2.cloned.1.call-update
  66.0 0.0 all-gather.8.cloned.1.call-start
  66.1 75.5 %all-gather.4.cloned.1.call-done = bf16[1024,1792]{1,0:T(8,128)(2,1)} async-done(((bf16[128,1792]{1,0:T(8,128)(2,1)}), bf16[1024,1792]{1,0:T(8,128)(2,1)}) %all-gather.4.cloned.1.call-update) | async-done | bytes 3670032 | tf_op jit(solution)/shard_map/all_gather | solution.py:12
  141.6 20.5 %fusion.3 = f32[1024,3584]{1,0:T(8,128)} fusion(bf16[1024,1792]{1,0:T(8,128)(2,1)} %all-gather.4.cloned.1.call-done, bf16[1792,3584]{1,0:T(8,128)(2,1)} %param.8), kind=kOutput, calls=%fused_computation.6 | convolution fusion | flops 13153337344 | bytes 31195136 | tf_op jit(solution)/shard_map/dot_general | solution.py:11
  162.0 33.7 %reduce-scatter.2.cloned.1.call-done = f32[128,512]{1,0:T(8,128)} async-done(((f32[1024,512]{1,0:T(8,128)}), f32[128,512]{1,0:T(8,128)}) %reduce-scatter.2.cloned.1.call-update) | async-done | bytes 262160 | tf_op jit(solution)/shard_map/reduce_scatter | solution.py:18
  195.8 1.6 convert_element_type.7
  197.4 0.0 all-gather.8.cloned.1.call-update
  197.4 335.6 %all-reduce.1 = bf16[1024,3584]{1,0:T(8,128)(2,1)} all-reduce(f32[1024,3584]{1,0:T(8,128)} %fusion.3), channel_id=1, replica_groups=mesh['out'=8,'in'=16] {'in'}, use_global_device_ids=true, to_apply=%region_0.0 | all-reduce | flops 3670016 | bytes 22020096 | tf_op jit(solution)/shard_map/psum | solution.py:16
  533.0 58.9 %while.14 = (s32[]{:T(128)}, f32[3584,512]{1,0:T(8,128)}, bf16[1024,3584]{1,0:T(8,128)(2,1)}, bf16[1024,512]{1,0:T(8,128)(2,1)}, s32[]{:T(128)}, /*index=5*/s32[]{:T(128)}, s32[]{:T(128)}, s32[]{:T(128)}) while((s32[]{:T(128)}, f32[3584,512]{1,0:T(8,128)}, bf16[1024,3584]{1,0:T(8,128)(2,1)}, bf16[1024,512]{1,0:T(8,128)(2,1)}, ...), condition=%wide.region_3.0_spmd.clone, body=%wide.region_2.0_spmd.clone.sunk | while | flops 475267072 | bytes 15730316 | solution.py:34
  533.0 5.4 select_add_fusion.2
  538.3 7.7 %select_add_fusion.2 = f32[3584,512]{1,0:T(8,128)} fusion(f32[3584,512]{1,0:T(8,128)} %get-tuple-element.142, pred[]{:T(512)S(6)} %compare.3, bf16[1024,3584]{1,0:T(8,128)(2,1)} %get-tuple-element.151, s32[]{:T(128)S(6)} %select_n.10, bf16[1024,512]{1,0:T(8,128)(2,1)} %get-tuple-element.152), kind=kOutput, calls=%fused_computation.1.clone.1 | convolution fusion | flops 475267072 | bytes 15730176 | tf_op jit(solution)/shard_map/while/body/eval_jaxpr/tk,tl->kl/dot_general | solution.py:30
  546.0 7.6 %select_add_fusion.2 = f32[3584,512]{1,0:T(8,128)} fusion(f32[3584,512]{1,0:T(8,128)} %get-tuple-element.142, pred[]{:T(512)S(6)} %compare.3, bf16[1024,3584]{1,0:T(8,128)(2,1)} %get-tuple-element.151, s32[]{:T(128)S(6)} %select_n.10, bf16[1024,512]{1,0:T(8,128)(2,1)} %get-tuple-element.152), kind=kOutput, calls=%fused_computation.1.clone.1 | convolution fusion | flops 475267072 | bytes 15730176 | tf_op jit(solution)/shard_map/while/body/eval_jaxpr/tk,tl->kl/dot_general | solution.py:30
  553.7 7.6 %select_add_fusion.2 = f32[3584,512]{1,0:T(8,128)} fusion(f32[3584,512]{1,0:T(8,128)} %get-tuple-element.142, pred[]{:T(512)S(6)} %compare.3, bf16[1024,3584]{1,0:T(8,128)(2,1)} %get-tuple-element.151, s32[]{:T(128)S(6)} %select_n.10, bf16[1024,512]{1,0:T(8,128)(2,1)} %get-tuple-element.152), kind=kOutput, calls=%fused_computation.1.clone.1 | convolution fusion | flops 475267072 | bytes 15730176 | tf_op jit(solution)/shard_map/while/body/eval_jaxpr/tk,tl->kl/dot_general | solution.py:30
  561.3 7.6 %select_add_fusion.2 = f32[3584,512]{1,0:T(8,128)} fusion(f32[3584,512]{1,0:T(8,128)} %get-tuple-element.142, pred[]{:T(512)S(6)} %compare.3, bf16[1024,3584]{1,0:T(8,128)(2,1)} %get-tuple-element.151, s32[]{:T(128)S(6)} %select_n.10, bf16[1024,512]{1,0:T(8,128)(2,1)} %get-tuple-element.152), kind=kOutput, calls=%fused_computation.1.clone.1 | convolution fusion | flops 475267072 | bytes 15730176 | tf_op jit(solution)/shard_map/while/body/eval_jaxpr/tk,tl->kl/dot_general | solution.py:30
  568.9 7.7 %select_add_fusion.2 = f32[3584,512]{1,0:T(8,128)} fusion(f32[3584,512]{1,0:T(8,128)} %get-tuple-element.142, pred[]{:T(512)S(6)} %compare.3, bf16[1024,3584]{1,0:T(8,128)(2,1)} %get-tuple-element.151, s32[]{:T(128)S(6)} %select_n.10, bf16[1024,512]{1,0:T(8,128)(2,1)} %get-tuple-element.152), kind=kOutput, calls=%fused_computation.1.clone.1 | convolution fusion | flops 475267072 | bytes 15730176 | tf_op jit(solution)/shard_map/while/body/eval_jaxpr/tk,tl->kl/dot_general | solution.py:30
  576.7 7.6 %select_add_fusion.2 = f32[3584,512]{1,0:T(8,128)} fusion(f32[3584,512]{1,0:T(8,128)} %get-tuple-element.142, pred[]{:T(512)S(6)} %compare.3, bf16[1024,3584]{1,0:T(8,128)(2,1)} %get-tuple-element.151, s32[]{:T(128)S(6)} %select_n.10, bf16[1024,512]{1,0:T(8,128)(2,1)} %get-tuple-element.152), kind=kOutput, calls=%fused_computation.1.clone.1 | convolution fusion | flops 475267072 | bytes 15730176 | tf_op jit(solution)/shard_map/while/body/eval_jaxpr/tk,tl->kl/dot_general | solution.py:30
  584.3 7.6 %select_add_fusion.2 = f32[3584,512]{1,0:T(8,128)} fusion(f32[3584,512]{1,0:T(8,128)} %get-tuple-element.142, pred[]{:T(512)S(6)} %compare.3, bf16[1024,3584]{1,0:T(8,128)(2,1)} %get-tuple-element.151, s32[]{:T(128)S(6)} %select_n.10, bf16[1024,512]{1,0:T(8,128)(2,1)} %get-tuple-element.152), kind=kOutput, calls=%fused_computation.1.clone.1 | convolution fusion | flops 475267072 | bytes 15730176 | tf_op jit(solution)/shard_map/while/body/eval_jaxpr/tk,tl->kl/dot_general | solution.py:30
  591.9 7.1 %broadcast_multiply_fusion = f32[3584,512]{1,0:T(8,128)} fusion(f32[3584,512]{1,0:T(8,128)} %get-tuple-element.84), kind=kLoop, calls=%fused_computation.5 | loop fusion | flops 1835008 | bytes 14680064 | tf_op jit(solution)/shard_map/div | solution.py:35
  (5 shorter events, 0.0 us)
Async XLA Ops:
  6.5 55.3 %copy-start = (bf16[1024,512]{1,0:T(8,128)(2,1)S(1)}, bf16[1024,512]{1,0:T(8,128)(2,1)}, u32[]{:S(2)}) copy-start(bf16[1024,512]{1,0:T(8,128)(2,1)} %param.9) | copy-start | bytes 3145732
  6.5 55.3 %all-gather.6.cloned.1.call-start = ((), (), s32[]{:S(2)}) async-start(), calls=%async_computation.2 | async-start | bytes 2228224 | tf_op jit(solution)/shard_map/all_gather | solution.py:17
  7.3 134.3 %all-gather.4.cloned.1.call-start = ((), (), s32[]{:S(2)}) async-start(), calls=%async_computation.1 | async-start | bytes 4128768 | tf_op jit(solution)/shard_map/all_gather | solution.py:12
  8.0 187.7 %reduce-scatter.2.cloned.1.call-start = ((), (), s32[]{:S(2)}) async-start(), calls=%async_computation.3 | async-start | bytes 2359296 | tf_op jit(solution)/shard_map/reduce_scatter | solution.py:18
  66.0 466.9 %all-gather.8.cloned.1.call-start = ((), (), s32[]{:S(2)}) async-start(), calls=%async_computation.4 | async-start | bytes 1179648 | tf_op jit(solution)/shard_map/all_gather | solution.py:24
Sparse Core Ops, SparseCore 0:
  9.8 52.0 all-gather.5
  63.5 78.0 all-gather.3
  144.0 51.7 reduce-scatter.1
  197.5 66.0 all-gather.7
where the time goes:
time: 606 us; the launch traced here: 605 us
  blocking collectives  336 us (55%)
  waiting for transfers between devices  164 us (27%)
  matrix products  83.5 us (14%)
  between operations  13.1 us (2%)
  other arithmetic  8.73 us (1%)
    psum x1, blocking collectives, body(): rotated_grads = lax.psum(partial_sums, 'in').astype(jnp.bfloat16)  336 us
    all_gather x1, waiting for transfers between devices, body(): lax.all_gather(out_grads, 'out', axis=0, tiled=True)  75.5 us
    dot_general x8, matrix products, add_sequence(): jnp.einsum('tk,tl->kl', grad_rows, input_rows, preferred_element_type=jnp...  58.9 us
    all_gather x1, waiting for transfers between devices, body(): all_inputs = lax.all_gather(layer_inputs, 'in', axis=0, tiled=True)  53.8 us
    reduce_scatter x1, waiting for transfers between devices, body(): lax.psum_scatter(jnp.dot(all_inputs, basis_in, preferred_element_type=jnp...  33.7 us
    dot_general x1, matrix products, body(): jnp.dot(lax.all_gather(out_grads, 'out', axis=0, tiled=True), basis_out,...  20.5 us
  transfers between devices with their start and end apart: 4, of which 3 were waited for; matrix products, arithmetic and copies ran while one was open for 4% of the time, Pallas kernels for 0%

commit v1 on v0

v1 whole, which is shorter than its diff:
```python
import jax
import jax.numpy as jnp
from jax import lax
from jax.experimental import pallas as pl
from jax.experimental.pallas import tpu as pltpu
from jax.sharding import Mesh
from jax.sharding import PartitionSpec as P

SEQ_LEN = 128
NX, NZL, NY, NZH, NC = 4, 2, 4, 2, 2
BLK = SEQ_LEN // (NY * NC)
BF = jnp.bfloat16
F32 = jnp.float32


def swap(v, axis):
    return lax.ppermute(v, axis, [(0, 1), (1, 0)])


def shift_x(v, by):
    return lax.ppermute(v, "x", [(i, (i + by) % NX) for i in range(NX)])


def ring_y(v):
    pairs = []
    for y in range(NY):
        pairs.append((y * NC, (y + 1) % NY * NC))
        pairs.append((y * NC + 1, (y - 1) % NY * NC + 1))
    return lax.ppermute(v, ("y", "core"), pairs)


def row_order(first_half):
    y, core = lax.axis_index("y"), lax.axis_index("core")
    i = lax.broadcasted_iota(jnp.int32, (SEQ_LEN, SEQ_LEN), 0)
    j = lax.broadcasted_iota(jnp.int32, (SEQ_LEN, SEQ_LEN), 1)
    half, t, r = i // (NY * BLK), (i // BLK) % NY, i % BLK
    sign = jnp.where((core + half) % 2 == 0, 1, -1)
    block = (y - sign * t + NY) % NY
    source = ((first_half + half) % 2) * (NY * BLK) + block * BLK + r
    return (source == j).astype(BF)


def reorder(v, first_half):
    return jnp.dot(row_order(first_half), v, preferred_element_type=F32).astype(BF)


def rotate_chunk(rows, basis):
    n = len(rows)
    k = rows[0].shape[1]
    lhs = jnp.concatenate(rows, axis=0) if n > 1 else rows[0]
    part = jnp.dot(lhs, basis, preferred_element_type=F32)
    width = part.shape[1]
    part = part.reshape(n, NC, NY, BLK, width)
    keep = part[:, 0] + swap(part[:, 1].astype(BF), "core").astype(F32)
    total = keep[:, 1]
    for t in range(2, NY + 1):
        total = ring_y(total.astype(BF)).astype(F32) + keep[:, t % NY]
    total = total + swap(total.astype(BF), "zh").astype(F32)
    pieces = [total.astype(BF)]
    for _ in range(NY - 1):
        pieces.append(ring_y(pieces[-1]))
    own = jnp.stack(pieces, axis=1).reshape(n, NY * BLK, width)
    return own, swap(own, "core")


def rotate_inputs(layer_inputs, basis):
    x, zl = lax.axis_index("x"), lax.axis_index("zl")
    y, zh, core = lax.axis_index("y"), lax.axis_index("zh"), lax.axis_index("core")
    channels = layer_inputs.shape[1]
    step = jnp.stack([layer_inputs, swap(layer_inputs, "zh")])
    steps = [step]
    for _ in range(NY - 1):
        steps.append(ring_y(steps[-1]))
    own = jnp.stack(steps)
    other = swap(own, "core")
    other = jnp.stack([other[0], other[3], other[2], other[1]])
    rows = jnp.concatenate([own, other], axis=2).reshape(-1, channels)
    part = jnp.dot(rows, basis, preferred_element_type=F32)
    width = part.shape[1]
    part = part.reshape(NY, NZH, SEQ_LEN, width)
    sign = jnp.where(core == 0, 1, -1)

    def of_x(xx):
        t = (sign * (y - xx) + 2 * NY) % NY
        return lax.dynamic_index_in_dim(part, t, 0, keepdims=False)

    total = (
        of_x(x)
        + shift_x(of_x((x + 1) % NX), 1)
        + shift_x(of_x((x + 3) % NX), -1)
        + shift_x(of_x((x + 2) % NX), 2)
    )
    flip = zl ^ zh
    mine = lax.dynamic_index_in_dim(total, flip, 0, keepdims=False)
    theirs = lax.dynamic_index_in_dim(total, 1 - flip, 0, keepdims=False)
    mine = (mine + swap(theirs, "zl")).astype(BF)
    mine = reorder(mine, 0)
    pair = jnp.stack([mine, swap(mine, "zl")])
    before, after, far = shift_x(pair, 1), shift_x(pair, -1), shift_x(pair, 2)
    return jnp.stack([pair[0], pair[1], before[0], after[0], before[1], after[1], far[0], far[1]])


def square_kernel(sizes, *refs):
    x_ref, out_ref = refs[-2], refs[-1]
    s = 0
    for c, n in enumerate(sizes):
        own, other = refs[2 * c], refs[2 * c + 1]
        for i in range(n):
            g = jnp.concatenate([own[i], other[i]], axis=0)
            p = lax.dot_general(g, x_ref[s], (((0,), (0,)), ((), ())), preferred_element_type=F32)
            if s == 0:
                out_ref[...] = p * p
            else:
                out_ref[...] += p * p
            s += 1
    out_ref[...] *= 1.0 / s


def square_sum(chunks, inputs):
    sizes = tuple(own.shape[0] for own, _ in chunks)
    rows = chunks[0][0].shape[2]
    cols = inputs.shape[2]
    tile = 512
    specs = []
    operands = []
    for own, other in chunks:
        for v in (own, other):
            specs.append(pl.BlockSpec((v.shape[0], v.shape[1], tile), lambda i: (0, 0, i)))
            operands.append(v)
    specs.append(pl.BlockSpec(inputs.shape, lambda i: (0, 0, 0)))
    return pl.pallas_call(
        lambda *refs: square_kernel(sizes, *refs),
        grid=(rows // tile,),
        in_specs=specs,
        out_specs=pl.BlockSpec((tile, cols), lambda i: (i, 0)),
        out_shape=jax.ShapeDtypeStruct((rows, cols), F32),
        compiler_params=pltpu.CompilerParams(vmem_limit_bytes=32 * 1024 * 1024),
        cost_estimate=pl.CostEstimate(
            flops=2 * sum(sizes) * SEQ_LEN * rows * cols, bytes_accessed=rows * cols * 4, transcendentals=0
        ),
    )(*operands, inputs)


def body(out_grads, layer_inputs, basis_out, basis_in):
    core = lax.axis_index("core")
    own = reorder(out_grads, core)
    near = swap(own, "zl")
    before, after = shift_x(own, 1), shift_x(own, -1)
    before_n, after_n = shift_x(near, 1), shift_x(near, -1)
    h = SEQ_LEN // 2
    far = jnp.concatenate([shift_x(before[:h], 1), shift_x(after[h:], -1)], axis=0)
    far_n = jnp.concatenate([shift_x(before_n[:h], 1), shift_x(after_n[h:], -1)], axis=0)
    inputs = rotate_inputs(layer_inputs, basis_in)
    chunks = [
        rotate_chunk(rows, basis_out)
        for rows in ([own], [near, before, after], [before_n, after_n], [far, far_n])
    ]
    return square_sum(chunks, inputs)


def solution(mesh):
    fine = Mesh(mesh.devices.reshape(NX, NZL, NY, NZH, NC), ("x", "zl", "y", "zh", "core"))
    out, inn = ("x", "zl"), ("y", "zh", "core")
    return jax.shard_map(
        body,
        mesh=fine,
        in_specs=(P(out, inn), P(inn, out), P(inn, out), P(out, inn)),
        out_specs=P(out, inn),
        check_vma=False,
    )
```

time: 606 us -> 203 us (0.33)
  blocking collectives: 336 us -> 0 us
  waiting for transfers between devices: 164 us -> 61.2 us
  starting transfers between devices: 0.12 us -> 95.6 us
  matrix products: 83.5 us -> 27.1 us
  between operations: 13.1 us -> 0.7 us
  Pallas kernels: 0 us -> 10.7 us
    psum x1 -> x0, blocking collectives: 336 us -> none  [body(): rotated_grads = lax.psum(partial_sums, 'in').astype(jnp.bfloat16)]
    all_gather x3 -> x0, waiting for transfers between devices: 129 us -> none  [the longest x1 75.5 us: body(): lax.all_gather(out_grads, 'out', axis=0, tiled=True)]
    ppermute x0 -> x58, starting transfers between devices: none -> 95.6 us  [the longest x27 42 us: ring_y(): return lax.ppermute(v, ('y', 'core'), pairs)]
    ppermute x0 -> x58, waiting for transfers between devices: none -> 61.2 us  [the longest x27 26.4 us: ring_y(): return lax.ppermute(v, ('y', 'core'), pairs)]
    dot_general x10 -> x7, matrix products: 83.5 us -> 27.1 us  [the longest x4 24 us: rotate_chunk(): part = jnp.dot(lhs, basis, preferred_element_type=F32)]
    reduce_scatter x1 -> x0, waiting for transfers between devices: 33.7 us -> none  [body(): lax.psum_scatter(jnp.dot(all_inputs, basis_in, preferred_element_type=jnp...]
    pallas_call x0 -> x1, Pallas kernels: none -> 10.7 us  [square_sum(): pl.pallas_call(lambda *refs: square_kernel(sizes, *refs), grid=(rows // t...]
    div x1, other arithmetic: 7.1 us -> 0.01 us  [row_order(): half, t, r = (i // (NY * BLK), i // BLK % NY, i % BLK)]
  transfers between devices with their start and end apart: 4 -> 58, of which waited for: 3 -> 19; matrix products, arithmetic and copies ran while one was open for 4% -> 13% of each run, Pallas kernels for 0% -> 0%
where the time goes in v1:
time: 203 us
  starting transfers between devices  95.6 us (47%)
  waiting for transfers between devices  61.2 us (30%)
  matrix products  27.1 us (13%)
  Pallas kernels  10.7 us (5%)
  other arithmetic  4.64 us (2%)
  local copies, waits for them, and re-layouts  3.32 us (2%)
    ppermute x27, starting transfers between devices, ring_y(): return lax.ppermute(v, ('y', 'core'), pairs)  42 us
    ppermute x17, starting transfers between devices, swap(): return lax.ppermute(v, axis, [(0, 1), (1, 0)])  36.2 us
    ppermute x27, waiting for transfers between devices, ring_y(): return lax.ppermute(v, ('y', 'core'), pairs)  26.4 us
    dot_general x4, matrix products, rotate_chunk(): part = jnp.dot(lhs, basis, preferred_element_type=F32)  24 us
    ppermute x14, waiting for transfers between devices, shift_x(): return lax.ppermute(v, 'x', [(i, (i + by) % NX) for i in range(NX)])  21.6 us
    ppermute x14, starting transfers between devices, shift_x(): return lax.ppermute(v, 'x', [(i, (i + by) % NX) for i in range(NX)])  17.4 us
    ppermute x17, waiting for transfers between devices, swap(): return lax.ppermute(v, axis, [(0, 1), (1, 0)])  13.2 us
    pallas_call x1, Pallas kernels, square_sum(): pl.pallas_call(lambda *refs: square_kernel(sizes, *refs), grid=(rows // t...  10.7 us
  transfers between devices with their start and end apart: 58, of which 19 were waited for; matrix products, arithmetic and copies ran while one was open for 13% of the time, Pallas kernels for 0%

profile of v1, /device:TPU:1, one launch (start us, length us, event | category | flops | bytes accessed | tf_op | source)
XLA Modules:
  0.0 203.2 jit_solution(6333531874807254233)
XLA Ops:
  1.6 6.5 %fusion.133 = f32[128,3584]{1,0:T(8,128)S(1)} fusion(bf16[128,1792]{1,0:T(8,128)(2,1)S(1)} %convolution_convert_fusion, bf16[1792,3584]{1,0:T(8,128)(2,1)} %param.6), kind=kOutput, calls=%fused_computation.207 | convolution fusion | flops 1644167168 | bytes 15138816 | tf_op jit(solution)/shard_map/dot_general | solution.py:51
  9.7 3.7 %collective-permute-start.45 = (bf16[64,1024]{1,0:T(8,128)(2,1)S(1)}, bf16[64,1024]{1,0:T(8,128)(2,1)S(1)}, u32[]{:S(2)}, u32[]{:S(2)}) collective-permute-start(bf16[64,1024]{1,0:T(8,128)(2,1)S(1)} %copy-done.5), channel_id=1, source_target_pairs={{0,2},{2,0},{1,3},{3,1},{4,6},{6,4},{5,7},{7,5},{8,10},{10,8},{9,1... | collective-permute-start | bytes 393224 | tf_op jit(solution)/shard_map/ppermute | solution.py:17
  23.3 3.5 %collective-permute-start.47 = (bf16[2,64,1024]{2,1,0:T(8,128)(2,1)S(1)}, bf16[2,64,1024]{2,1,0:T(8,128)(2,1)S(1)}, u32[]{:S(2)}, u32[]{:S(2)}) collective-permute-start(bf16[2,64,1024]{2,1,0:T(8,128)(2,1)S(1)} %collective-permute-done.46), channel_id=1, source_target_pairs={{0,4},{1,13},{4,8},{5,1},{8,12},{9,5},{12,0},{13,9},{2,6},{3,15},{... | collective-permute-start | bytes 786440 | tf_op jit(solution)/shard_map/ppermute | solution.py:29
  33.9 9.3 %fusion.20 = f32[384,3584]{1,0:T(8,128)S(1)} fusion(bf16[1792,3584]{1,0:T(8,128)(2,1)} %param.6, bf16[128,1792]{1,0:T(8,128)(2,1)} %collective-permute-done.11, bf16[128,1792]{1,0:T(8,128)(2,1)} %collective-permute-done.10, bf16[128,1792]{1,0:T(8,128)(2,1)} %collective-permute-done.9), kind=kOutput, calls=%fused_computation.27 | convolution fusion | flops 4936630272 | bytes 19726336 | tf_op jit(solution)/shard_map/dot_general | solution.py:51
  48.2 6.0 %collective-permute-done.22 = bf16[128,1792]{1,0:T(8,128)(2,1)S(1)} collective-permute-done((bf16[128,1792]{1,0:T(8,128)(2,1)}, bf16[128,1792]{1,0:T(8,128)(2,1)S(1)}, u32[]{:S(2)}, u32[]{:S(2)}) %collective-permute-start.22) | collective-permute-done | bytes 458784 | tf_op jit(solution)/shard_map/ppermute | solution.py:21
  54.2 3.0 %collective-permute-done.21 = bf16[128,1792]{1,0:T(8,128)(2,1)S(1)} collective-permute-done((bf16[128,1792]{1,0:T(8,128)(2,1)}, bf16[128,1792]{1,0:T(8,128)(2,1)S(1)}, u32[]{:S(2)}, u32[]{:S(2)}) %collective-permute-start.21) | collective-permute-done | bytes 458784 | tf_op jit(solution)/shard_map/ppermute | solution.py:21
  57.8 3.5 %fusion.30 = f32[256,3584]{1,0:T(8,128)S(1)} fusion(bf16[1792,3584]{1,0:T(8,128)(2,1)S(1)} %bitcast.206, bf16[128,1792]{1,0:T(8,128)(2,1)S(1)} %collective-permute-done.22, bf16[128,1792]{1,0:T(8,128)(2,1)S(1)} %collective-permute-done.21), kind=kOutput, calls=%fused_computation.42 | convolution fusion | flops 3290169344 | bytes 17432576 | tf_op jit(solution)/shard_map/dot_general | solution.py:51
  62.7 5.7 %collective-permute-start.12 = (bf16[3,4,16,3584]{3,2,0,1:T(8,128)(2,1)S(1)}, bf16[3,4,16,3584]{3,2,0,1:T(8,128)(2,1)S(1)}, u32[]{:S(2)}, u32[]{:S(2)}) collective-permute-start(bf16[3,4,16,3584]{3,2,0,1:T(8,128)(2,1)S(1)} %fusion.19), channel_id=1, source_target_pairs={{0,1},{1,0},{2,3},{3,2},{4,5},{5,4},{6,7},{7,6},{8,9},{9,8},{10,11... | collective-permute-start | bytes 4128776 | tf_op jit(solution)/shard_map/ppermute | solution.py:17
  68.5 3.9 %collective-permute-start.23 = (bf16[2,4,16,3584]{3,2,0,1:T(8,128)(2,1)S(1)}, bf16[2,4,16,3584]{3,2,0,1:T(8,128)(2,1)}, u32[]{:S(2)}, u32[]{:S(2)}) collective-permute-start(bf16[2,4,16,3584]{3,2,0,1:T(8,128)(2,1)S(1)} %fusion.27), channel_id=1, source_target_pairs={{0,1},{1,0},{2,3},{3,2},{4,5},{5,4},{6,7},{7,6},{8,9},{9,8},{10,11... | collective-permute-start | bytes 2752520 | tf_op jit(solution)/shard_map/ppermute | solution.py:17
  72.5 4.8 %fusion.34 = f32[256,3584]{1,0:T(8,128)S(1)} fusion(bf16[1792,3584]{1,0:T(8,128)(2,1)S(1)} %bitcast.206, bf16[64,1792]{1,0:T(8,128)(2,1)} %collective-permute-done.35, bf16[64,1792]{1,0:T(8,128)(2,1)} %collective-permute-done.34, bf16[64,1792]{1,0:T(8,128)(2,1)} %collective-permute-done.33, bf16[64,1792]{1,0:T(8,128)(2,1)} %collective-permute-done.32), kind=kOutput, calls=%fused_computation.47 | convolution fusion | flops 3292004352 | bytes 17432576 | tf_op jit(solution)/shard_map/dot_general | solution.py:51
  92.6 3.3 %collective-permute-done.37 = bf16[2,16,3584]{2,1,0:T(8,128)(2,1)S(1)} collective-permute-done((bf16[2,16,3584]{2,1,0:T(8,128)(2,1)S(1)}, bf16[2,16,3584]{2,1,0:T(8,128)(2,1)S(1)}, u32[]{:S(2)}, u32[]{:S(2)}) %collective-permute-start.37) | collective-permute-done | bytes 229408 | tf_op jit(solution)/shard_map/ppermute | solution.py:29
  95.9 3.0 %collective-permute-start.25 = (bf16[2,16,3584]{2,1,0:T(8,128)(2,1)S(1)}, bf16[2,16,3584]{2,1,0:T(8,128)(2,1)S(1)}, u32[]{:S(2)}, u32[]{:S(2)}) collective-permute-start(bf16[2,16,3584]{2,1,0:T(8,128)(2,1)S(1)} %fusion.59), channel_id=1, source_target_pairs={{0,4},{1,13},{4,8},{5,1},{8,12},{9,5},{12,0},{13,9},{2,6},{3,15},{... | collective-permute-start | bytes 688136 | tf_op jit(solution)/shard_map/ppermute | solution.py:29
  99.0 2.9 %collective-permute-done.25 = bf16[2,16,3584]{2,1,0:T(8,128)(2,1)S(1)} collective-permute-done((bf16[2,16,3584]{2,1,0:T(8,128)(2,1)S(1)}, bf16[2,16,3584]{2,1,0:T(8,128)(2,1)S(1)}, u32[]{:S(2)}, u32[]{:S(2)}) %collective-permute-start.25) | collective-permute-done | bytes 229408 | tf_op jit(solution)/shard_map/ppermute | solution.py:29
  101.9 3.4 %collective-permute-start.14 = (bf16[3,16,3584]{2,1,0:T(8,128)(2,1)S(1)}, bf16[3,16,3584]{2,1,0:T(8,128)(2,1)S(1)}, u32[]{:S(2)}, u32[]{:S(2)}) collective-permute-start(bf16[3,16,3584]{2,1,0:T(8,128)(2,1)S(1)} %fusion.46), channel_id=1, source_target_pairs={{0,4},{1,13},{4,8},{5,1},{8,12},{9,5},{12,0},{13,9},{2,6},{3,15},{... | collective-permute-start | bytes 1032200 | tf_op jit(solution)/shard_map/ppermute | solution.py:29
  105.5 4.9 %collective-permute-done.52 = f32[2,128,512]{2,1,0:T(8,128)S(1)} collective-permute-done((f32[2,128,512]{2,1,0:T(8,128)S(1)}, f32[2,128,512]{2,1,0:T(8,128)S(1)}, u32[]{:S(2)}, u32[]{:S(2)}) %collective-permute-start.52) | collective-permute-done | bytes 524320 | tf_op jit(solution)/shard_map/ppermute | solution.py:21
  116.2 3.0 %collective-permute-start.27 = (bf16[2,16,3584]{2,1,0:T(8,128)(2,1)S(1)}, bf16[2,16,3584]{2,1,0:T(8,128)(2,1)S(1)}, u32[]{:S(2)}, u32[]{:S(2)}) collective-permute-start(bf16[2,16,3584]{2,1,0:T(8,128)(2,1)S(1)} %fusion.62), channel_id=1, source_target_pairs={{0,2},{2,0},{1,3},{3,1},{4,6},{6,4},{5,7},{7,5},{8,10},{10,8},{9,1... | collective-permute-start | bytes 688136 | tf_op jit(solution)/shard_map/ppermute | solution.py:17
  125.6 2.9 %collective-permute-start.28 = (bf16[2,16,3584]{2,1,0:T(8,128)(2,1)S(1)}, bf16[2,16,3584]{2,1,0:T(8,128)(2,1)S(1)}, u32[]{:S(2)}, u32[]{:S(2)}) collective-permute-start(bf16[2,16,3584]{2,1,0:T(8,128)(2,1)S(1)} %add_convert_fusion.2), channel_id=1, source_target_pairs={{0,4},{1,13},{4,8},{5,1},{8,12},{9,5},{12,0},{13,9},{2,6},{3,15},{... | collective-permute-start | bytes 688136 | tf_op jit(solution)/shard_map/ppermute | solution.py:29
  128.5 11.9 %collective-permute-done.16 = bf16[3,16,3584]{2,1,0:T(8,128)(2,1)S(1)} collective-permute-done((bf16[3,16,3584]{2,1,0:T(8,128)(2,1)S(1)}, bf16[3,16,3584]{2,1,0:T(8,128)(2,1)S(1)}, u32[]{:S(2)}, u32[]{:S(2)}) %collective-permute-start.16) | collective-permute-done | bytes 344096 | tf_op jit(solution)/shard_map/ppermute | solution.py:17
  156.0 3.5 %collective-permute-done.41 = bf16[2,16,3584]{2,1,0:T(8,128)(2,1)S(1)} collective-permute-done((bf16[2,16,3584]{2,1,0:T(8,128)(2,1)S(1)}, bf16[2,16,3584]{2,1,0:T(8,128)(2,1)S(1)}, u32[]{:S(2)}, u32[]{:S(2)}) %collective-permute-start.41) | collective-permute-done | bytes 229408 | tf_op jit(solution)/shard_map/ppermute | solution.py:29
  164.8 2.8 %collective-permute-done.42 = bf16[2,16,3584]{2,1,0:T(8,128)(2,1)S(1)} collective-permute-done((bf16[2,16,3584]{2,1,0:T(8,128)(2,1)S(1)}, bf16[2,16,3584]{2,1,0:T(8,128)(2,1)S(1)}, u32[]{:S(2)}, u32[]{:S(2)}) %collective-permute-start.42) | collective-permute-done | bytes 229408 | tf_op jit(solution)/shard_map/ppermute | solution.py:29
  167.6 4.8 %collective-permute-start.31 = (bf16[2,64,3584]{2,1,0:T(8,128)(2,1)S(1)}, bf16[2,64,3584]{2,1,0:T(8,128)(2,1)S(1)}, u32[]{:S(2)}, u32[]{:S(2)}) collective-permute-start(bf16[2,64,3584]{2,1,0:T(8,128)(2,1)S(1)} %bitcast.199), channel_id=1, source_target_pairs={{0,1},{1,0},{2,3},{3,2},{4,5},{5,4},{6,7},{7,6},{8,9},{9,8},{10,11... | collective-permute-start | bytes 2752520 | tf_op jit(solution)/shard_map/ppermute | solution.py:17
  177.3 5.9 %collective-permute-start.20 = (bf16[3,64,3584]{2,1,0:T(8,128)(2,1)S(1)}, bf16[3,64,3584]{2,1,0:T(8,128)(2,1)S(1)}, u32[]{:S(2)}, u32[]{:S(2)}) collective-permute-start(bf16[3,64,3584]{2,1,0:T(8,128)(2,1)S(1)} %bitcast.197), channel_id=1, source_target_pairs={{0,1},{1,0},{2,3},{3,2},{4,5},{5,4},{6,7},{7,6},{8,9},{9,8},{10,11... | collective-permute-start | bytes 4128776 | tf_op jit(solution)/shard_map/ppermute | solution.py:17
  185.2 7.3 %collective-permute-done.57 = bf16[2,128,512]{2,1,0:T(8,128)(2,1)S(1)} collective-permute-done((bf16[2,128,512]{2,1,0:T(8,128)(2,1)S(1)}, bf16[2,128,512]{2,1,0:T(8,128)(2,1)S(1)}, u32[]{:S(2)}, u32[]{:S(2)}) %collective-permute-start.57) | collective-permute-done | bytes 262176 | tf_op jit(solution)/shard_map/ppermute | solution.py:21
  192.5 10.7 %shard_map.46 = f32[3584,512]{1,0:T(8,128)} custom-call(bf16[1,64,3584]{2,1,0:T(8,128)(2,1)S(1)} %bitcast.204, bf16[1,64,3584]{2,1,0:T(8,128)(2,1)S(1)} %collective-permute-done.8.refs_1_, bf16[3,64,3584]{2,1,0:T(8,128)(2,1)S(1)} %bitcast.198, bf16[3,64,3584]{2,1,0:T(8,128)(2,1)S(1)} %collective-permute-done.20.refs_3_, bf16[2,64,3584]{2,1,0:T(8,128)(2,1)S(1)} %bitcast.200, ...), custom_call_target="tpu_custom_call" | custom-call | flops 3758096384 | bytes 7340032 | tf_op jit(solution)/shard_map/pallas_call | solution.py:131
  (183 shorter events, 82.5 us)
Async XLA Ops:
  13.4 13.4 %collective-permute-start.11 = (bf16[128,1792]{1,0:T(8,128)(2,1)S(1)}, bf16[128,1792]{1,0:T(8,128)(2,1)}, u32[]{:S(2)}, u32[]{:S(2)}) collective-permute-start(bf16[128,1792]{1,0:T(8,128)(2,1)S(1)} %convolution_convert_fusion), channel_id=1, source_target_pairs={{0,96},{32,0},{64,32},{96,64},{1,97},{33,1},{65,33},{97,65},{2,98}... | collective-permute-start | bytes 1376264 | tf_op jit(solution)/shard_map/ppermute | solution.py:21
  15.9 14.5 %collective-permute-start.10 = (bf16[128,1792]{1,0:T(8,128)(2,1)S(1)}, bf16[128,1792]{1,0:T(8,128)(2,1)}, u32[]{:S(2)}, u32[]{:S(2)}) collective-permute-start(bf16[128,1792]{1,0:T(8,128)(2,1)S(1)} %convolution_convert_fusion), channel_id=1, source_target_pairs={{0,32},{32,64},{64,96},{96,0},{1,33},{33,65},{65,97},{97,1},{2,34}... | collective-permute-start | bytes 1376264 | tf_op jit(solution)/shard_map/ppermute | solution.py:21
  20.7 13.3 %collective-permute-start.9 = (bf16[128,1792]{1,0:T(8,128)(2,1)S(1)}, bf16[128,1792]{1,0:T(8,128)(2,1)}, u32[]{:S(2)}, u32[]{:S(2)}) collective-permute-start(bf16[128,1792]{1,0:T(8,128)(2,1)S(1)} %convolution_convert_fusion), channel_id=1, source_target_pairs={{0,16},{16,0},{1,17},{17,1},{2,18},{18,2},{3,19},{19,3},{4,20},{20... | collective-permute-start | bytes 1376264 | tf_op jit(solution)/shard_map/ppermute | solution.py:17
  23.3 22.9 %collective-permute-start.47 = (bf16[2,64,1024]{2,1,0:T(8,128)(2,1)S(1)}, bf16[2,64,1024]{2,1,0:T(8,128)(2,1)S(1)}, u32[]{:S(2)}, u32[]{:S(2)}) collective-permute-start(bf16[2,64,1024]{2,1,0:T(8,128)(2,1)S(1)} %collective-permute-done.46), channel_id=1, source_target_pairs={{0,4},{1,13},{4,8},{5,1},{8,12},{9,5},{12,0},{13,9},{2,6},{3,15},{... | collective-permute-start | bytes 786440 | tf_op jit(solution)/shard_map/ppermute | solution.py:29
  27.8 34.9 %collective-permute-start.33 = (bf16[64,1792]{1,0:T(8,128)(2,1)S(1)}, bf16[64,1792]{1,0:T(8,128)(2,1)}, u32[]{:S(2)}, u32[]{:S(2)}) collective-permute-start(bf16[64,1792]{1,0:T(8,128)(2,1)S(1)} %slice.174), channel_id=1, source_target_pairs={{0,96},{32,0},{64,32},{96,64},{1,97},{33,1},{65,33},{97,65},{2,98}... | collective-permute-start | bytes 688136 | tf_op jit(solution)/shard_map/ppermute | solution.py:21
  31.3 37.1 %collective-permute-start.32 = (bf16[64,1792]{1,0:T(8,128)(2,1)S(1)}, bf16[64,1792]{1,0:T(8,128)(2,1)}, u32[]{:S(2)}, u32[]{:S(2)}) collective-permute-start(bf16[64,1792]{1,0:T(8,128)(2,1)S(1)} %slice.173), channel_id=1, source_target_pairs={{0,32},{32,64},{64,96},{96,0},{1,33},{33,65},{65,97},{97,1},{2,34}... | collective-permute-start | bytes 688136 | tf_op jit(solution)/shard_map/ppermute | solution.py:21
  47.0 15.5 %collective-permute-start.48 = (bf16[2,64,1024]{2,1,0:T(8,128)(2,1)S(1)}, bf16[2,64,1024]{2,1,0:T(8,128)(2,1)S(1)}, u32[]{:S(2)}, u32[]{:S(2)}) collective-permute-start(bf16[2,64,1024]{2,1,0:T(8,128)(2,1)S(1)} %collective-permute-done.47), channel_id=1, source_target_pairs={{0,4},{1,13},{4,8},{5,1},{8,12},{9,5},{12,0},{13,9},{2,6},{3,15},{... | collective-permute-start | bytes 786440 | tf_op jit(solution)/shard_map/ppermute | solution.py:29
  57.2 15.2 %collective-permute-start.35 = (bf16[64,1792]{1,0:T(8,128)(2,1)S(1)}, bf16[64,1792]{1,0:T(8,128)(2,1)}, u32[]{:S(2)}, u32[]{:S(2)}) collective-permute-start(bf16[64,1792]{1,0:T(8,128)(2,1)S(1)} %slice.176), channel_id=1, source_target_pairs={{0,96},{32,0},{64,32},{96,64},{1,97},{33,1},{65,33},{97,65},{2,98}... | collective-permute-start | bytes 688136 | tf_op jit(solution)/shard_map/ppermute | solution.py:21
  62.7 19.8 %collective-permute-start.12 = (bf16[3,4,16,3584]{3,2,0,1:T(8,128)(2,1)S(1)}, bf16[3,4,16,3584]{3,2,0,1:T(8,128)(2,1)S(1)}, u32[]{:S(2)}, u32[]{:S(2)}) collective-permute-start(bf16[3,4,16,3584]{3,2,0,1:T(8,128)(2,1)S(1)} %fusion.19), channel_id=1, source_target_pairs={{0,1},{1,0},{2,3},{3,2},{4,5},{5,4},{6,7},{7,6},{8,9},{9,8},{10,11... | collective-permute-start | bytes 4128776 | tf_op jit(solution)/shard_map/ppermute | solution.py:17
  68.4 14.8 %collective-permute-start.49 = (bf16[4,2,64,1024]{3,2,1,0:T(8,128)(2,1)S(1)}, bf16[4,2,64,1024]{3,2,1,0:T(8,128)(2,1)S(1)}, u32[]{:S(2)}, u32[]{:S(2)}) collective-permute-start(bf16[4,2,64,1024]{3,2,1,0:T(8,128)(2,1)S(1)} %pad_maximum_fusion.1), channel_id=1, source_target_pairs={{0,1},{1,0},{2,3},{3,2},{4,5},{5,4},{6,7},{7,6},{8,9},{9,8},{10,11... | collective-permute-start | bytes 3145736 | tf_op jit(solution)/shard_map/ppermute | solution.py:17
  78.0 65.1 %collective-permute-start.7 = (bf16[1,16,3584]{2,1,0:T(8,128)(2,1)}, bf16[1,16,3584]{2,1,0:T(8,128)(2,1)S(1)}, u32[]{:S(2)}, u32[]{:S(2)}) collective-permute-start(bf16[1,16,3584]{2,1,0:T(8,128)(2,1)} %collective-permute-done.6), channel_id=1, source_target_pairs={{0,4},{1,13},{4,8},{5,1},{8,12},{9,5},{12,0},{13,9},{2,6},{3,15},{... | collective-permute-start | bytes 344072 | tf_op jit(solution)/shard_map/ppermute | solution.py:29
  85.2 20.2 %collective-permute-start.50 = (f32[2,128,512]{2,1,0:T(8,128)S(1)}, f32[2,128,512]{2,1,0:T(8,128)S(1)}, u32[]{:S(2)}, u32[]{:S(2)}) collective-permute-start(f32[2,128,512]{2,1,0:T(8,128)S(1)} %get-tuple-element.5), channel_id=1, source_target_pairs={{0,32},{32,64},{64,96},{96,0},{1,33},{33,65},{65,97},{97,1},{2,34}... | collective-permute-start | bytes 1572872 | tf_op jit(solution)/shard_map/ppermute | solution.py:21
  85.3 25.0 %collective-permute-start.52 = (f32[2,128,512]{2,1,0:T(8,128)S(1)}, f32[2,128,512]{2,1,0:T(8,128)S(1)}, u32[]{:S(2)}, u32[]{:S(2)}) collective-permute-start(f32[2,128,512]{2,1,0:T(8,128)S(1)} %get-tuple-element.6), channel_id=1, source_target_pairs={{0,64},{32,96},{64,0},{96,32},{1,65},{33,97},{65,1},{97,33},{2,66}... | collective-permute-start | bytes 1572872 | tf_op jit(solution)/shard_map/ppermute | solution.py:21
  88.3 22.8 %collective-permute-start.51 = (f32[2,128,512]{2,1,0:T(8,128)S(1)}, f32[2,128,512]{2,1,0:T(8,128)S(1)}, u32[]{:S(2)}, u32[]{:S(2)}) collective-permute-start(f32[2,128,512]{2,1,0:T(8,128)S(1)} %get-tuple-element.7), channel_id=1, source_target_pairs={{0,96},{32,0},{64,32},{96,64},{1,97},{33,1},{65,33},{97,65},{2,98}... | collective-permute-start | bytes 1572872 | tf_op jit(solution)/shard_map/ppermute | solution.py:21
  119.5 26.0 %collective-permute-start.54 = (bf16[128,512]{1,0:T(8,128)(2,1)S(1)}, bf16[128,512]{1,0:T(8,128)(2,1)S(1)}, u32[]{:S(2)}, u32[]{:S(2)}) collective-permute-start(bf16[128,512]{1,0:T(8,128)(2,1)S(1)} %get-tuple-element.15), channel_id=1, source_target_pairs={{0,16},{16,0},{1,17},{17,1},{2,18},{18,2},{3,19},{19,3},{4,20},{20... | collective-permute-start | bytes 393224 | tf_op jit(solution)/shard_map/ppermute | solution.py:17
  122.3 28.1 %collective-permute-start.40 = (bf16[2,16,3584]{2,1,0:T(8,128)(2,1)S(1)}, bf16[2,16,3584]{2,1,0:T(8,128)(2,1)S(1)}, u32[]{:S(2)}, u32[]{:S(2)}) collective-permute-start(bf16[2,16,3584]{2,1,0:T(8,128)(2,1)S(1)} %fusion.63), channel_id=1, source_target_pairs={{0,2},{2,0},{1,3},{3,1},{4,6},{6,4},{5,7},{7,5},{8,10},{10,8},{9,1... | collective-permute-start | bytes 688136 | tf_op jit(solution)/shard_map/ppermute | solution.py:17
  125.0 15.3 %collective-permute-start.16 = (bf16[3,16,3584]{2,1,0:T(8,128)(2,1)S(1)}, bf16[3,16,3584]{2,1,0:T(8,128)(2,1)S(1)}, u32[]{:S(2)}, u32[]{:S(2)}) collective-permute-start(bf16[3,16,3584]{2,1,0:T(8,128)(2,1)S(1)} %fusion.60), channel_id=1, source_target_pairs={{0,2},{2,0},{1,3},{3,1},{4,6},{6,4},{5,7},{7,5},{8,10},{10,8},{9,1... | collective-permute-start | bytes 1032200 | tf_op jit(solution)/shard_map/ppermute | solution.py:17
  125.6 22.6 %collective-permute-start.28 = (bf16[2,16,3584]{2,1,0:T(8,128)(2,1)S(1)}, bf16[2,16,3584]{2,1,0:T(8,128)(2,1)S(1)}, u32[]{:S(2)}, u32[]{:S(2)}) collective-permute-start(bf16[2,16,3584]{2,1,0:T(8,128)(2,1)S(1)} %add_convert_fusion.2), channel_id=1, source_target_pairs={{0,4},{1,13},{4,8},{5,1},{8,12},{9,5},{12,0},{13,9},{2,6},{3,15},{... | collective-permute-start | bytes 688136 | tf_op jit(solution)/shard_map/ppermute | solution.py:29
  144.1 48.5 %collective-permute-start.8 = (bf16[1,64,3584]{2,1,0:T(8,128)(2,1)S(1)}, bf16[1,64,3584]{2,1,0:T(8,128)(2,1)S(1)}, u32[]{:S(2)}, u32[]{:S(2)}) collective-permute-start(bf16[1,64,3584]{2,1,0:T(8,128)(2,1)S(1)} %bitcast.203), channel_id=1, source_target_pairs={{0,1},{1,0},{2,3},{3,2},{4,5},{5,4},{6,7},{7,6},{8,9},{9,8},{10,11... | collective-permute-start | bytes 1376264 | tf_op jit(solution)/shard_map/ppermute | solution.py:17
  145.5 38.0 %collective-permute-start.56 = (bf16[2,128,512]{2,1,0:T(8,128)(2,1)S(1)}, bf16[2,128,512]{2,1,0:T(8,128)(2,1)S(1)}, u32[]{:S(2)}, u32[]{:S(2)}) collective-permute-start(bf16[2,128,512]{2,1,0:T(8,128)(2,1)S(1)} %pad_maximum_fusion.6), channel_id=1, source_target_pairs={{0,96},{32,0},{64,32},{96,64},{1,97},{33,1},{65,33},{97,65},{2,98}... | collective-permute-start | bytes 786440 | tf_op jit(solution)/shard_map/ppermute | solution.py:21
  149.9 14.7 %collective-permute-start.18 = (bf16[3,16,3584]{2,1,0:T(8,128)(2,1)S(1)}, bf16[3,16,3584]{2,1,0:T(8,128)(2,1)S(1)}, u32[]{:S(2)}, u32[]{:S(2)}) collective-permute-start(bf16[3,16,3584]{2,1,0:T(8,128)(2,1)S(1)} %collective-permute-done.17), channel_id=1, source_target_pairs={{0,4},{1,13},{4,8},{5,1},{8,12},{9,5},{12,0},{13,9},{2,6},{3,15},{... | collective-permute-start | bytes 1032200 | tf_op jit(solution)/shard_map/ppermute | solution.py:29
  159.5 23.9 %collective-permute-start.55 = (bf16[2,128,512]{2,1,0:T(8,128)(2,1)S(1)}, bf16[2,128,512]{2,1,0:T(8,128)(2,1)S(1)}, u32[]{:S(2)}, u32[]{:S(2)}) collective-permute-start(bf16[2,128,512]{2,1,0:T(8,128)(2,1)S(1)} %pad_maximum_fusion.6), channel_id=1, source_target_pairs={{0,32},{32,64},{64,96},{96,0},{1,33},{33,65},{65,97},{97,1},{2,34}... | collective-permute-start | bytes 786440 | tf_op jit(solution)/shard_map/ppermute | solution.py:21
  167.6 24.9 %collective-permute-start.31 = (bf16[2,64,3584]{2,1,0:T(8,128)(2,1)S(1)}, bf16[2,64,3584]{2,1,0:T(8,128)(2,1)S(1)}, u32[]{:S(2)}, u32[]{:S(2)}) collective-permute-start(bf16[2,64,3584]{2,1,0:T(8,128)(2,1)S(1)} %bitcast.199), channel_id=1, source_target_pairs={{0,1},{1,0},{2,3},{3,2},{4,5},{5,4},{6,7},{7,6},{8,9},{9,8},{10,11... | collective-permute-start | bytes 2752520 | tf_op jit(solution)/shard_map/ppermute | solution.py:17
  177.3 15.2 %collective-permute-start.20 = (bf16[3,64,3584]{2,1,0:T(8,128)(2,1)S(1)}, bf16[3,64,3584]{2,1,0:T(8,128)(2,1)S(1)}, u32[]{:S(2)}, u32[]{:S(2)}) collective-permute-start(bf16[3,64,3584]{2,1,0:T(8,128)(2,1)S(1)} %bitcast.197), channel_id=1, source_target_pairs={{0,1},{1,0},{2,3},{3,2},{4,5},{5,4},{6,7},{7,6},{8,9},{9,8},{10,11... | collective-permute-start | bytes 4128776 | tf_op jit(solution)/shard_map/ppermute | solution.py:17
  (48 other events, 550.9 us)

commit v2 on v1

v2 whole, which is shorter than its diff:
```python
import jax
import jax.numpy as jnp
from jax import lax
from jax.experimental import pallas as pl
from jax.experimental.pallas import tpu as pltpu
from jax.sharding import Mesh
from jax.sharding import PartitionSpec as P

SEQ_LEN = 128
NX, NZL, NY, NZH, NC = 4, 2, 4, 2, 2
BLK = SEQ_LEN // (NY * NC)
BF = jnp.bfloat16
F32 = jnp.float32


def swap(v, axis):
    return lax.ppermute(v, axis, [(0, 1), (1, 0)])


def shift_x(v, by):
    return lax.ppermute(v, "x", [(i, (i + by) % NX) for i in range(NX)])


def near_bit():
    return jnp.where(lax.axis_index("core") == 0, 1, 3)


def trade(v, axis, other=False):
    pairs = []
    for i in range(4):
        for core, bit in ((0, 1), (1, 3)):
            pairs.append((i * NC + core, (i ^ (4 - bit if other else bit)) * NC + core))
    return lax.ppermute(v, (axis, "core"), pairs)


def pick(v, index, axis):
    return lax.dynamic_index_in_dim(v, index, axis, keepdims=False)


class Line:
    def __init__(self):
        self.last = ()

    def run(self, step, *operands):
        result = step(*lax.optimization_barrier(operands + self.last)[: len(operands)])
        self.last = tuple(result) if isinstance(result, (tuple, list)) else (result,)
        return result

    def put(self, v):
        return self.run(lambda u: u, v)


def reorder(v):
    y, a = lax.axis_index("y"), near_bit()
    i = lax.broadcasted_iota(jnp.int32, (SEQ_LEN, SEQ_LEN), 0)
    j = lax.broadcasted_iota(jnp.int32, (SEQ_LEN, SEQ_LEN), 1)
    half, t, r = i // (NY * BLK), (i // BLK) % NY, i % BLK
    bit = jnp.where(t == 0, 0, jnp.where(t == 3, 2, jnp.where(t == 1 + half, 4 - a, a)))
    hot = (half * (NY * BLK) + (y ^ bit) * BLK + r == j).astype(BF)
    return jnp.einsum("ij,njk->nik", hot, v, preferred_element_type=F32).astype(BF)


class Chunk:
    def __init__(self, line, basis):
        self.line, self.basis = line, basis

    def multiply(self, join, *received):
        def step(*received):
            lhs = join(*received)
            part = jnp.dot(lhs, self.basis, preferred_element_type=F32)
            part = part.reshape(lhs.shape[0] // SEQ_LEN, NC, NY, BLK, part.shape[1])
            core = lax.axis_index("core")
            return pick(part, 1 - core, 1).astype(BF), pick(part, core, 1)

        self.send, self.mine = self.line.run(step, *received)

    def cross(self):
        self.theirs = swap(self.send, "core")

    def blocks(self):
        y, a = lax.axis_index("y"), near_bit()

        def step(mine, theirs):
            def block(bit):
                return pick(mine, y ^ bit, 1) + pick(theirs, y ^ bit, 1).astype(F32)

            send = jnp.stack([block(a).astype(BF), block(2).astype(BF)])
            return send, block(0), block(4 - a)

        send, self.here, self.next = self.line.run(step, self.mine, self.theirs)
        self.r = trade(send, "y")

    def reduce(self):
        def step(here, next_, r):
            return (next_ + r[1].astype(F32)).astype(BF), here + r[0].astype(F32)

        send, self.here = self.line.run(step, self.here, self.next, self.r)
        self.r = trade(send, "y", other=True)

    def exchange(self):
        def step(here, r):
            total = here + r.astype(F32)
            return total.astype(BF), total

        send, self.here = self.line.run(step, self.here, self.r)
        self.r = swap(send, "zh")

    def gather(self):
        self.g = self.line.run(lambda u, v: (u + v.astype(F32)).astype(BF), self.here, self.r)
        self.r = trade(self.g, "y", other=True)

    def gather_more(self):
        self.g = self.line.run(lambda u, v: jnp.stack([u, v]), self.g, self.r)
        self.r = trade(self.g, "y")

    def cross_back(self):
        def step(u, v):
            own = jnp.concatenate([u, v], axis=0).swapaxes(0, 1)
            return own.reshape(own.shape[0], NY * BLK, own.shape[-1])

        self.own = self.line.run(step, self.g, self.r)
        self.other = swap(self.own, "core")


class Inputs:
    def __init__(self, line, basis):
        self.line, self.basis = line, basis

    def rows(self, rows):
        self.g = rows
        self.r = trade(rows, "y", other=True)

    def rows_more(self):
        self.g = self.line.run(lambda u, v: jnp.stack([u, v]), self.g, self.r)
        self.r = trade(self.g, "y")

    def rows_z(self):
        self.g = self.line.run(lambda u, v: jnp.concatenate([u, v], axis=0), self.g, self.r)
        self.r = swap(self.g, "zh")

    def rows_cross(self):
        self.g = self.line.run(lambda u, v: jnp.stack([u, v]), self.g, self.r)
        self.r = swap(self.g, "core")

    def multiply(self):
        def step(own, other):
            other = jnp.stack([other[:, t] for t in (0, 2, 1, 3)], axis=1)
            rows = jnp.concatenate([own, other], axis=2).reshape(-1, own.shape[-1])
            part = jnp.dot(rows, self.basis, preferred_element_type=F32)
            return part.reshape(NZH, NY, SEQ_LEN, part.shape[1])

        self.part = self.line.run(step, self.g, self.r)

    def block(self, part, bit):
        off = lax.axis_index("y") ^ lax.axis_index("x") ^ bit
        t = jnp.where(off == 0, 0, jnp.where(off == 2, 3, jnp.where(off == near_bit(), 2, 1)))
        return pick(part, t, 1)

    def reduce(self):
        a = near_bit()

        def step(p):
            return jnp.stack([self.block(p, a), self.block(p, 2)]), self.block(p, 0), self.block(p, 4 - a)

        send, self.here, self.next = self.line.run(step, self.part)
        self.r = trade(send, "x")

    def reduce_more(self):
        def step(here, next_, r):
            return next_ + r[1], here + r[0]

        send, self.here = self.line.run(step, self.here, self.next, self.r)
        self.r = trade(send, "x", other=True)

    def exchange(self):
        self.here = self.line.run(lambda u, v: u + v, self.here, self.r)
        self.r = swap(self.here, "zl")

    def gather(self):
        flip = lax.axis_index("zl") ^ lax.axis_index("zh")

        def step(u, v):
            total = (u + v).astype(BF)
            return reorder(jnp.stack([pick(total, flip, 0), pick(total, 1 - flip, 0)]))

        self.g = self.line.run(step, self.here, self.r)
        self.r = trade(self.g, "x", other=True)

    def gather_more(self):
        self.g = self.line.run(lambda u, v: jnp.stack([u, v]), self.g, self.r)
        self.r = trade(self.g, "x")

    def all(self):
        straight = (lax.axis_index("x") + lax.axis_index("core")) % 2 == 0

        def step(g, r):
            before, after = jnp.where(straight, g[1], r[0]), jnp.where(straight, r[0], g[1])
            return jnp.stack(
                [g[0, 0], g[0, 1], before[0], after[0], before[1], after[1], r[1, 0], r[1, 1]]
            )

        return self.line.run(step, self.g, self.r)


def square_kernel(sizes, *refs):
    x_ref, out_ref = refs[-2], refs[-1]
    s = 0
    for c, n in enumerate(sizes):
        own, other = refs[2 * c], refs[2 * c + 1]
        for i in range(n):
            g = jnp.concatenate([own[i], other[i]], axis=0)
            p = lax.dot_general(g, x_ref[s], (((0,), (0,)), ((), ())), preferred_element_type=F32)
            if s == 0:
                out_ref[...] = p * p
            else:
                out_ref[...] += p * p
            s += 1
    out_ref[...] *= 1.0 / s


def square_sum(chunks, inputs):
    sizes = tuple(own.shape[0] for own, _ in chunks)
    rows = chunks[0][0].shape[2]
    cols = inputs.shape[2]
    tile = 512
    specs = []
    operands = []
    for own, other in chunks:
        for v in (own, other):
            specs.append(pl.BlockSpec((v.shape[0], v.shape[1], tile), lambda i: (0, 0, i)))
            operands.append(v)
    specs.append(pl.BlockSpec(inputs.shape, lambda i: (0, 0, 0)))
    return pl.pallas_call(
        lambda *refs: square_kernel(sizes, *refs),
        grid=(rows // tile,),
        in_specs=specs,
        out_specs=pl.BlockSpec((tile, cols), lambda i: (i, 0)),
        out_shape=jax.ShapeDtypeStruct((rows, cols), F32),
        compiler_params=pltpu.CompilerParams(vmem_limit_bytes=32 * 1024 * 1024),
        cost_estimate=pl.CostEstimate(
            flops=2 * sum(sizes) * SEQ_LEN * rows * cols, bytes_accessed=rows * cols * 4, transcendentals=0
        ),
    )(*operands, inputs)


def body(out_grads, layer_inputs, basis_out, basis_in):
    line = Line()
    one, two, three = (Chunk(line, basis_out) for _ in range(3))
    inputs = Inputs(line, basis_in)
    half = SEQ_LEN // 2

    def join(*rows):
        return jnp.concatenate(rows, axis=0)

    def join_far(low, high):
        return jnp.concatenate([low, high], axis=1).reshape(-1, low.shape[-1])

    near = swap(out_grads, "zl")
    before, after = shift_x(out_grads, 1), shift_x(out_grads, -1)
    inputs.rows(layer_inputs)
    inputs.rows_more()
    near = line.put(near)
    before_n, after_n = shift_x(near, 1), shift_x(near, -1)
    one.multiply(join, out_grads, near, before, after)
    inputs.rows_z()
    one.cross()
    low = shift_x(line.run(lambda u, v: jnp.stack([u[:half], v[:half]]), before, before_n), 1)
    high = shift_x(line.run(lambda u, v: jnp.stack([u[half:], v[half:]]), after, after_n), -1)
    two.multiply(join, before_n, after_n)
    two.cross()
    one.blocks()
    inputs.rows_cross()
    two.blocks()
    three.multiply(join_far, low, high)
    three.cross()
    inputs.multiply()
    inputs.reduce()
    one.reduce()
    three.blocks()
    two.reduce()
    one.exchange()
    inputs.reduce_more()
    three.reduce()
    two.exchange()
    inputs.exchange()
    three.exchange()
    one.gather()
    two.gather()
    inputs.gather()
    three.gather()
    one.gather_more()
    inputs.gather_more()
    two.gather_more()
    three.gather_more()
    one.cross_back()
    two.cross_back()
    x_rows = inputs.all()
    three.cross_back()
    return square_sum([(c.own, c.other) for c in (one, two, three)], x_rows)


def solution(mesh):
    fine = Mesh(mesh.devices.reshape(NX, NZL, NY, NZH, NC), ("x", "zl", "y", "zh", "core"))
    out, inn = ("x", "zl"), ("y", "zh", "core")
    return jax.shard_map(
        body,
        mesh=fine,
        in_specs=(P(out, inn), P(inn, out), P(inn, out), P(out, inn)),
        out_specs=P(out, inn),
        check_vma=False,
    )
```

time: 203 us -> 152 us (0.75)
  starting transfers between devices: 95.6 us -> 50.7 us
  waiting for transfers between devices: 61.2 us -> 37.4 us
  other arithmetic: 4.64 us -> 24 us
  matrix products: 27.1 us -> 18.4 us
  local copies, waits for them, and re-layouts: 3.32 us -> 9.43 us
    ppermute x14 -> x6, waiting for transfers between devices: 21.6 us -> 0.02 us  [shift_x(): return lax.ppermute(v, 'x', [(i, (i + by) % NX) for i in range(NX)])]
    ppermute x27 -> x18, starting transfers between devices: 42 us -> 23.9 us  [trade(): return lax.ppermute(v, (axis, 'core'), pairs)]
    ppermute x17 -> x13, starting transfers between devices: 36.2 us -> 18.9 us  [swap(): return lax.ppermute(v, axis, [(0, 1), (1, 0)])]
    ppermute x14 -> x6, starting transfers between devices: 17.4 us -> 7.9 us  [shift_x(): return lax.ppermute(v, 'x', [(i, (i + by) % NX) for i in range(NX)])]
    dot_general x7 -> x5, matrix products: 27.1 us -> 18.4 us  [the longest x3 16.8 us: step(): part = jnp.dot(lhs, self.basis, preferred_element_type=F32)]
    convert_element_type x16 -> x10, other arithmetic: 0.89 us -> 8.29 us  [the longest x2 3.38 us: step(): return ((next_ + r[1].astype(F32)).astype(BF), here + r[0].astype(F32))]
    add x5 -> x6, other arithmetic: 2.16 us -> 8.42 us  [the longest x3 4.96 us: block(): return pick(mine, y ^ bit, 1) + pick(theirs, y ^ bit, 1).astype(F32)]
    ppermute x27 -> x18, waiting for transfers between devices: 26.4 us -> 21.9 us  [trade(): return lax.ppermute(v, (axis, 'core'), pairs)]
  transfers between devices with their start and end apart: 58 -> 37, of which waited for: 19 -> 10; matrix products, arithmetic and copies ran while one was open for 13% -> 34% of each run, Pallas kernels for 0% -> 0%
where the time goes in v2:
time: 152 us; the launch traced here: 151 us
  starting transfers between devices  50.7 us (33%)
  waiting for transfers between devices  37.4 us (25%)
  other arithmetic  24 us (16%)
  matrix products  18.4 us (12%)
  Pallas kernels  10.6 us (7%)
  local copies, waits for them, and re-layouts  9.43 us (6%)
    ppermute x18, starting transfers between devices, trade(): return lax.ppermute(v, (axis, 'core'), pairs)  23.9 us
    ppermute x18, waiting for transfers between devices, trade(): return lax.ppermute(v, (axis, 'core'), pairs)  21.9 us
    ppermute x13, starting transfers between devices, swap(): return lax.ppermute(v, axis, [(0, 1), (1, 0)])  18.9 us
    dot_general x3, matrix products, step(): part = jnp.dot(lhs, self.basis, preferred_element_type=F32)  16.8 us
    ppermute x13, waiting for transfers between devices, swap(): return lax.ppermute(v, axis, [(0, 1), (1, 0)])  15.5 us
    pallas_call x1, Pallas kernels, square_sum(): pl.pallas_call(lambda *refs: square_kernel(sizes, *refs), grid=(rows // t...  10.6 us
    ppermute x6, starting transfers between devices, shift_x(): return lax.ppermute(v, 'x', [(i, (i + by) % NX) for i in range(NX)])  7.9 us
    add x3, other arithmetic, block(): return pick(mine, y ^ bit, 1) + pick(theirs, y ^ bit, 1).astype(F32)  4.96 us
  transfers between devices with their start and end apart: 37, of which 10 were waited for; matrix products, arithmetic and copies ran while one was open for 34% of the time, Pallas kernels for 0%

profile of v2, /device:TPU:1, one launch (start us, length us, event | category | flops | bytes accessed | tf_op | source)
XLA Modules:
  0.0 151.0 jit_solution(9789672760879690115)
XLA Ops:
  0.0 2.0 %collective-permute-start.2 = (bf16[128,1792]{1,0:T(8,128)(2,1)}, bf16[128,1792]{1,0:T(8,128)(2,1)S(1)}, u32[]{:S(2)}, u32[]{:S(2)}) collective-permute-start(bf16[128,1792]{1,0:T(8,128)(2,1)} %param.4), channel_id=1, source_target_pairs={{0,32},{32,64},{64,96},{96,0},{1,33},{33,65},{65,97},{97,1},{2,34}... | collective-permute-start | bytes 1376264 | tf_op jit(solution)/shard_map/ppermute | solution.py:21
  10.4 2.8 %collective-permute-start.7 = (bf16[2,64,1024]{2,1,0:T(8,128)(2,1)S(1)}, bf16[2,64,1024]{2,1,0:T(8,128)(2,1)S(1)}, u32[]{:S(2)}, u32[]{:S(2)}) collective-permute-start(bf16[2,64,1024]{2,1,0:T(8,128)(2,1)S(1)} %pad_maximum_fusion.14), channel_id=1, source_target_pairs={{0,4},{1,13},{4,0},{5,9},{8,12},{9,5},{12,8},{13,1},{2,6},{3,15},{... | collective-permute-start | bytes 786440 | tf_op jit(solution)/shard_map/ppermute | solution.py:33
  15.3 9.9 %fusion.13 = f32[512,3584]{1,0:T(8,128)S(1)} fusion(bf16[1792,3584]{1,0:T(8,128)(2,1)} %param.6, bf16[128,1792]{1,0:T(8,128)(2,1)S(1)} %collective-permute-done.3, bf16[128,1792]{1,0:T(8,128)(2,1)S(1)} %collective-permute-done.2, bf16[128,1792]{1,0:T(8,128)(2,1)S(1)} %collective-permute-done, bf16[128,1792]{1,0:T(8,128)(2,1)} %param.4), kind=kOutput, calls=%fused_computation.15 | convolution fusion | flops 6584008704 | bytes 22020096 | tf_op jit(solution)/shard_map/dot_general | solution.py:70
  25.7 2.2 %collective-permute-start.4 = (bf16[4,4,16,3584]{3,2,0,1:T(8,128)(2,1)S(1)}, bf16[4,4,16,3584]{3,2,0,1:T(8,128)(2,1)S(1)}, u32[]{:S(2)}, u32[]{:S(2)}) collective-permute-start(bf16[4,4,16,3584]{3,2,0,1:T(8,128)(2,1)S(1)} %fusion.12), channel_id=1, source_target_pairs={{0,1},{1,0},{2,3},{3,2},{4,5},{5,4},{6,7},{7,6},{8,9},{9,8},{10,11... | collective-permute-start | bytes 5505032 | tf_op jit(solution)/shard_map/ppermute | solution.py:17
  28.0 3.5 %collective-permute-start.9 = (bf16[4,64,1024]{2,1,0:T(8,128)(2,1)S(1)}, bf16[4,64,1024]{2,1,0:T(8,128)(2,1)S(1)}, u32[]{:S(2)}, u32[]{:S(2)}) collective-permute-start(bf16[4,64,1024]{2,1,0:T(8,128)(2,1)S(1)} %constant_dynamic-update-slice_fusion), channel_id=1, source_target_pairs={{0,2},{2,0},{1,3},{3,1},{4,6},{6,4},{5,7},{7,5},{8,10},{10,8},{9,1... | collective-permute-start | bytes 1572872 | tf_op jit(solution)/shard_map/ppermute | solution.py:17
  34.5 3.5 %fusion.25 = f32[256,3584]{1,0:T(8,128)S(1)} fusion(bf16[1792,3584]{1,0:T(8,128)(2,1)S(1)} %copy-done.6, bf16[128,1792]{1,0:T(8,128)(2,1)S(1)} %collective-permute-done.6, bf16[128,1792]{1,0:T(8,128)(2,1)S(1)} %collective-permute-done.5), kind=kOutput, calls=%fused_computation.35 | convolution fusion | flops 3290169344 | bytes 17432576 | tf_op jit(solution)/shard_map/dot_general | solution.py:70
  41.9 2.7 %collective-permute-start.8 = (bf16[2,4,16,3584]{3,2,1,0:T(8,128)(2,1)}, bf16[2,4,16,3584]{3,2,1,0:T(8,128)(2,1)}, u32[]{:S(2)}, u32[]{:S(2)}) collective-permute-start(bf16[2,4,16,3584]{3,2,1,0:T(8,128)(2,1)} %pad_maximum_fusion.3), channel_id=1, source_target_pairs={{0,4},{1,13},{4,0},{5,9},{8,12},{9,5},{12,8},{13,1},{2,6},{3,15},{... | collective-permute-start | bytes 2752520 | tf_op jit(solution)/shard_map/ppermute | solution.py:33
  46.8 2.4 %collective-permute-start.15 = (bf16[2,2,16,3584]{3,2,1,0:T(8,128)(2,1)}, bf16[2,2,16,3584]{3,2,1,0:T(8,128)(2,1)}, u32[]{:S(2)}, u32[]{:S(2)}) collective-permute-start(bf16[2,2,16,3584]{3,2,1,0:T(8,128)(2,1)} %pad_maximum_fusion.10), channel_id=1, source_target_pairs={{0,4},{1,13},{4,0},{5,9},{8,12},{9,5},{12,8},{13,1},{2,6},{3,15},{... | collective-permute-start | bytes 1376264 | tf_op jit(solution)/shard_map/ppermute | solution.py:33
  49.3 3.5 %fusion = f32[2,2,4,16,3584]{4,3,2,1,0:T(8,128)S(1)} fusion(bf16[2,2,4,16,1792]{4,3,2,1,0:T(8,128)(2,1)S(1)} %bitcast.158, bf16[1792,3584]{1,0:T(8,128)(2,1)S(1)} %copy-done.6), kind=kOutput, calls=%fused_computation | convolution fusion | flops 3288334336 | bytes 17432576 | tf_op jit(solution)/shard_map/dot_general | solution.py:70
  58.0 2.0 %copy.21 = f32[1,2,128,512]{2,3,1,0:T(8,128)} copy(f32[1,2,128,512]{3,2,1,0:T(8,128)} %get-tuple-element.167) | data formatting | bytes 1048576 | tf_op jit(solution)/shard_map/stack | solution.py:163
  61.1 2.8 %collective-permute-start.19 = (f32[2,2,128,512]{2,3,1,0:T(8,128)S(1)}, f32[2,2,128,512]{2,3,1,0:T(8,128)S(1)}, u32[]{:S(2)}, u32[]{:S(2)}) collective-permute-start(f32[2,2,128,512]{2,3,1,0:T(8,128)S(1)} %pad_maximum_fusion.2), channel_id=1, source_target_pairs={{0,32},{1,97},{32,0},{33,65},{64,96},{65,33},{96,64},{97,1},{2,34}... | collective-permute-start | bytes 3145736 | tf_op jit(solution)/shard_map/ppermute | solution.py:33
  63.9 2.0 %fusion.29 = (bf16[4,16,3584]{2,1,0:T(8,128)(2,1)S(1)}, f32[4,16,3584]{2,1,0:T(8,128)S(1)}) fusion(f32[4,16,3584]{2,1,0:T(8,128)} %get-tuple-element.103, bf16[2,4,16,3584]{3,2,1,0:T(8,128)(2,1)} %collective-permute-done.8, f32[4,16,3584]{2,1,0:T(8,128)} %get-tuple-element.101), kind=kLoop, calls=%fused_computation.45 | loop fusion | flops 1146880 | bytes 4128768 | tf_op jit(solution)/shard_map/convert_element_type | solution.py:95
  66.0 2.1 %add_bitcast_fusion.3 = (f32[2,16,3584]{2,1,0:T(8,128)}, bf16[1,2,16,3584]{3,2,1,0:T(8,128)(2,1)S(1)}, bf16[1,2,16,3584]{3,2,1,0:T(8,128)(2,1)S(1)}) fusion(s32[]{:T(128)S(6)} %select_n.171, s32[]{:T(128)S(6)} %select_n.175, s32[]{:T(128)S(6)} %select_n.174, bf16[2,4,16,3584]{3,2,1,0:T(8,128)(2,1)} %collective-permute-done.16, ...), kind=kLoop, calls=%fused_computation.80 | loop fusion | flops 917504 | bytes 2981900 | tf_op jit(solution)/shard_map/add | solution.py:85
  72.3 2.0 %convert_add_fusion.5 = (f32[2,16,3584]{2,1,0:T(8,128)}, bf16[2,16,3584]{2,1,0:T(8,128)(2,1)}) fusion(f32[2,16,3584]{2,1,0:T(8,128)S(1)} %copy-done.3, bf16[2,2,16,3584]{3,2,1,0:T(8,128)(2,1)} %collective-permute-done.15, f32[2,16,3584]{2,1,0:T(8,128)S(1)} %copy-done.2), kind=kLoop, calls=%fused_computation.72 | loop fusion | flops 573440 | bytes 2064384 | tf_op jit(solution)/shard_map/add | solution.py:95
  76.0 3.0 %collective-permute-start.17 = (bf16[4,16,3584]{2,1,0:T(8,128)(2,1)}, bf16[4,16,3584]{2,1,0:T(8,128)(2,1)}, u32[]{:S(2)}, u32[]{:S(2)}) collective-permute-start(bf16[4,16,3584]{2,1,0:T(8,128)(2,1)} %get-tuple-element.151), channel_id=1, source_target_pairs={{0,2},{2,0},{1,3},{3,1},{4,6},{6,4},{5,7},{7,5},{8,10},{10,8},{9,1... | collective-permute-start | bytes 1376264 | tf_op jit(solution)/shard_map/ppermute | solution.py:17
  86.8 4.4 %collective-permute-done.21 = f32[2,128,512]{1,2,0:T(8,128)S(1)} collective-permute-done((f32[2,128,512]{1,2,0:T(8,128)S(1)}, f32[2,128,512]{1,2,0:T(8,128)S(1)}, u32[]{:S(2)}, u32[]{:S(2)}) %collective-permute-start.21) | collective-permute-done | bytes 524320 | tf_op jit(solution)/shard_map/ppermute | solution.py:33
  96.0 8.7 %collective-permute-done.25 = f32[2,128,512]{1,2,0:T(8,128)S(1)} collective-permute-done((f32[2,128,512]{1,2,0:T(8,128)S(1)}, f32[2,128,512]{1,2,0:T(8,128)S(1)}, u32[]{:S(2)}, u32[]{:S(2)}) %collective-permute-start.25) | collective-permute-done | bytes 524320 | tf_op jit(solution)/shard_map/ppermute | solution.py:17
  105.3 4.1 %collective-permute-done.24 = bf16[2,16,3584]{2,1,0:T(8,128)(2,1)S(1)} collective-permute-done((bf16[2,16,3584]{2,1,0:T(8,128)(2,1)S(1)}, bf16[2,16,3584]{2,1,0:T(8,128)(2,1)S(1)}, u32[]{:S(2)}, u32[]{:S(2)}) %collective-permute-start.24) | collective-permute-done | bytes 229408 | tf_op jit(solution)/shard_map/ppermute | solution.py:17
  114.5 2.7 %collective-permute-start.34 = (bf16[2,2,16,3584]{3,2,1,0:T(8,128)(2,1)S(1)}, bf16[2,2,16,3584]{3,2,1,0:T(8,128)(2,1)S(1)}, u32[]{:S(2)}, u32[]{:S(2)}) collective-permute-start(bf16[2,2,16,3584]{3,2,1,0:T(8,128)(2,1)S(1)} %pad_maximum_fusion.13), channel_id=1, source_target_pairs={{0,4},{1,13},{4,0},{5,9},{8,12},{9,5},{12,8},{13,1},{2,6},{3,15},{... | collective-permute-start | bytes 1376264 | tf_op jit(solution)/shard_map/ppermute | solution.py:33
  117.2 9.5 %collective-permute-done.27 = bf16[2,4,16,3584]{3,2,0,1:T(8,128)(2,1)S(1)} collective-permute-done((bf16[2,4,16,3584]{3,2,0,1:T(8,128)(2,1)S(1)}, bf16[2,4,16,3584]{3,2,0,1:T(8,128)(2,1)S(1)}, u32[]{:S(2)}, u32[]{:S(2)}) %collective-permute-start.27) | collective-permute-done | bytes 917536 | tf_op jit(solution)/shard_map/ppermute | solution.py:33
  128.5 3.1 %collective-permute-done.32 = bf16[2,2,16,3584]{3,2,0,1:T(8,128)(2,1)S(1)} collective-permute-done((bf16[2,2,16,3584]{3,2,0,1:T(8,128)(2,1)S(1)}, bf16[2,2,16,3584]{3,2,0,1:T(8,128)(2,1)S(1)}, u32[]{:S(2)}, u32[]{:S(2)}) %collective-permute-start.32) | collective-permute-done | bytes 458784 | tf_op jit(solution)/shard_map/ppermute | solution.py:33
  133.6 3.0 %collective-permute-done.34 = bf16[2,2,16,3584]{3,2,1,0:T(8,128)(2,1)S(1)} collective-permute-done((bf16[2,2,16,3584]{3,2,1,0:T(8,128)(2,1)S(1)}, bf16[2,2,16,3584]{3,2,1,0:T(8,128)(2,1)S(1)}, u32[]{:S(2)}, u32[]{:S(2)}) %collective-permute-start.34) | collective-permute-done | bytes 458784 | tf_op jit(solution)/shard_map/ppermute | solution.py:33
  138.4 2.1 %collective-permute-done.36.refs_5_ = bf16[2,64,3584]{2,1,0:T(8,128)(2,1)S(1)} collective-permute-done((bf16[2,64,3584]{2,1,0:T(8,128)(2,1)S(1)}, bf16[2,64,3584]{2,1,0:T(8,128)(2,1)S(1)}, u32[]{:S(2)}, u32[]{:S(2)}) %collective-permute-start.36) | collective-permute-done | bytes 917536 | tf_op jit(solution)/shard_map/ppermute | solution.py:17
  140.5 10.6 %shard_map.46 = f32[3584,512]{1,0:T(8,128)} custom-call(bf16[4,64,3584]{2,1,0:T(8,128)(2,1)S(1)} %bitcast.145, bf16[4,64,3584]{2,1,0:T(8,128)(2,1)S(1)} %collective-permute-done.31.refs_1_, bf16[2,64,3584]{2,1,0:T(8,128)(2,1)S(1)} %bitcast.147, bf16[2,64,3584]{2,1,0:T(8,128)(2,1)S(1)} %collective-permute-done.33.refs_3_, bf16[2,64,3584]{2,1,0:T(8,128)(2,1)S(1)} %bitcast.149, ...), custom_call_target="tpu_custom_call" | custom-call | flops 3758096384 | bytes 7340032 | tf_op jit(solution)/shard_map/pallas_call | solution.py:233
  (145 shorter events, 56.2 us)
Async XLA Ops:
  0.0 15.3 %collective-permute-start.2 = (bf16[128,1792]{1,0:T(8,128)(2,1)}, bf16[128,1792]{1,0:T(8,128)(2,1)S(1)}, u32[]{:S(2)}, u32[]{:S(2)}) collective-permute-start(bf16[128,1792]{1,0:T(8,128)(2,1)} %param.4), channel_id=1, source_target_pairs={{0,32},{32,64},{64,96},{96,0},{1,33},{33,65},{65,97},{97,1},{2,34}... | collective-permute-start | bytes 1376264 | tf_op jit(solution)/shard_map/ppermute | solution.py:21
  2.0 11.7 %collective-permute-start = (bf16[128,1792]{1,0:T(8,128)(2,1)}, bf16[128,1792]{1,0:T(8,128)(2,1)S(1)}, u32[]{:S(2)}, u32[]{:S(2)}) collective-permute-start(bf16[128,1792]{1,0:T(8,128)(2,1)} %param.4), channel_id=1, source_target_pairs={{0,16},{16,0},{1,17},{17,1},{2,18},{18,2},{3,19},{19,3},{4,20},{20... | collective-permute-start | bytes 1376264 | tf_op jit(solution)/shard_map/ppermute | solution.py:17
  10.4 17.5 %collective-permute-start.7 = (bf16[2,64,1024]{2,1,0:T(8,128)(2,1)S(1)}, bf16[2,64,1024]{2,1,0:T(8,128)(2,1)S(1)}, u32[]{:S(2)}, u32[]{:S(2)}) collective-permute-start(bf16[2,64,1024]{2,1,0:T(8,128)(2,1)S(1)} %pad_maximum_fusion.14), channel_id=1, source_target_pairs={{0,4},{1,13},{4,0},{5,9},{8,12},{9,5},{12,8},{13,1},{2,6},{3,15},{... | collective-permute-start | bytes 786440 | tf_op jit(solution)/shard_map/ppermute | solution.py:33
  13.8 19.0 %collective-permute-start.6 = (bf16[128,1792]{1,0:T(8,128)(2,1)S(1)}, bf16[128,1792]{1,0:T(8,128)(2,1)S(1)}, u32[]{:S(2)}, u32[]{:S(2)}) collective-permute-start(bf16[128,1792]{1,0:T(8,128)(2,1)S(1)} %collective-permute-done), channel_id=1, source_target_pairs={{0,96},{32,0},{64,32},{96,64},{1,97},{33,1},{65,33},{97,65},{2,98}... | collective-permute-start | bytes 1376264 | tf_op jit(solution)/shard_map/ppermute | solution.py:21
  15.3 16.1 %collective-permute-start.5 = (bf16[128,1792]{1,0:T(8,128)(2,1)S(1)}, bf16[128,1792]{1,0:T(8,128)(2,1)S(1)}, u32[]{:S(2)}, u32[]{:S(2)}) collective-permute-start(bf16[128,1792]{1,0:T(8,128)(2,1)S(1)} %collective-permute-done), channel_id=1, source_target_pairs={{0,32},{32,64},{64,96},{96,0},{1,33},{33,65},{65,97},{97,1},{2,34}... | collective-permute-start | bytes 1376264 | tf_op jit(solution)/shard_map/ppermute | solution.py:21
  25.7 13.4 %collective-permute-start.4 = (bf16[4,4,16,3584]{3,2,0,1:T(8,128)(2,1)S(1)}, bf16[4,4,16,3584]{3,2,0,1:T(8,128)(2,1)S(1)}, u32[]{:S(2)}, u32[]{:S(2)}) collective-permute-start(bf16[4,4,16,3584]{3,2,0,1:T(8,128)(2,1)S(1)} %fusion.12), channel_id=1, source_target_pairs={{0,1},{1,0},{2,3},{3,2},{4,5},{5,4},{6,7},{7,6},{8,9},{9,8},{10,11... | collective-permute-start | bytes 5505032 | tf_op jit(solution)/shard_map/ppermute | solution.py:17
  28.0 16.7 %collective-permute-start.9 = (bf16[4,64,1024]{2,1,0:T(8,128)(2,1)S(1)}, bf16[4,64,1024]{2,1,0:T(8,128)(2,1)S(1)}, u32[]{:S(2)}, u32[]{:S(2)}) collective-permute-start(bf16[4,64,1024]{2,1,0:T(8,128)(2,1)S(1)} %constant_dynamic-update-slice_fusion), channel_id=1, source_target_pairs={{0,2},{2,0},{1,3},{3,1},{4,6},{6,4},{5,7},{7,5},{8,10},{10,8},{9,1... | collective-permute-start | bytes 1572872 | tf_op jit(solution)/shard_map/ppermute | solution.py:17
  31.5 17.7 %collective-permute-start.11 = (bf16[2,64,1792]{2,1,0:T(8,128)(2,1)S(1)}, bf16[2,64,1792]{2,1,0:T(8,128)(2,1)S(1)}, u32[]{:S(2)}, u32[]{:S(2)}) collective-permute-start(bf16[2,64,1792]{2,1,0:T(8,128)(2,1)S(1)} %pad_maximum_fusion.8), channel_id=1, source_target_pairs={{0,32},{32,64},{64,96},{96,0},{1,33},{33,65},{65,97},{97,1},{2,34}... | collective-permute-start | bytes 1376264 | tf_op jit(solution)/shard_map/ppermute | solution.py:21
  32.9 16.3 %collective-permute-start.12 = (bf16[2,64,1792]{2,1,0:T(8,128)(2,1)S(1)}, bf16[2,64,1792]{2,1,0:T(8,128)(2,1)S(1)}, u32[]{:S(2)}, u32[]{:S(2)}) collective-permute-start(bf16[2,64,1792]{2,1,0:T(8,128)(2,1)S(1)} %pad_maximum_fusion.9), channel_id=1, source_target_pairs={{0,96},{32,0},{64,32},{96,64},{1,97},{33,1},{65,33},{97,65},{2,98}... | collective-permute-start | bytes 1376264 | tf_op jit(solution)/shard_map/ppermute | solution.py:21
  41.9 22.0 %collective-permute-start.8 = (bf16[2,4,16,3584]{3,2,1,0:T(8,128)(2,1)}, bf16[2,4,16,3584]{3,2,1,0:T(8,128)(2,1)}, u32[]{:S(2)}, u32[]{:S(2)}) collective-permute-start(bf16[2,4,16,3584]{3,2,1,0:T(8,128)(2,1)} %pad_maximum_fusion.3), channel_id=1, source_target_pairs={{0,4},{1,13},{4,0},{5,9},{8,12},{9,5},{12,8},{13,1},{2,6},{3,15},{... | collective-permute-start | bytes 2752520 | tf_op jit(solution)/shard_map/ppermute | solution.py:33
  46.8 25.5 %collective-permute-start.15 = (bf16[2,2,16,3584]{3,2,1,0:T(8,128)(2,1)}, bf16[2,2,16,3584]{3,2,1,0:T(8,128)(2,1)}, u32[]{:S(2)}, u32[]{:S(2)}) collective-permute-start(bf16[2,2,16,3584]{3,2,1,0:T(8,128)(2,1)} %pad_maximum_fusion.10), channel_id=1, source_target_pairs={{0,4},{1,13},{4,0},{5,9},{8,12},{9,5},{12,8},{13,1},{2,6},{3,15},{... | collective-permute-start | bytes 1376264 | tf_op jit(solution)/shard_map/ppermute | solution.py:33
  53.8 12.1 %collective-permute-start.16 = (bf16[2,4,16,3584]{3,2,1,0:T(8,128)(2,1)}, bf16[2,4,16,3584]{3,2,1,0:T(8,128)(2,1)}, u32[]{:S(2)}, u32[]{:S(2)}) collective-permute-start(bf16[2,4,16,3584]{3,2,1,0:T(8,128)(2,1)} %fusion.23), channel_id=1, source_target_pairs={{0,1},{1,0},{2,3},{3,2},{4,5},{5,4},{6,7},{7,6},{8,9},{9,8},{10,11... | collective-permute-start | bytes 2752520 | tf_op jit(solution)/shard_map/ppermute | solution.py:17
  61.1 17.8 %collective-permute-start.19 = (f32[2,2,128,512]{2,3,1,0:T(8,128)S(1)}, f32[2,2,128,512]{2,3,1,0:T(8,128)S(1)}, u32[]{:S(2)}, u32[]{:S(2)}) collective-permute-start(f32[2,2,128,512]{2,3,1,0:T(8,128)S(1)} %pad_maximum_fusion.2), channel_id=1, source_target_pairs={{0,32},{1,97},{32,0},{33,65},{64,96},{65,33},{96,64},{97,1},{2,34}... | collective-permute-start | bytes 3145736 | tf_op jit(solution)/shard_map/ppermute | solution.py:33
  68.8 14.0 %collective-permute-start.18 = (bf16[2,2,16,3584]{3,2,1,0:T(8,128)(2,1)}, bf16[2,2,16,3584]{3,2,1,0:T(8,128)(2,1)}, u32[]{:S(2)}, u32[]{:S(2)}) collective-permute-start(bf16[2,2,16,3584]{3,2,1,0:T(8,128)(2,1)} %pad_maximum_fusion.11), channel_id=1, source_target_pairs={{0,4},{1,13},{4,0},{5,9},{8,12},{9,5},{12,8},{13,1},{2,6},{3,15},{... | collective-permute-start | bytes 1376264 | tf_op jit(solution)/shard_map/ppermute | solution.py:33
  76.0 17.2 %collective-permute-start.17 = (bf16[4,16,3584]{2,1,0:T(8,128)(2,1)}, bf16[4,16,3584]{2,1,0:T(8,128)(2,1)}, u32[]{:S(2)}, u32[]{:S(2)}) collective-permute-start(bf16[4,16,3584]{2,1,0:T(8,128)(2,1)} %get-tuple-element.151), channel_id=1, source_target_pairs={{0,2},{2,0},{1,3},{3,1},{4,6},{6,4},{5,7},{7,5},{8,10},{10,8},{9,1... | collective-permute-start | bytes 1376264 | tf_op jit(solution)/shard_map/ppermute | solution.py:17
  91.2 13.4 %collective-permute-start.25 = (f32[2,128,512]{1,2,0:T(8,128)S(1)}, f32[2,128,512]{1,2,0:T(8,128)S(1)}, u32[]{:S(2)}, u32[]{:S(2)}) collective-permute-start(f32[2,128,512]{1,2,0:T(8,128)S(1)} %add.282), channel_id=1, source_target_pairs={{0,16},{16,0},{1,17},{17,1},{2,18},{18,2},{3,19},{19,3},{4,20},{20... | collective-permute-start | bytes 1572872 | tf_op jit(solution)/shard_map/ppermute | solution.py:17
  92.1 17.3 %collective-permute-start.24 = (bf16[2,16,3584]{2,1,0:T(8,128)(2,1)S(1)}, bf16[2,16,3584]{2,1,0:T(8,128)(2,1)S(1)}, u32[]{:S(2)}, u32[]{:S(2)}) collective-permute-start(bf16[2,16,3584]{2,1,0:T(8,128)(2,1)S(1)} %get-tuple-element.147), channel_id=1, source_target_pairs={{0,2},{2,0},{1,3},{3,1},{4,6},{6,4},{5,7},{7,5},{8,10},{10,8},{9,1... | collective-permute-start | bytes 688136 | tf_op jit(solution)/shard_map/ppermute | solution.py:17
  94.3 16.3 %collective-permute-start.23 = (bf16[4,16,3584]{2,1,0:T(8,128)(2,1)S(1)}, bf16[4,16,3584]{2,1,0:T(8,128)(2,1)S(1)}, u32[]{:S(2)}, u32[]{:S(2)}) collective-permute-start(bf16[4,16,3584]{2,1,0:T(8,128)(2,1)S(1)} %add_convert_fusion), channel_id=1, source_target_pairs={{0,12},{1,5},{4,8},{5,1},{8,4},{9,13},{12,0},{13,9},{2,14},{3,7},{... | collective-permute-start | bytes 1376264 | tf_op jit(solution)/shard_map/ppermute | solution.py:33
  95.2 19.1 %collective-permute-start.29 = (bf16[2,16,3584]{2,1,0:T(8,128)(2,1)S(1)}, bf16[2,16,3584]{2,1,0:T(8,128)(2,1)S(1)}, u32[]{:S(2)}, u32[]{:S(2)}) collective-permute-start(bf16[2,16,3584]{2,1,0:T(8,128)(2,1)S(1)} %add_convert_fusion.5), channel_id=1, source_target_pairs={{0,12},{1,5},{4,8},{5,1},{8,4},{9,13},{12,0},{13,9},{2,14},{3,7},{... | collective-permute-start | bytes 688136 | tf_op jit(solution)/shard_map/ppermute | solution.py:33
  110.7 16.0 %collective-permute-start.27 = (bf16[2,4,16,3584]{3,2,0,1:T(8,128)(2,1)S(1)}, bf16[2,4,16,3584]{3,2,0,1:T(8,128)(2,1)S(1)}, u32[]{:S(2)}, u32[]{:S(2)}) collective-permute-start(bf16[2,4,16,3584]{3,2,0,1:T(8,128)(2,1)S(1)} %pad_maximum_fusion.5), channel_id=1, source_target_pairs={{0,4},{1,13},{4,0},{5,9},{8,12},{9,5},{12,8},{13,1},{2,6},{3,15},{... | collective-permute-start | bytes 2752520 | tf_op jit(solution)/shard_map/ppermute | solution.py:33
  112.5 20.9 %collective-permute-start.35 = (bf16[2,2,128,512]{3,2,1,0:T(8,128)(2,1)S(1)}, bf16[2,2,128,512]{3,2,1,0:T(8,128)(2,1)S(1)}, u32[]{:S(2)}, u32[]{:S(2)}) collective-permute-start(bf16[2,2,128,512]{3,2,1,0:T(8,128)(2,1)S(1)} %pad_maximum_fusion.7), channel_id=1, source_target_pairs={{0,32},{1,97},{32,0},{33,65},{64,96},{65,33},{96,64},{97,1},{2,34}... | collective-permute-start | bytes 1572872 | tf_op jit(solution)/shard_map/ppermute | solution.py:33
  114.3 17.3 %collective-permute-start.32 = (bf16[2,2,16,3584]{3,2,0,1:T(8,128)(2,1)S(1)}, bf16[2,2,16,3584]{3,2,0,1:T(8,128)(2,1)S(1)}, u32[]{:S(2)}, u32[]{:S(2)}) collective-permute-start(bf16[2,2,16,3584]{3,2,0,1:T(8,128)(2,1)S(1)} %pad_maximum_fusion.12), channel_id=1, source_target_pairs={{0,4},{1,13},{4,0},{5,9},{8,12},{9,5},{12,8},{13,1},{2,6},{3,15},{... | collective-permute-start | bytes 1376264 | tf_op jit(solution)/shard_map/ppermute | solution.py:33
  114.5 22.0 %collective-permute-start.34 = (bf16[2,2,16,3584]{3,2,1,0:T(8,128)(2,1)S(1)}, bf16[2,2,16,3584]{3,2,1,0:T(8,128)(2,1)S(1)}, u32[]{:S(2)}, u32[]{:S(2)}) collective-permute-start(bf16[2,2,16,3584]{3,2,1,0:T(8,128)(2,1)S(1)} %pad_maximum_fusion.13), channel_id=1, source_target_pairs={{0,4},{1,13},{4,0},{5,9},{8,12},{9,5},{12,8},{13,1},{2,6},{3,15},{... | collective-permute-start | bytes 1376264 | tf_op jit(solution)/shard_map/ppermute | solution.py:33
  126.9 13.6 %collective-permute-start.31 = (bf16[4,64,3584]{2,1,0:T(8,128)(2,1)S(1)}, bf16[4,64,3584]{2,1,0:T(8,128)(2,1)S(1)}, u32[]{:S(2)}, u32[]{:S(2)}) collective-permute-start(bf16[4,64,3584]{2,1,0:T(8,128)(2,1)S(1)} %bitcast.144), channel_id=1, source_target_pairs={{0,1},{1,0},{2,3},{3,2},{4,5},{5,4},{6,7},{7,6},{8,9},{9,8},{10,11... | collective-permute-start | bytes 5505032 | tf_op jit(solution)/shard_map/ppermute | solution.py:17
  (25 other events, 265.2 us)

commit v3 on v2

v3 whole, which is shorter than its diff:
```python
import jax
import jax.numpy as jnp
from jax import lax
from jax.experimental import pallas as pl
from jax.experimental.pallas import tpu as pltpu
from jax.sharding import Mesh
from jax.sharding import PartitionSpec as P

SEQ_LEN = 128
NX, NZL, NY, NZH, NC = 4, 2, 4, 2, 2
BLK = SEQ_LEN // (NY * NC)
BF = jnp.bfloat16
F32 = jnp.float32


def swap(v, axis):
    return lax.ppermute(v, axis, [(0, 1), (1, 0)])


def shift_x(v, by):
    return lax.ppermute(v, "x", [(i, (i + by) % NX) for i in range(NX)])


def near_bit():
    return jnp.where(lax.axis_index("core") == 0, 1, 3)


def trade(v, axis, other=False):
    pairs = []
    for i in range(4):
        for core, bit in ((0, 1), (1, 3)):
            pairs.append((i * NC + core, (i ^ (4 - bit if other else bit)) * NC + core))
    return lax.ppermute(v, (axis, "core"), pairs)


def pick(v, index, axis):
    return lax.dynamic_index_in_dim(v, index, axis, keepdims=False)


class Line:
    def __init__(self):
        self.last = ()

    def run(self, step, received, *at_hand):
        received = lax.optimization_barrier((received,) + self.last)[0]
        result = step(received, *at_hand)
        self.last = (result[0] if isinstance(result, tuple) else result,)
        return result

    def put(self, v):
        return self.run(lambda u: u, v)


def order_matrix(half, block):
    i = lax.broadcasted_iota(jnp.int32, (SEQ_LEN, SEQ_LEN), 0)
    j = lax.broadcasted_iota(jnp.int32, (SEQ_LEN, SEQ_LEN), 1)
    h, t, r = i // (NY * BLK), (i // BLK) % NY, i % BLK
    return (half(h) * (NY * BLK) + block(h, t) * BLK + r == j).astype(BF)


def bit_of(t, first, second):
    return jnp.where(t == 0, 0, jnp.where(t == 3, 2, jnp.where(t == 1, first, second)))


def to_send_order(v):
    y, a, core = lax.axis_index("y"), near_bit(), lax.axis_index("core")

    def block(h, t):
        ha = jnp.where(h == 0, 4 - a, a)
        return y ^ bit_of((t + 2) % NY, 4 - ha, ha)

    hot = order_matrix(lambda h: (core + 1 + h) % 2, block)
    return jnp.dot(hot, v, preferred_element_type=F32).astype(BF)


def to_gather_order(v):
    y, a = lax.axis_index("y"), near_bit()

    def block(h, t):
        ha = jnp.where(h == 0, a, 4 - a)
        return y ^ bit_of(t, 4 - ha, ha)

    hot = order_matrix(lambda h: h, block)
    return jnp.einsum("ij,njk->nik", hot, v, preferred_element_type=F32).astype(BF)


def to_blocks(rows):
    k = rows[0].shape[-1]
    return jnp.stack([v.reshape(NC, NY, BLK, k) for v in rows], axis=2).reshape(NC, -1, k)


class Chunk:
    def __init__(self, line, basis, n):
        self.line, self.basis, self.n = line, basis, n

    def dot(self, rows):
        return jnp.dot(rows, self.basis, preferred_element_type=F32)

    def shape(self, v):
        return v.reshape(-1, self.n, BLK, v.shape[-1])

    def multiply(self, join, received, *at_hand):
        def step(received, *at_hand):
            rows = to_blocks(join(received, *at_hand))
            if self.n > 2:
                return self.dot(rows[0]).astype(BF), rows[1]
            part = self.dot(rows.reshape(-1, rows.shape[-1]))
            half = part.shape[0] // 2
            return part[:half].astype(BF), part[half:]

        send, self.mine = self.line.run(step, received, *at_hand)
        self.r = swap(self.shape(send), "core")
        if self.n > 2:
            self.mine = self.line.run(self.dot, self.mine)
        self.mine = self.shape(self.mine)

    def blocks(self):
        def step(r, mine):
            return (mine[:2] + r[:2].astype(F32)).astype(BF), mine[2:] + r[2:].astype(F32)

        send, self.here = self.line.run(step, self.r, self.mine)
        self.r = trade(send, "y")

    def reduce(self):
        def step(r, here):
            return (here[1] + r[1].astype(F32)).astype(BF), here[0] + r[0].astype(F32)

        send, self.here = self.line.run(step, self.r, self.here)
        self.r = trade(send, "y", other=True)

    def exchange(self):
        def step(r, here):
            total = here + r.astype(F32)
            return total.astype(BF), total

        send, self.here = self.line.run(step, self.r, self.here)
        self.r = swap(send, "zh")

    def gather(self):
        self.g = self.line.run(lambda r, u: (u + r.astype(F32)).astype(BF), self.r, self.here)
        self.r = trade(self.g, "y", other=True)

    def gather_more(self):
        self.g = self.line.run(lambda r, u: jnp.stack([u, r]), self.r, self.g)
        self.r = trade(self.g, "y")

    def cross_back(self):
        def step(r, u):
            own = jnp.concatenate([u, r], axis=0).swapaxes(0, 1)
            return own.reshape(own.shape[0], NY * BLK, own.shape[-1])

        self.own = self.line.run(step, self.r, self.g)
        self.other = swap(self.own, "core")


def part_kernel(own_at, other_at, own, other, basis, out):
    rows = jnp.concatenate([own[0, 0], other[0, 0], own[1, 0], other[1, 0]], axis=0)
    part = jnp.dot(rows, basis[...], preferred_element_type=F32)
    out[...] = part.reshape(out.shape)


def part_sums(own_at, other_at, own, other, basis):
    steps, (k, width) = own_at.shape[0], basis.shape
    block = (NZH, 1) + own.shape[2:]
    return pl.pallas_call(
        part_kernel,
        grid_spec=pltpu.PrefetchScalarGridSpec(
            num_scalar_prefetch=2,
            grid=(steps,),
            in_specs=[
                pl.BlockSpec(block, lambda i, own_at, other_at: (0, own_at[i], 0, 0)),
                pl.BlockSpec(block, lambda i, own_at, other_at: (0, other_at[i], 0, 0)),
                pl.BlockSpec((k, width), lambda i, own_at, other_at: (0, 0)),
            ],
            out_specs=pl.BlockSpec((1, NZH, SEQ_LEN, width), lambda i, own_at, other_at: (i, 0, 0, 0)),
        ),
        out_shape=jax.ShapeDtypeStruct((steps, NZH, SEQ_LEN, width), F32),
        compiler_params=pltpu.CompilerParams(vmem_limit_bytes=16 * 1024 * 1024),
        cost_estimate=pl.CostEstimate(
            flops=2 * steps * NZH * SEQ_LEN * k * width, bytes_accessed=k * width * 2, transcendentals=0
        ),
    )(own_at, other_at, own, other, basis)


class Inputs:
    def __init__(self, line, basis):
        self.line, self.basis = line, basis

    def rows(self, rows):
        self.g = rows
        self.r = trade(rows, "y", other=True)

    def rows_more(self):
        self.g = self.line.run(lambda r, u: jnp.stack([u, r]), self.r, self.g)
        self.r = trade(self.g, "y")

    def rows_z(self):
        self.g = self.line.run(lambda r, u: jnp.concatenate([u, r], axis=0), self.r, self.g)
        self.r = swap(self.g, "zh")

    def rows_cross(self):
        self.g = self.line.run(lambda r, u: jnp.stack([u, r]), self.r, self.g)
        self.r = swap(self.g, "core")

    def multiply(self):
        a = near_bit()
        off = lax.axis_index("y") ^ lax.axis_index("x")

        def at(bits, b):
            bits = jnp.stack([off ^ bit for bit in bits])
            return jnp.where(bits == 0, 0, jnp.where(bits == 2, 3, jnp.where(bits == b, 1, 2)))

        def step(r, g, bits):
            return part_sums(at(bits, 4 - a), at(bits, a), g, r, self.basis)

        send = self.line.run(lambda r, g: step(r, g, (a, 2)), self.r, self.g)
        other = self.r
        self.r = trade(send, "x")
        self.here = self.line.run(lambda r, g: step(r, g, (0, 4 - a)), other, self.g)

    def reduce(self):
        send, self.here = self.line.run(lambda r, u: (u[1] + r[1], u[0] + r[0]), self.r, self.here)
        self.r = trade(send, "x", other=True)

    def exchange(self):
        self.here = self.line.run(lambda r, u: u + r, self.r, self.here)
        self.r = swap(self.here, "zl")

    def gather(self):
        flip = lax.axis_index("zl") ^ lax.axis_index("zh")

        def step(r, u):
            total = (u + r).astype(BF)
            return to_gather_order(jnp.stack([pick(total, flip, 0), pick(total, 1 - flip, 0)]))

        self.g = self.line.run(step, self.r, self.here)
        self.r = trade(self.g, "x", other=True)

    def gather_more(self):
        self.g = self.line.run(lambda r, u: jnp.stack([u, r]), self.r, self.g)
        self.r = trade(self.g, "x")

    def all(self):
        straight = (lax.axis_index("x") + lax.axis_index("core")) % 2 == 0

        def step(r, g):
            before, after = jnp.where(straight, g[1], r[0]), jnp.where(straight, r[0], g[1])
            return jnp.stack(
                [g[0, 0], g[0, 1], before[0], after[0], before[1], after[1], r[1, 0], r[1, 1]]
            )

        return self.line.run(step, self.r, self.g)


def square_kernel(sizes, *refs):
    x_ref, out_ref = refs[-2], refs[-1]
    s = 0
    for c, n in enumerate(sizes):
        own, other = refs[2 * c], refs[2 * c + 1]
        for i in range(n):
            g = jnp.concatenate([own[i], other[i]], axis=0)
            p = lax.dot_general(g, x_ref[s], (((0,), (0,)), ((), ())), preferred_element_type=F32)
            if s == 0:
                out_ref[...] = p * p
            else:
                out_ref[...] += p * p
            s += 1
    out_ref[...] *= 1.0 / s


def square_sum(chunks, inputs):
    sizes = tuple(own.shape[0] for own, _ in chunks)
    rows = chunks[0][0].shape[2]
    cols = inputs.shape[2]
    tile = 512
    specs = []
    operands = []
    for own, other in chunks:
        for v in (own, other):
            specs.append(pl.BlockSpec((v.shape[0], v.shape[1], tile), lambda i: (0, 0, i)))
            operands.append(v)
    specs.append(pl.BlockSpec(inputs.shape, lambda i: (0, 0, 0)))
    return pl.pallas_call(
        lambda *refs: square_kernel(sizes, *refs),
        grid=(rows // tile,),
        in_specs=specs,
        out_specs=pl.BlockSpec((tile, cols), lambda i: (i, 0)),
        out_shape=jax.ShapeDtypeStruct((rows, cols), F32),
        compiler_params=pltpu.CompilerParams(vmem_limit_bytes=32 * 1024 * 1024),
        cost_estimate=pl.CostEstimate(
            flops=2 * sum(sizes) * SEQ_LEN * rows * cols, bytes_accessed=rows * cols * 4, transcendentals=0
        ),
    )(*operands, inputs)


def body(out_grads, layer_inputs, basis_out, basis_in):
    line = Line()
    one, two, three = (Chunk(line, basis_out, n) for n in (4, 2, 2))
    inputs = Inputs(line, basis_in)
    half = SEQ_LEN // 2

    inputs.rows(layer_inputs)
    own = to_send_order(out_grads)
    near = swap(own, "zl")
    before, after = shift_x(own, 1), shift_x(own, -1)
    inputs.rows_more()
    near = line.put(near)
    before_n, after_n = shift_x(near, 1), shift_x(near, -1)
    one.multiply(lambda u, *v: [own, near, *v, u], after, before)
    inputs.rows_z()
    one.blocks()
    low = shift_x(line.run(lambda v, u: jnp.stack([u[:half], v[:half]]), before_n, before), 1)
    high = shift_x(line.run(lambda v, u: jnp.stack([u[half:], v[half:]]), after_n, after), -1)
    two.multiply(lambda u, v: [u, v], before_n, after_n)
    inputs.rows_cross()
    two.blocks()
    inputs.multiply()
    three.multiply(lambda v, u: list(jnp.concatenate([u, v], axis=1)), high, low)
    one.reduce()
    three.blocks()
    two.reduce()
    one.exchange()
    inputs.reduce()
    three.reduce()
    two.exchange()
    one.gather()
    inputs.exchange()
    three.exchange()
    two.gather()
    one.gather_more()
    inputs.gather()
    three.gather()
    two.gather_more()
    inputs.gather_more()
    one.cross_back()
    three.gather_more()
    two.cross_back()
    x_rows = inputs.all()
    three.cross_back()
    return square_sum([(c.own, c.other) for c in (one, two, three)], x_rows)


def solution(mesh):
    fine = Mesh(mesh.devices.reshape(NX, NZL, NY, NZH, NC), ("x", "zl", "y", "zh", "core"))
    out, inn = ("x", "zl"), ("y", "zh", "core")
    return jax.shard_map(
        body,
        mesh=fine,
        in_specs=(P(out, inn), P(inn, out), P(inn, out), P(out, inn)),
        out_specs=P(out, inn),
        check_vma=False,
    )
```

time: 152 us -> 137 us (0.901)
  other arithmetic: 24 us -> 4.45 us
  starting transfers between devices: 50.7 us -> 57.5 us
  local copies, waits for them, and re-layouts: 9.43 us -> 3.05 us
  Pallas kernels: 10.6 us -> 13.7 us
    add x6 -> x4, other arithmetic: 8.42 us -> 0.52 us  [the longest x2 0.29 us: step(): mine[2:] + r[2:].astype(F32)]
    convert_element_type x7 -> x8, other arithmetic: 6.35 us -> 1.2 us  [the longest x1 0.48 us: step(): (mine[:2] + r[:2].astype(F32)).astype(BF)]
    ppermute x6, waiting for transfers between devices: 0.02 us -> 5.01 us  [shift_x(): return lax.ppermute(v, 'x', [(i, (i + by) % NX) for i in range(NX)])]
    ppermute x18, starting transfers between devices: 23.9 us -> 28.1 us  [trade(): return lax.ppermute(v, (axis, 'core'), pairs)]
    another operation x10, other arithmetic: 5.03 us -> 1.74 us  [the longest x1 0.93 us: rows_more(): self.g = self.line.run(lambda r, u: jnp.stack([u, r]), self.r, self.g)]
    another operation x2 -> x1, local copies, waits for them, and re-layouts: 3.27 us -> 0.06 us  [body(): list(jnp.concatenate([u, v], axis=1))]
    pallas_call x0 -> x2, Pallas kernels: none -> 3.1 us  [part_sums(): pl.pallas_call(part_kernel, grid_spec=pltpu.PrefetchScalarGridSpec(num_sc...]
    ppermute x18, waiting for transfers between devices: 21.9 us -> 19.3 us  [trade(): return lax.ppermute(v, (axis, 'core'), pairs)]
  transfers between devices with their start and end apart: 37 -> 37, of which waited for: 10 -> 17; matrix products, arithmetic and copies ran while one was open for 34% -> 18% of each run, Pallas kernels for 0% -> 2%
where the time goes in v3:
time: 137 us
  starting transfers between devices  57.5 us (42%)
  waiting for transfers between devices  38.3 us (28%)
  matrix products  19.5 us (14%)
  Pallas kernels  13.7 us (10%)
  other arithmetic  4.45 us (3%)
  local copies, waits for them, and re-layouts  3.05 us (2%)
    ppermute x18, starting transfers between devices, trade(): return lax.ppermute(v, (axis, 'core'), pairs)  28.1 us
    ppermute x13, starting transfers between devices, swap(): return lax.ppermute(v, axis, [(0, 1), (1, 0)])  21.3 us
    ppermute x18, waiting for transfers between devices, trade(): return lax.ppermute(v, (axis, 'core'), pairs)  19.3 us
    dot_general x4, matrix products, dot(): return jnp.dot(rows, self.basis, preferred_element_type=F32)  18.7 us
    ppermute x13, waiting for transfers between devices, swap(): return lax.ppermute(v, axis, [(0, 1), (1, 0)])  14 us
    pallas_call x1, Pallas kernels, square_sum(): pl.pallas_call(lambda *refs: square_kernel(sizes, *refs), grid=(rows // t...  10.6 us
    ppermute x6, starting transfers between devices, shift_x(): return lax.ppermute(v, 'x', [(i, (i + by) % NX) for i in range(NX)])  8.13 us
    ppermute x6, waiting for transfers between devices, shift_x(): return lax.ppermute(v, 'x', [(i, (i + by) % NX) for i in range(NX)])  5.01 us
  transfers between devices with their start and end apart: 37, of which 17 were waited for; matrix products, arithmetic and copies ran while one was open for 18% of the time, Pallas kernels for 2%

profile of v3, /device:TPU:1, one launch (start us, length us, event | category | flops | bytes accessed | tf_op | source)
XLA Modules:
  0.0 137.1 jit_solution(7401495228878685401)
XLA Ops:
  1.5 2.5 %collective-permute-start = (bf16[128,1792]{1,0:T(8,128)(2,1)S(1)}, bf16[128,1792]{1,0:T(8,128)(2,1)S(1)}, u32[]{:S(2)}, u32[]{:S(2)}) collective-permute-start(bf16[128,1792]{1,0:T(8,128)(2,1)S(1)} %convolution_convert_fusion.1), channel_id=1, source_target_pairs={{0,16},{16,0},{1,17},{17,1},{2,18},{18,2},{3,19},{19,3},{4,20},{20... | collective-permute-start | bytes 1376264 | tf_op jit(solution)/shard_map/ppermute | solution.py:17
  8.0 2.9 %collective-permute-done.1 = bf16[64,1024]{1,0:T(8,128)(2,1)S(1)} collective-permute-done((bf16[64,1024]{1,0:T(8,128)(2,1)}, bf16[64,1024]{1,0:T(8,128)(2,1)S(1)}, u32[]{:S(2)}, u32[]{:S(2)}) %collective-permute-start.1) | collective-permute-done | bytes 131104 | tf_op jit(solution)/shard_map/ppermute | solution.py:33
  11.8 2.8 %collective-permute-start.5 = (bf16[2,64,1024]{2,1,0:T(8,128)(2,1)S(1)}, bf16[2,64,1024]{2,1,0:T(8,128)(2,1)S(1)}, u32[]{:S(2)}, u32[]{:S(2)}) collective-permute-start(bf16[2,64,1024]{2,1,0:T(8,128)(2,1)S(1)} %pad_maximum_fusion.14), channel_id=1, source_target_pairs={{0,4},{1,13},{4,0},{5,9},{8,12},{9,5},{12,8},{13,1},{2,6},{3,15},{... | collective-permute-start | bytes 786440 | tf_op jit(solution)/shard_map/ppermute | solution.py:33
  14.6 2.7 %collective-permute-start.9 = (bf16[128,1792]{1,0:T(8,128)(2,1)S(1)}, bf16[128,1792]{1,0:T(8,128)(2,1)S(1)}, u32[]{:S(2)}, u32[]{:S(2)}) collective-permute-start(bf16[128,1792]{1,0:T(8,128)(2,1)S(1)} %collective-permute-done), channel_id=1, source_target_pairs={{0,96},{32,0},{64,32},{96,64},{1,97},{33,1},{65,33},{97,65},{2,98}... | collective-permute-start | bytes 1376264 | tf_op jit(solution)/shard_map/ppermute | solution.py:21
  18.9 8.3 %convolution_convert_fusion = bf16[256,3584]{1,0:T(8,128)(2,1)S(1)} fusion(bf16[256,1792]{1,0:T(8,128)(2,1)S(1)} %bitcast.177, bf16[1792,3584]{1,0:T(8,128)(2,1)} %param.6), kind=kOutput, calls=%fused_computation | convolution fusion | flops 3289251840 | bytes 15597568 | tf_op jit(solution)/shard_map/dot_general | solution.py:97
  29.4 3.5 %fusion.118 = f32[256,3584]{1,0:T(8,128)S(1)} fusion(bf16[256,1792]{1,0:T(8,128)(2,1)S(1)} %bitcast.176, bf16[1792,3584]{1,0:T(8,128)(2,1)S(1)} %bitcast.194), kind=kOutput, calls=%fused_computation.214 | convolution fusion | flops 3288334336 | bytes 17432576 | tf_op jit(solution)/shard_map/dot_general | solution.py:97
  33.0 3.4 %collective-permute-start.11 = (bf16[4,64,1024]{2,1,0:T(8,128)(2,1)S(1)}, bf16[4,64,1024]{2,1,0:T(8,128)(2,1)S(1)}, u32[]{:S(2)}, u32[]{:S(2)}) collective-permute-start(bf16[4,64,1024]{2,1,0:T(8,128)(2,1)S(1)} %get-tuple-element.92), channel_id=1, source_target_pairs={{0,2},{2,0},{1,3},{3,1},{4,6},{6,4},{5,7},{7,5},{8,10},{10,8},{9,1... | collective-permute-start | bytes 1572872 | tf_op jit(solution)/shard_map/ppermute | solution.py:17
  37.2 2.8 %collective-permute-start.6 = (bf16[2,4,16,3584]{3,2,1,0:T(8,128)(2,1)S(1)}, bf16[2,4,16,3584]{3,2,1,0:T(8,128)(2,1)S(1)}, u32[]{:S(2)}, u32[]{:S(2)}) collective-permute-start(bf16[2,4,16,3584]{3,2,1,0:T(8,128)(2,1)S(1)} %get-tuple-element.79), channel_id=1, source_target_pairs={{0,4},{1,13},{4,0},{5,9},{8,12},{9,5},{12,8},{13,1},{2,6},{3,15},{... | collective-permute-start | bytes 2752520 | tf_op jit(solution)/shard_map/ppermute | solution.py:33
  40.3 2.9 %collective-permute-start.10 = (bf16[2,64,1792]{2,1,0:T(8,128)(2,1)S(1)}, bf16[2,64,1792]{2,1,0:T(8,128)(2,1)S(1)}, u32[]{:S(2)}, u32[]{:S(2)}) collective-permute-start(bf16[2,64,1792]{2,1,0:T(8,128)(2,1)S(1)} %pad_maximum_fusion.11), channel_id=1, source_target_pairs={{0,96},{32,0},{64,32},{96,64},{1,97},{33,1},{65,33},{97,65},{2,98}... | collective-permute-start | bytes 1376264 | tf_op jit(solution)/shard_map/ppermute | solution.py:21
  43.3 3.5 %fusion.119 = f32[256,3584]{1,0:T(8,128)S(1)} fusion(bf16[256,1792]{1,0:T(8,128)(2,1)S(1)} %bitcast.184, bf16[1792,3584]{1,0:T(8,128)(2,1)S(1)} %bitcast.194), kind=kOutput, calls=%fused_computation.215 | convolution fusion | flops 3288334336 | bytes 17432576 | tf_op jit(solution)/shard_map/dot_general | solution.py:97
  49.5 3.8 %collective-permute-done.8 = bf16[2,64,1792]{2,1,0:T(8,128)(2,1)S(1)} collective-permute-done((bf16[2,64,1792]{2,1,0:T(8,128)(2,1)S(1)}, bf16[2,64,1792]{2,1,0:T(8,128)(2,1)S(1)}, u32[]{:S(2)}, u32[]{:S(2)}) %collective-permute-start.8) | collective-permute-done | bytes 458784 | tf_op jit(solution)/shard_map/ppermute | solution.py:21
  58.2 3.5 %fusion.120 = f32[256,3584]{1,0:T(8,128)S(1)} fusion(bf16[256,1792]{1,0:T(8,128)(2,1)S(1)} %bitcast.185, bf16[1792,3584]{1,0:T(8,128)(2,1)S(1)} %bitcast.194), kind=kOutput, calls=%fused_computation.216 | convolution fusion | flops 3288334336 | bytes 17432576 | tf_op jit(solution)/shard_map/dot_general | solution.py:97
  67.5 2.5 %collective-permute-done.14 = bf16[4,16,3584]{2,1,0:T(8,128)(2,1)S(1)} collective-permute-done((bf16[4,16,3584]{2,1,0:T(8,128)(2,1)S(1)}, bf16[4,16,3584]{2,1,0:T(8,128)(2,1)S(1)}, u32[]{:S(2)}, u32[]{:S(2)}) %collective-permute-start.14) | collective-permute-done | bytes 458784 | tf_op jit(solution)/shard_map/ppermute | solution.py:33
  71.5 7.3 %collective-permute-done.19 = bf16[2,2,16,3584]{3,2,1,0:T(8,128)(2,1)S(1)} collective-permute-done((bf16[2,2,16,3584]{3,2,1,0:T(8,128)(2,1)S(1)}, bf16[2,2,16,3584]{3,2,1,0:T(8,128)(2,1)S(1)}, u32[]{:S(2)}, u32[]{:S(2)}) %collective-permute-start.19) | collective-permute-done | bytes 458784 | tf_op jit(solution)/shard_map/ppermute | solution.py:33
  80.3 3.2 %collective-permute-start.21 = (bf16[4,16,3584]{2,1,0:T(8,128)(2,1)S(1)}, bf16[4,16,3584]{2,1,0:T(8,128)(2,1)S(1)}, u32[]{:S(2)}, u32[]{:S(2)}) collective-permute-start(bf16[4,16,3584]{2,1,0:T(8,128)(2,1)S(1)} %add_convert_fusion.1), channel_id=1, source_target_pairs={{0,12},{1,5},{4,8},{5,1},{8,4},{9,13},{12,0},{13,9},{2,14},{3,7},{... | collective-permute-start | bytes 1376264 | tf_op jit(solution)/shard_map/ppermute | solution.py:33
  84.1 3.6 %collective-permute-start.29 = (bf16[2,16,3584]{2,1,0:T(8,128)(2,1)S(1)}, bf16[2,16,3584]{2,1,0:T(8,128)(2,1)S(1)}, u32[]{:S(2)}, u32[]{:S(2)}) collective-permute-start(bf16[2,16,3584]{2,1,0:T(8,128)(2,1)S(1)} %fusion.22), channel_id=1, source_target_pairs={{0,2},{2,0},{1,3},{3,1},{4,6},{6,4},{5,7},{7,5},{8,10},{10,8},{9,1... | collective-permute-start | bytes 688136 | tf_op jit(solution)/shard_map/ppermute | solution.py:17
  89.8 4.0 %collective-permute-start.25 = (bf16[2,4,16,3584]{3,2,0,1:T(8,128)(2,1)S(1)}, bf16[2,4,16,3584]{3,2,0,1:T(8,128)(2,1)S(1)}, u32[]{:S(2)}, u32[]{:S(2)}) collective-permute-start(bf16[2,4,16,3584]{3,2,0,1:T(8,128)(2,1)S(1)} %pad_maximum_fusion.5), channel_id=1, source_target_pairs={{0,4},{1,13},{4,0},{5,9},{8,12},{9,5},{12,8},{13,1},{2,6},{3,15},{... | collective-permute-start | bytes 2752520 | tf_op jit(solution)/shard_map/ppermute | solution.py:33
  93.8 3.2 %collective-permute-done.26 = f32[2,128,512]{2,1,0:T(8,128)S(1)} collective-permute-done((f32[2,128,512]{2,1,0:T(8,128)S(1)}, f32[2,128,512]{2,1,0:T(8,128)S(1)}, u32[]{:S(2)}, u32[]{:S(2)}) %collective-permute-start.26) | collective-permute-done | bytes 524320 | tf_op jit(solution)/shard_map/ppermute | solution.py:17
  97.6 3.7 %collective-permute-done.29 = bf16[2,16,3584]{2,1,0:T(8,128)(2,1)S(1)} collective-permute-done((bf16[2,16,3584]{2,1,0:T(8,128)(2,1)S(1)}, bf16[2,16,3584]{2,1,0:T(8,128)(2,1)S(1)}, u32[]{:S(2)}, u32[]{:S(2)}) %collective-permute-start.29) | collective-permute-done | bytes 229408 | tf_op jit(solution)/shard_map/ppermute | solution.py:17
  101.5 4.2 %collective-permute-start.32 = (bf16[2,16,3584]{2,1,0:T(8,128)(2,1)S(1)}, bf16[2,16,3584]{2,1,0:T(8,128)(2,1)S(1)}, u32[]{:S(2)}, u32[]{:S(2)}) collective-permute-start(bf16[2,16,3584]{2,1,0:T(8,128)(2,1)S(1)} %add_convert_fusion.5), channel_id=1, source_target_pairs={{0,12},{1,5},{4,8},{5,1},{8,4},{9,13},{12,0},{13,9},{2,14},{3,7},{... | collective-permute-start | bytes 688136 | tf_op jit(solution)/shard_map/ppermute | solution.py:33
  105.7 3.0 %collective-permute-start.31 = (bf16[2,2,16,3584]{3,2,0,1:T(8,128)(2,1)S(1)}, bf16[2,2,16,3584]{3,2,0,1:T(8,128)(2,1)S(1)}, u32[]{:S(2)}, u32[]{:S(2)}) collective-permute-start(bf16[2,2,16,3584]{3,2,0,1:T(8,128)(2,1)S(1)} %pad_maximum_fusion.12), channel_id=1, source_target_pairs={{0,4},{1,13},{4,0},{5,9},{8,12},{9,5},{12,8},{13,1},{2,6},{3,15},{... | collective-permute-start | bytes 1376264 | tf_op jit(solution)/shard_map/ppermute | solution.py:33
  109.4 3.0 %collective-permute-start.30 = (bf16[4,64,3584]{2,1,0:T(8,128)(2,1)S(1)}, bf16[4,64,3584]{2,1,0:T(8,128)(2,1)S(1)}, u32[]{:S(2)}, u32[]{:S(2)}) collective-permute-start(bf16[4,64,3584]{2,1,0:T(8,128)(2,1)S(1)} %bitcast.145), channel_id=1, source_target_pairs={{0,1},{1,0},{2,3},{3,2},{4,5},{5,4},{6,7},{7,6},{8,9},{9,8},{10,11... | collective-permute-start | bytes 5505032 | tf_op jit(solution)/shard_map/ppermute | solution.py:17
  118.3 3.7 %collective-permute-done.34 = bf16[2,2,16,3584]{3,2,0,1:T(8,128)(2,1)S(1)} collective-permute-done((bf16[2,2,16,3584]{3,2,0,1:T(8,128)(2,1)S(1)}, bf16[2,2,16,3584]{3,2,0,1:T(8,128)(2,1)S(1)}, u32[]{:S(2)}, u32[]{:S(2)}) %collective-permute-start.34) | collective-permute-done | bytes 458784 | tf_op jit(solution)/shard_map/ppermute | solution.py:33
  126.5 10.6 %shard_map.48 = f32[3584,512]{1,0:T(8,128)} custom-call(bf16[4,64,3584]{2,1,0:T(8,128)(2,1)S(1)} %bitcast.146, bf16[4,64,3584]{2,1,0:T(8,128)(2,1)S(1)} %collective-permute-done.30.refs_1_, bf16[2,64,3584]{2,1,0:T(8,128)(2,1)S(1)} %bitcast.148, bf16[2,64,3584]{2,1,0:T(8,128)(2,1)S(1)} %collective-permute-done.33.refs_3_, bf16[2,64,3584]{2,1,0:T(8,128)(2,1)S(1)} %bitcast.150, ...), custom_call_target="tpu_custom_call" | custom-call | flops 3758096384 | bytes 7340032 | tf_op jit(solution)/shard_map/pallas_call | solution.py:283
  (136 shorter events, 42.0 us)
Async XLA Ops:
  1.5 13.1 %collective-permute-start = (bf16[128,1792]{1,0:T(8,128)(2,1)S(1)}, bf16[128,1792]{1,0:T(8,128)(2,1)S(1)}, u32[]{:S(2)}, u32[]{:S(2)}) collective-permute-start(bf16[128,1792]{1,0:T(8,128)(2,1)S(1)} %convolution_convert_fusion.1), channel_id=1, source_target_pairs={{0,16},{16,0},{1,17},{17,1},{2,18},{18,2},{3,19},{19,3},{4,20},{20... | collective-permute-start | bytes 1376264 | tf_op jit(solution)/shard_map/ppermute | solution.py:17
  4.0 13.2 %collective-permute-start.3 = (bf16[128,1792]{1,0:T(8,128)(2,1)S(1)}, bf16[128,1792]{1,0:T(8,128)(2,1)S(1)}, u32[]{:S(2)}, u32[]{:S(2)}) collective-permute-start(bf16[128,1792]{1,0:T(8,128)(2,1)S(1)} %convolution_convert_fusion.1), channel_id=1, source_target_pairs={{0,96},{32,0},{64,32},{96,64},{1,97},{33,1},{65,33},{97,65},{2,98}... | collective-permute-start | bytes 1376264 | tf_op jit(solution)/shard_map/ppermute | solution.py:21
  6.5 12.0 %collective-permute-start.2 = (bf16[128,1792]{1,0:T(8,128)(2,1)S(1)}, bf16[128,1792]{1,0:T(8,128)(2,1)S(1)}, u32[]{:S(2)}, u32[]{:S(2)}) collective-permute-start(bf16[128,1792]{1,0:T(8,128)(2,1)S(1)} %convolution_convert_fusion.1), channel_id=1, source_target_pairs={{0,32},{32,64},{64,96},{96,0},{1,33},{33,65},{65,97},{97,1},{2,34}... | collective-permute-start | bytes 1376264 | tf_op jit(solution)/shard_map/ppermute | solution.py:21
  11.8 21.2 %collective-permute-start.5 = (bf16[2,64,1024]{2,1,0:T(8,128)(2,1)S(1)}, bf16[2,64,1024]{2,1,0:T(8,128)(2,1)S(1)}, u32[]{:S(2)}, u32[]{:S(2)}) collective-permute-start(bf16[2,64,1024]{2,1,0:T(8,128)(2,1)S(1)} %pad_maximum_fusion.14), channel_id=1, source_target_pairs={{0,4},{1,13},{4,0},{5,9},{8,12},{9,5},{12,8},{13,1},{2,6},{3,15},{... | collective-permute-start | bytes 786440 | tf_op jit(solution)/shard_map/ppermute | solution.py:33
  14.6 25.6 %collective-permute-start.9 = (bf16[128,1792]{1,0:T(8,128)(2,1)S(1)}, bf16[128,1792]{1,0:T(8,128)(2,1)S(1)}, u32[]{:S(2)}, u32[]{:S(2)}) collective-permute-start(bf16[128,1792]{1,0:T(8,128)(2,1)S(1)} %collective-permute-done), channel_id=1, source_target_pairs={{0,96},{32,0},{64,32},{96,64},{1,97},{33,1},{65,33},{97,65},{2,98}... | collective-permute-start | bytes 1376264 | tf_op jit(solution)/shard_map/ppermute | solution.py:21
  17.2 22.8 %collective-permute-start.7 = (bf16[128,1792]{1,0:T(8,128)(2,1)S(1)}, bf16[128,1792]{1,0:T(8,128)(2,1)S(1)}, u32[]{:S(2)}, u32[]{:S(2)}) collective-permute-start(bf16[128,1792]{1,0:T(8,128)(2,1)S(1)} %collective-permute-done), channel_id=1, source_target_pairs={{0,32},{32,64},{64,96},{96,0},{1,33},{33,65},{65,97},{97,1},{2,34}... | collective-permute-start | bytes 1376264 | tf_op jit(solution)/shard_map/ppermute | solution.py:21
  33.0 15.6 %collective-permute-start.11 = (bf16[4,64,1024]{2,1,0:T(8,128)(2,1)S(1)}, bf16[4,64,1024]{2,1,0:T(8,128)(2,1)S(1)}, u32[]{:S(2)}, u32[]{:S(2)}) collective-permute-start(bf16[4,64,1024]{2,1,0:T(8,128)(2,1)S(1)} %get-tuple-element.92), channel_id=1, source_target_pairs={{0,2},{2,0},{1,3},{3,1},{4,6},{6,4},{5,7},{7,5},{8,10},{10,8},{9,1... | collective-permute-start | bytes 1572872 | tf_op jit(solution)/shard_map/ppermute | solution.py:17
  37.2 24.5 %collective-permute-start.6 = (bf16[2,4,16,3584]{3,2,1,0:T(8,128)(2,1)S(1)}, bf16[2,4,16,3584]{3,2,1,0:T(8,128)(2,1)S(1)}, u32[]{:S(2)}, u32[]{:S(2)}) collective-permute-start(bf16[2,4,16,3584]{3,2,1,0:T(8,128)(2,1)S(1)} %get-tuple-element.79), channel_id=1, source_target_pairs={{0,4},{1,13},{4,0},{5,9},{8,12},{9,5},{12,8},{13,1},{2,6},{3,15},{... | collective-permute-start | bytes 2752520 | tf_op jit(solution)/shard_map/ppermute | solution.py:33
  40.1 13.2 %collective-permute-start.8 = (bf16[2,64,1792]{2,1,0:T(8,128)(2,1)S(1)}, bf16[2,64,1792]{2,1,0:T(8,128)(2,1)S(1)}, u32[]{:S(2)}, u32[]{:S(2)}) collective-permute-start(bf16[2,64,1792]{2,1,0:T(8,128)(2,1)S(1)} %pad_maximum_fusion.10), channel_id=1, source_target_pairs={{0,32},{32,64},{64,96},{96,0},{1,33},{33,65},{65,97},{97,1},{2,34}... | collective-permute-start | bytes 1376264 | tf_op jit(solution)/shard_map/ppermute | solution.py:21
  40.3 17.7 %collective-permute-start.10 = (bf16[2,64,1792]{2,1,0:T(8,128)(2,1)S(1)}, bf16[2,64,1792]{2,1,0:T(8,128)(2,1)S(1)}, u32[]{:S(2)}, u32[]{:S(2)}) collective-permute-start(bf16[2,64,1792]{2,1,0:T(8,128)(2,1)S(1)} %pad_maximum_fusion.11), channel_id=1, source_target_pairs={{0,96},{32,0},{64,32},{96,64},{1,97},{33,1},{65,33},{97,65},{2,98}... | collective-permute-start | bytes 1376264 | tf_op jit(solution)/shard_map/ppermute | solution.py:21
  53.5 13.9 %collective-permute-start.15 = (bf16[2,2,16,3584]{3,2,1,0:T(8,128)(2,1)S(1)}, bf16[2,2,16,3584]{3,2,1,0:T(8,128)(2,1)S(1)}, u32[]{:S(2)}, u32[]{:S(2)}) collective-permute-start(bf16[2,2,16,3584]{3,2,1,0:T(8,128)(2,1)S(1)} %get-tuple-element.86), channel_id=1, source_target_pairs={{0,4},{1,13},{4,0},{5,9},{8,12},{9,5},{12,8},{13,1},{2,6},{3,15},{... | collective-permute-start | bytes 1376264 | tf_op jit(solution)/shard_map/ppermute | solution.py:33
  56.1 15.2 %collective-permute-start.20 = (f32[2,2,128,512]{3,2,1,0:T(8,128)S(1)}, f32[2,2,128,512]{3,2,1,0:T(8,128)S(1)}, u32[]{:S(2)}, u32[]{:S(2)}) collective-permute-start(f32[2,2,128,512]{3,2,1,0:T(8,128)S(1)} %shard_map.46), channel_id=1, source_target_pairs={{0,32},{1,97},{32,0},{33,65},{64,96},{65,33},{96,64},{97,1},{2,34}... | collective-permute-start | bytes 3145736 | tf_op jit(solution)/shard_map/ppermute | solution.py:33
  65.3 13.4 %collective-permute-start.19 = (bf16[2,2,16,3584]{3,2,1,0:T(8,128)(2,1)S(1)}, bf16[2,2,16,3584]{3,2,1,0:T(8,128)(2,1)S(1)}, u32[]{:S(2)}, u32[]{:S(2)}) collective-permute-start(bf16[2,2,16,3584]{3,2,1,0:T(8,128)(2,1)S(1)} %get-tuple-element.84), channel_id=1, source_target_pairs={{0,4},{1,13},{4,0},{5,9},{8,12},{9,5},{12,8},{13,1},{2,6},{3,15},{... | collective-permute-start | bytes 1376264 | tf_op jit(solution)/shard_map/ppermute | solution.py:33
  67.4 11.5 %collective-permute-start.18 = (bf16[2,16,3584]{2,1,0:T(8,128)(2,1)S(1)}, bf16[2,16,3584]{2,1,0:T(8,128)(2,1)S(1)}, u32[]{:S(2)}, u32[]{:S(2)}) collective-permute-start(bf16[2,16,3584]{2,1,0:T(8,128)(2,1)S(1)} %fusion.17), channel_id=1, source_target_pairs={{0,12},{1,5},{4,8},{5,1},{8,4},{9,13},{12,0},{13,9},{2,14},{3,7},{... | collective-permute-start | bytes 688136 | tf_op jit(solution)/shard_map/ppermute | solution.py:33
  70.2 9.9 %collective-permute-start.17 = (bf16[4,16,3584]{2,1,0:T(8,128)(2,1)S(1)}, bf16[4,16,3584]{2,1,0:T(8,128)(2,1)S(1)}, u32[]{:S(2)}, u32[]{:S(2)}) collective-permute-start(bf16[4,16,3584]{2,1,0:T(8,128)(2,1)S(1)} %fusion.16), channel_id=1, source_target_pairs={{0,2},{2,0},{1,3},{3,1},{4,6},{6,4},{5,7},{7,5},{8,10},{10,8},{9,1... | collective-permute-start | bytes 1376264 | tf_op jit(solution)/shard_map/ppermute | solution.py:17
  71.4 12.2 %collective-permute-start.24 = (f32[2,128,512]{2,1,0:T(8,128)S(1)}, f32[2,128,512]{2,1,0:T(8,128)S(1)}, u32[]{:S(2)}, u32[]{:S(2)}) collective-permute-start(f32[2,128,512]{2,1,0:T(8,128)S(1)} %fusion.5), channel_id=1, source_target_pairs={{0,96},{1,33},{32,64},{33,1},{64,32},{65,97},{96,0},{97,65},{2,98}... | collective-permute-start | bytes 1572872 | tf_op jit(solution)/shard_map/ppermute | solution.py:33
  83.7 13.3 %collective-permute-start.26 = (f32[2,128,512]{2,1,0:T(8,128)S(1)}, f32[2,128,512]{2,1,0:T(8,128)S(1)}, u32[]{:S(2)}, u32[]{:S(2)}) collective-permute-start(f32[2,128,512]{2,1,0:T(8,128)S(1)} %fusion.4), channel_id=1, source_target_pairs={{0,16},{16,0},{1,17},{17,1},{2,18},{18,2},{3,19},{19,3},{4,20},{20... | collective-permute-start | bytes 1572872 | tf_op jit(solution)/shard_map/ppermute | solution.py:17
  84.1 17.2 %collective-permute-start.29 = (bf16[2,16,3584]{2,1,0:T(8,128)(2,1)S(1)}, bf16[2,16,3584]{2,1,0:T(8,128)(2,1)S(1)}, u32[]{:S(2)}, u32[]{:S(2)}) collective-permute-start(bf16[2,16,3584]{2,1,0:T(8,128)(2,1)S(1)} %fusion.22), channel_id=1, source_target_pairs={{0,2},{2,0},{1,3},{3,1},{4,6},{6,4},{5,7},{7,5},{8,10},{10,8},{9,1... | collective-permute-start | bytes 688136 | tf_op jit(solution)/shard_map/ppermute | solution.py:17
  88.4 17.2 %collective-permute-start.28 = (bf16[2,16,3584]{2,1,0:T(8,128)(2,1)S(1)}, bf16[2,16,3584]{2,1,0:T(8,128)(2,1)S(1)}, u32[]{:S(2)}, u32[]{:S(2)}) collective-permute-start(bf16[2,16,3584]{2,1,0:T(8,128)(2,1)S(1)} %add_convert_fusion.6), channel_id=1, source_target_pairs={{0,12},{1,5},{4,8},{5,1},{8,4},{9,13},{12,0},{13,9},{2,14},{3,7},{... | collective-permute-start | bytes 688136 | tf_op jit(solution)/shard_map/ppermute | solution.py:33
  89.8 19.4 %collective-permute-start.25 = (bf16[2,4,16,3584]{3,2,0,1:T(8,128)(2,1)S(1)}, bf16[2,4,16,3584]{3,2,0,1:T(8,128)(2,1)S(1)}, u32[]{:S(2)}, u32[]{:S(2)}) collective-permute-start(bf16[2,4,16,3584]{3,2,0,1:T(8,128)(2,1)S(1)} %pad_maximum_fusion.5), channel_id=1, source_target_pairs={{0,4},{1,13},{4,0},{5,9},{8,12},{9,5},{12,8},{13,1},{2,6},{3,15},{... | collective-permute-start | bytes 2752520 | tf_op jit(solution)/shard_map/ppermute | solution.py:33
  97.5 11.2 %collective-permute-start.27 = (bf16[2,128,512]{2,1,0:T(8,128)(2,1)S(1)}, bf16[2,128,512]{2,1,0:T(8,128)(2,1)S(1)}, u32[]{:S(2)}, u32[]{:S(2)}) collective-permute-start(bf16[2,128,512]{2,1,0:T(8,128)(2,1)S(1)} %bitcast.167), channel_id=1, source_target_pairs={{0,96},{1,33},{32,64},{33,1},{64,32},{65,97},{96,0},{97,65},{2,98}... | collective-permute-start | bytes 786440 | tf_op jit(solution)/shard_map/ppermute | solution.py:33
  101.5 11.0 %collective-permute-start.32 = (bf16[2,16,3584]{2,1,0:T(8,128)(2,1)S(1)}, bf16[2,16,3584]{2,1,0:T(8,128)(2,1)S(1)}, u32[]{:S(2)}, u32[]{:S(2)}) collective-permute-start(bf16[2,16,3584]{2,1,0:T(8,128)(2,1)S(1)} %add_convert_fusion.5), channel_id=1, source_target_pairs={{0,12},{1,5},{4,8},{5,1},{8,4},{9,13},{12,0},{13,9},{2,14},{3,7},{... | collective-permute-start | bytes 688136 | tf_op jit(solution)/shard_map/ppermute | solution.py:33
  105.7 11.3 %collective-permute-start.31 = (bf16[2,2,16,3584]{3,2,0,1:T(8,128)(2,1)S(1)}, bf16[2,2,16,3584]{3,2,0,1:T(8,128)(2,1)S(1)}, u32[]{:S(2)}, u32[]{:S(2)}) collective-permute-start(bf16[2,2,16,3584]{3,2,0,1:T(8,128)(2,1)S(1)} %pad_maximum_fusion.12), channel_id=1, source_target_pairs={{0,4},{1,13},{4,0},{5,9},{8,12},{9,5},{12,8},{13,1},{2,6},{3,15},{... | collective-permute-start | bytes 1376264 | tf_op jit(solution)/shard_map/ppermute | solution.py:33
  109.4 17.1 %collective-permute-start.30 = (bf16[4,64,3584]{2,1,0:T(8,128)(2,1)S(1)}, bf16[4,64,3584]{2,1,0:T(8,128)(2,1)S(1)}, u32[]{:S(2)}, u32[]{:S(2)}) collective-permute-start(bf16[4,64,3584]{2,1,0:T(8,128)(2,1)S(1)} %bitcast.145), channel_id=1, source_target_pairs={{0,1},{1,0},{2,3},{3,2},{4,5},{5,4},{6,7},{7,6},{8,9},{9,8},{10,11... | collective-permute-start | bytes 5505032 | tf_op jit(solution)/shard_map/ppermute | solution.py:17
  (21 other events, 151.8 us)

commit v4 on v3

--- a/solution.py
+++ b/solution.py
@@ -17,10 +17,6 @@
     return lax.ppermute(v, axis, [(0, 1), (1, 0)])
 
 
-def shift_x(v, by):
-    return lax.ppermute(v, "x", [(i, (i + by) % NX) for i in range(NX)])
-
-
 def near_bit():
     return jnp.where(lax.axis_index("core") == 0, 1, 3)
 
@@ -42,9 +38,10 @@
         self.last = ()
 
     def run(self, step, received, *at_hand):
-        received = lax.optimization_barrier((received,) + self.last)[0]
-        result = step(received, *at_hand)
-        self.last = (result[0] if isinstance(result, tuple) else result,)
+        received = received if isinstance(received, tuple) else (received,)
+        received = lax.optimization_barrier(received + self.last)[: len(received)]
+        result = step(*received, *at_hand)
+        self.last = (result[0] if isinstance(result, (tuple, list)) else result,)
         return result
 
     def put(self, v):
@@ -89,30 +86,58 @@
     return jnp.stack([v.reshape(NC, NY, BLK, k) for v in rows], axis=2).reshape(NC, -1, k)
 
 
+SPANS = 7
+
+
+def rotate_kernel(rows, basis, *refs):
+    have, outs = refs[:-2], refs[-2:]
+    span, half = basis.shape[1] // SPANS, rows.shape[0] // 2
+    for i in range(SPANS):
+        at = pl.ds(i * span, span)
+        part = jnp.dot(rows[...], basis[:, at], preferred_element_type=F32)
+        for h, out in enumerate(outs):
+            mine = part[h * half : (h + 1) * half].astype(out.dtype)
+            if not have:
+                out[:, at] = mine
+                continue
+            old, new, both = (v // NY for v in (have[h].shape[0], half, out.shape[0]))
+            for t in range(NY):
+                out[pl.ds(t * both, old), at] = have[h][pl.ds(t * old, old), at]
+                out[pl.ds(t * both + old, new), at] = mine[t * new : (t + 1) * new]
+
+
+def rotated(rows, basis, have=()):
+    (m, k), n = rows.shape, basis.shape[1]
+    height = m // 2 + (have[0].shape[0] if have else 0)
+    vmem = pl.BlockSpec(memory_space=pltpu.VMEM)
+    return pl.pallas_call(
+        rotate_kernel,
+        in_specs=[vmem] * (2 + len(have)),
+        out_specs=[vmem] * 2,
+        out_shape=[jax.ShapeDtypeStruct((height, n), t) for t in (BF, F32)],
+        compiler_params=pltpu.CompilerParams(vmem_limit_bytes=8 * 1024 * 1024),
+    )(rows, basis, *have)
+
+
 class Chunk:
     def __init__(self, line, basis, n):
-        self.line, self.basis, self.n = line, basis, n
-
-    def dot(self, rows):
-        return jnp.dot(rows, self.basis, preferred_element_type=F32)
+        self.line, self.basis, self.n, self.have = line, basis, n, ()
 
     def shape(self, v):
-        return v.reshape(-1, self.n, BLK, v.shape[-1])
-
-    def multiply(self, join, received, *at_hand):
-        def step(received, *at_hand):
-            rows = to_blocks(join(received, *at_hand))
-            if self.n > 2:
-                return self.dot(rows[0]).astype(BF), rows[1]
-            part = self.dot(rows.reshape(-1, rows.shape[-1]))
-            half = part.shape[0] // 2
-            return part[:half].astype(BF), part[half:]
-
-        send, self.mine = self.line.run(step, received, *at_hand)
-        self.r = swap(self.shape(send), "core")
-        if self.n > 2:
-            self.mine = self.line.run(self.dot, self.mine)
-        self.mine = self.shape(self.mine)
+        return v.reshape(NY, -1, BLK, v.shape[-1])
+
+    def multiply_own(self, rows):
+        rows = to_blocks([rows]).reshape(-1, rows.shape[-1])
+        self.have = self.line.run(lambda v: rotated(v, self.basis), rows)
+
+    def multiply(self, join, *received):
+        def step(*received):
+            rows = to_blocks(join(*received))
+            send, mine = rotated(rows.reshape(-1, rows.shape[-1]), self.basis, self.have)
+            return self.shape(send), self.shape(mine)
+
+        send, self.mine = self.line.run(step, received)
+        self.r = swap(send, "core")
 
     def blocks(self):
         def step(r, mine):
@@ -154,28 +179,28 @@
 
 
 def part_kernel(own_at, other_at, own, other, basis, out):
-    rows = jnp.concatenate([own[0, 0], other[0, 0], own[1, 0], other[1, 0]], axis=0)
+    rows = jnp.concatenate([own[0, 0], other[0, 0], own[0, 1], other[0, 1]], axis=0)
     part = jnp.dot(rows, basis[...], preferred_element_type=F32)
     out[...] = part.reshape(out.shape)
 
 
 def part_sums(own_at, other_at, own, other, basis):
     steps, (k, width) = own_at.shape[0], basis.shape
-    block = (NZH, 1) + own.shape[2:]
+    block = (1,) + own.shape[1:]
     return pl.pallas_call(
         part_kernel,
         grid_spec=pltpu.PrefetchScalarGridSpec(
             num_scalar_prefetch=2,
             grid=(steps,),
             in_specs=[
-                pl.BlockSpec(block, lambda i, own_at, other_at: (0, own_at[i], 0, 0)),
-                pl.BlockSpec(block, lambda i, own_at, other_at: (0, other_at[i], 0, 0)),
+                pl.BlockSpec(block, lambda i, own_at, other_at: (own_at[i], 0, 0, 0)),
+                pl.BlockSpec(block, lambda i, own_at, other_at: (other_at[i], 0, 0, 0)),
                 pl.BlockSpec((k, width), lambda i, own_at, other_at: (0, 0)),
             ],
             out_specs=pl.BlockSpec((1, NZH, SEQ_LEN, width), lambda i, own_at, other_at: (i, 0, 0, 0)),
         ),
         out_shape=jax.ShapeDtypeStruct((steps, NZH, SEQ_LEN, width), F32),
-        compiler_params=pltpu.CompilerParams(vmem_limit_bytes=16 * 1024 * 1024),
+        compiler_params=pltpu.CompilerParams(vmem_limit_bytes=8 * 1024 * 1024),
         cost_estimate=pl.CostEstimate(
             flops=2 * steps * NZH * SEQ_LEN * k * width, bytes_accessed=k * width * 2, transcendentals=0
         ),
@@ -199,7 +224,7 @@
         self.r = swap(self.g, "zh")
 
     def rows_cross(self):
-        self.g = self.line.run(lambda r, u: jnp.stack([u, r]), self.r, self.g)
+        self.g = self.line.run(lambda r, u: jnp.stack([u, r], axis=1), self.r, self.g)
         self.r = swap(self.g, "core")
 
     def multiply(self):
@@ -241,13 +266,11 @@
         self.r = trade(self.g, "x")
 
     def all(self):
-        straight = (lax.axis_index("x") + lax.axis_index("core")) % 2 == 0
+        straight = near_bit() == 1
 
         def step(r, g):
-            before, after = jnp.where(straight, g[1], r[0]), jnp.where(straight, r[0], g[1])
-            return jnp.stack(
-                [g[0, 0], g[0, 1], before[0], after[0], before[1], after[1], r[1, 0], r[1, 1]]
-            )
+            one, three = jnp.where(straight, r[0], g[1]), jnp.where(straight, g[1], r[0])
+            return jnp.stack([g[0, 0], g[0, 1], one[0], three[0], one[1], three[1], r[1, 0], r[1, 1]])
 
         return self.line.run(step, self.r, self.g)
 
@@ -272,7 +295,7 @@
     sizes = tuple(own.shape[0] for own, _ in chunks)
     rows = chunks[0][0].shape[2]
     cols = inputs.shape[2]
-    tile = 512
+    tile = rows // 4
     specs = []
     operands = []
     for own, other in chunks:
@@ -286,7 +309,7 @@
         in_specs=specs,
         out_specs=pl.BlockSpec((tile, cols), lambda i: (i, 0)),
         out_shape=jax.ShapeDtypeStruct((rows, cols), F32),
-        compiler_params=pltpu.CompilerParams(vmem_limit_bytes=32 * 1024 * 1024),
+        compiler_params=pltpu.CompilerParams(vmem_limit_bytes=20 * 1024 * 1024),
         cost_estimate=pl.CostEstimate(
             flops=2 * sum(sizes) * SEQ_LEN * rows * cols, bytes_accessed=rows * cols * 4, transcendentals=0
         ),
@@ -299,44 +322,49 @@
     inputs = Inputs(line, basis_in)
     half = SEQ_LEN // 2
 
+    def by_bit(first, second):
+        straight = near_bit() == 1
+        return [jnp.where(straight, first, second), jnp.where(straight, second, first)]
+
     inputs.rows(layer_inputs)
     own = to_send_order(out_grads)
     near = swap(own, "zl")
-    before, after = shift_x(own, 1), shift_x(own, -1)
+    first, second = trade(own, "x"), trade(own, "x", other=True)
+    one.multiply_own(own)
     inputs.rows_more()
     near = line.put(near)
-    before_n, after_n = shift_x(near, 1), shift_x(near, -1)
-    one.multiply(lambda u, *v: [own, near, *v, u], after, before)
+    first_n, second_n = trade(near, "x"), trade(near, "x", other=True)
+    one.multiply(lambda u, v: [near] + by_bit(u, v), first, second)
     inputs.rows_z()
     one.blocks()
-    low = shift_x(line.run(lambda v, u: jnp.stack([u[:half], v[:half]]), before_n, before), 1)
-    high = shift_x(line.run(lambda v, u: jnp.stack([u[half:], v[half:]]), after_n, after), -1)
-    two.multiply(lambda u, v: [u, v], before_n, after_n)
+    low = trade(line.run(lambda v, u: jnp.stack([u[:half], v[:half]]), second_n, second), "x")
+    high = trade(line.run(lambda v, u: jnp.stack([u[half:], v[half:]]), first_n, first), "x", other=True)
+    two.multiply(by_bit, first_n, second_n)
     inputs.rows_cross()
+    one.reduce()
     two.blocks()
     inputs.multiply()
     three.multiply(lambda v, u: list(jnp.concatenate([u, v], axis=1)), high, low)
-    one.reduce()
+    one.exchange()
     three.blocks()
     two.reduce()
-    one.exchange()
     inputs.reduce()
     three.reduce()
     two.exchange()
     one.gather()
+    three.exchange()
     inputs.exchange()
-    three.exchange()
     two.gather()
     one.gather_more()
-    inputs.gather()
     three.gather()
     two.gather_more()
+    inputs.gather()
+    three.gather_more()
+    one.cross_back()
     inputs.gather_more()
-    one.cross_back()
-    three.gather_more()
     two.cross_back()
+    three.cross_back()
     x_rows = inputs.all()
-    three.cross_back()
     return square_sum([(c.own, c.other) for c in (one, two, three)], x_rows)
 
 

time: 137 us -> 123 us (0.90); the launches traced: 137 us -> 122 us
  matrix products: 19.5 us -> 0.82 us
  Pallas kernels: 13.7 us -> 27.2 us
  starting transfers between devices: 57.5 us -> 46 us
  local copies, waits for them, and re-layouts: 3.05 us -> 6.41 us
    dot_general x4 -> x0, matrix products: 18.7 us -> none  [dot(): return jnp.dot(rows, self.basis, preferred_element_type=F32)]
    pallas_call x0 -> x4, Pallas kernels: none -> 13.9 us  [rotated(): pl.pallas_call(rotate_kernel, in_specs=[vmem] * (2 + len(have)), out_spec...]
    ppermute x6 -> x0, starting transfers between devices: 8.13 us -> none  [shift_x(): return lax.ppermute(v, 'x', [(i, (i + by) % NX) for i in range(NX)])]
    ppermute x6 -> x0, waiting for transfers between devices: 5.01 us -> none  [shift_x(): return lax.ppermute(v, 'x', [(i, (i + by) % NX) for i in range(NX)])]
    ppermute x18 -> x24, starting transfers between devices: 28.1 us -> 23.9 us  [trade(): return lax.ppermute(v, (axis, 'core'), pairs)]
    ppermute x18 -> x24, waiting for transfers between devices: 19.3 us -> 23 us  [trade(): return lax.ppermute(v, (axis, 'core'), pairs)]
    unnamed x24 -> x20, local copies, waits for them, and re-layouts: 2.05 us -> 5.73 us
  transfers between devices with their start and end apart: 37 -> 37, of which waited for: 17 -> 14; matrix products, arithmetic and copies ran while one was open for 18% -> 4% of each run, Pallas kernels for 2% -> 14%
where the time goes in v4:
time: 123 us; the launch traced here: 122 us
  starting transfers between devices  46 us (37%)
  waiting for transfers between devices  37.2 us (30%)
  Pallas kernels  27.2 us (22%)
  local copies, waits for them, and re-layouts  6.41 us (5%)
  other arithmetic  3.51 us (3%)
    ppermute x24, starting transfers between devices, trade(): return lax.ppermute(v, (axis, 'core'), pairs)  23.9 us
    ppermute x24, waiting for transfers between devices, trade(): return lax.ppermute(v, (axis, 'core'), pairs)  23 us
    ppermute x13, starting transfers between devices, swap(): return lax.ppermute(v, axis, [(0, 1), (1, 0)])  22.1 us
    ppermute x13, waiting for transfers between devices, swap(): return lax.ppermute(v, axis, [(0, 1), (1, 0)])  14.2 us
    pallas_call x4, Pallas kernels, rotated(): pl.pallas_call(rotate_kernel, in_specs=[vmem] * (2 + len(have)), out_spec...  13.9 us
    pallas_call x1, Pallas kernels, square_sum(): pl.pallas_call(lambda *refs: square_kernel(sizes, *refs), grid=(rows // t...  10.4 us
    unnamed x20, local copies, waits for them, and re-layouts  5.73 us
    pallas_call x2, Pallas kernels, part_sums(): pl.pallas_call(part_kernel, grid_spec=pltpu.PrefetchScalarGridSpec(num_sc...  2.87 us
  transfers between devices with their start and end apart: 37, of which 14 were waited for; matrix products, arithmetic and copies ran while one was open for 4% of the time, Pallas kernels for 14%

profile of v4, /device:TPU:1, one launch (start us, length us, event | category | flops | bytes accessed | tf_op | source)
XLA Modules:
  0.0 121.6 jit_solution(10844435532346317260)
XLA Ops:
  1.5 2.5 %collective-permute-start = (bf16[128,1792]{1,0:T(8,128)(2,1)S(1)}, bf16[128,1792]{1,0:T(8,128)(2,1)S(1)}, u32[]{:S(2)}, u32[]{:S(2)}) collective-permute-start(bf16[128,1792]{1,0:T(8,128)(2,1)S(1)} %convolution_convert_fusion.rows), channel_id=1, source_target_pairs={{0,16},{16,0},{1,17},{17,1},{2,18},{18,2},{3,19},{19,3},{4,20},{20... | collective-permute-start | bytes 1376264 | tf_op jit(solution)/shard_map/ppermute | solution.py:17
  8.4 4.6 %copy-done.2 = bf16[1792,3584]{1,0:T(8,128)(2,1)S(1)} copy-done((bf16[1792,3584]{1,0:T(8,128)(2,1)S(1)}, bf16[1792,3584]{1,0:T(8,128)(2,1)}, u32[]{:S(2)}) %copy-start.2) | copy-done | bytes 12845080
  15.0 2.0 %collective-permute-start.5 = (bf16[2,64,1024]{2,1,0:T(8,128)(2,1)S(1)}, bf16[2,64,1024]{2,1,0:T(8,128)(2,1)S(1)}, u32[]{:S(2)}, u32[]{:S(2)}) collective-permute-start(bf16[2,64,1024]{2,1,0:T(8,128)(2,1)S(1)} %pad_maximum_fusion.14), channel_id=1, source_target_pairs={{0,4},{1,13},{4,0},{5,9},{8,12},{9,5},{12,8},{13,1},{2,6},{3,15},{... | collective-permute-start | bytes 786440 | tf_op jit(solution)/shard_map/ppermute | solution.py:29
  19.0 5.1 %shard_map.47 = (bf16[256,3584]{1,0:T(8,128)(2,1)S(1)}, f32[256,3584]{1,0:T(8,128)S(1)}) custom-call(bf16[384,1792]{1,0:T(8,128)(2,1)S(1)} %bitcast.137, bf16[1792,3584]{1,0:T(8,128)(2,1)S(1)} %copy-done.3, bf16[64,3584]{1,0:T(8,128)(2,1)S(1)} %get-tuple-element.50.refs_0_, f32[64,3584]{1,0:T(8,128)S(1)} %get-tuple-element.55.refs_1_), custom_call_target="tpu_custom_call" | custom-call | tf_op jit(solution)/shard_map/pallas_call | solution.py:113
  25.7 3.4 %collective-permute-start.7 = (bf16[4,64,1024]{2,1,0:T(8,128)(2,1)S(1)}, bf16[4,64,1024]{2,1,0:T(8,128)(2,1)S(1)}, u32[]{:S(2)}, u32[]{:S(2)}) collective-permute-start(bf16[4,64,1024]{2,1,0:T(8,128)(2,1)S(1)} %get-tuple-element.116), channel_id=1, source_target_pairs={{0,2},{2,0},{1,3},{3,1},{4,6},{6,4},{5,7},{7,5},{8,10},{10,8},{9,1... | collective-permute-start | bytes 1572872 | tf_op jit(solution)/shard_map/ppermute | solution.py:17
  29.8 2.0 %collective-permute-start.6 = (bf16[2,4,16,3584]{3,2,1,0:T(8,128)(2,1)S(1)}, bf16[2,4,16,3584]{3,2,1,0:T(8,128)(2,1)S(1)}, u32[]{:S(2)}, u32[]{:S(2)}) collective-permute-start(bf16[2,4,16,3584]{3,2,1,0:T(8,128)(2,1)S(1)} %get-tuple-element.101), channel_id=1, source_target_pairs={{0,4},{1,13},{4,0},{5,9},{8,12},{9,5},{12,8},{13,1},{2,6},{3,15},{... | collective-permute-start | bytes 2752520 | tf_op jit(solution)/shard_map/ppermute | solution.py:29
  31.9 1.9 %collective-permute-start.12 = (bf16[2,64,1792]{2,1,0:T(8,128)(2,1)S(1)}, bf16[2,64,1792]{2,1,0:T(8,128)(2,1)S(1)}, u32[]{:S(2)}, u32[]{:S(2)}) collective-permute-start(bf16[2,64,1792]{2,1,0:T(8,128)(2,1)S(1)} %pad_maximum_fusion.10), channel_id=1, source_target_pairs={{0,32},{1,97},{32,0},{33,65},{64,96},{65,33},{96,64},{97,1},{2,34}... | collective-permute-start | bytes 1376264 | tf_op jit(solution)/shard_map/ppermute | solution.py:29
  34.1 3.5 %shard_map.48 = (bf16[128,3584]{1,0:T(8,128)(2,1)S(1)}, f32[128,3584]{1,0:T(8,128)S(1)}) custom-call(bf16[256,1792]{1,0:T(8,128)(2,1)S(1)} %bitcast.138, bf16[1792,3584]{1,0:T(8,128)(2,1)S(1)} %copy-done.3), custom_call_target="tpu_custom_call" | custom-call | tf_op jit(solution)/shard_map/pallas_call | solution.py:113
  39.1 2.3 %collective-permute-done.7 = bf16[4,64,1024]{2,1,0:T(8,128)(2,1)S(1)} collective-permute-done((bf16[4,64,1024]{2,1,0:T(8,128)(2,1)S(1)}, bf16[4,64,1024]{2,1,0:T(8,128)(2,1)S(1)}, u32[]{:S(2)}, u32[]{:S(2)}) %collective-permute-start.7) | collective-permute-done | bytes 524320 | tf_op jit(solution)/shard_map/ppermute | solution.py:17
  44.0 2.0 %collective-permute-start.16 = (bf16[2,2,16,3584]{3,2,1,0:T(8,128)(2,1)S(1)}, bf16[2,2,16,3584]{3,2,1,0:T(8,128)(2,1)S(1)}, u32[]{:S(2)}, u32[]{:S(2)}) collective-permute-start(bf16[2,2,16,3584]{3,2,1,0:T(8,128)(2,1)S(1)} %get-tuple-element.106), channel_id=1, source_target_pairs={{0,4},{1,13},{4,0},{5,9},{8,12},{9,5},{12,8},{13,1},{2,6},{3,15},{... | collective-permute-start | bytes 1376264 | tf_op jit(solution)/shard_map/ppermute | solution.py:29
  47.4 1.9 %collective-permute-start.20 = (f32[2,2,128,512]{3,2,1,0:T(8,128)S(1)}, f32[2,2,128,512]{3,2,1,0:T(8,128)S(1)}, u32[]{:S(2)}, u32[]{:S(2)}) collective-permute-start(f32[2,2,128,512]{3,2,1,0:T(8,128)S(1)} %shard_map.49), channel_id=1, source_target_pairs={{0,32},{1,97},{32,0},{33,65},{64,96},{65,33},{96,64},{97,1},{2,34}... | collective-permute-start | bytes 3145736 | tf_op jit(solution)/shard_map/ppermute | solution.py:29
  51.0 3.5 %shard_map.51 = (bf16[128,3584]{1,0:T(8,128)(2,1)S(1)}, f32[128,3584]{1,0:T(8,128)S(1)}) custom-call(bf16[256,1792]{1,0:T(8,128)(2,1)S(1)} %bitcast.139, bf16[1792,3584]{1,0:T(8,128)(2,1)S(1)} %copy-done.3), custom_call_target="tpu_custom_call" | custom-call | tf_op jit(solution)/shard_map/pallas_call | solution.py:113
  55.3 3.1 %collective-permute-start.15 = (bf16[4,16,3584]{2,1,0:T(8,128)(2,1)S(1)}, bf16[4,16,3584]{2,1,0:T(8,128)(2,1)S(1)}, u32[]{:S(2)}, u32[]{:S(2)}) collective-permute-start(bf16[4,16,3584]{2,1,0:T(8,128)(2,1)S(1)} %fusion.16), channel_id=1, source_target_pairs={{0,2},{2,0},{1,3},{3,1},{4,6},{6,4},{5,7},{7,5},{8,10},{10,8},{9,1... | collective-permute-start | bytes 1376264 | tf_op jit(solution)/shard_map/ppermute | solution.py:17
  60.4 2.0 %collective-permute-done.20 = f32[2,2,128,512]{3,2,1,0:T(8,128)S(1)} collective-permute-done((f32[2,2,128,512]{3,2,1,0:T(8,128)S(1)}, f32[2,2,128,512]{3,2,1,0:T(8,128)S(1)}, u32[]{:S(2)}, u32[]{:S(2)}) %collective-permute-start.20) | collective-permute-done | bytes 1048608 | tf_op jit(solution)/shard_map/ppermute | solution.py:29
  62.6 5.6 %collective-permute-done.19 = bf16[2,2,16,3584]{3,2,1,0:T(8,128)(2,1)S(1)} collective-permute-done((bf16[2,2,16,3584]{3,2,1,0:T(8,128)(2,1)S(1)}, bf16[2,2,16,3584]{3,2,1,0:T(8,128)(2,1)S(1)}, u32[]{:S(2)}, u32[]{:S(2)}) %collective-permute-start.19) | collective-permute-done | bytes 458784 | tf_op jit(solution)/shard_map/ppermute | solution.py:29
  68.4 3.6 %collective-permute-start.22 = (bf16[2,16,3584]{2,1,0:T(8,128)(2,1)S(1)}, bf16[2,16,3584]{2,1,0:T(8,128)(2,1)S(1)}, u32[]{:S(2)}, u32[]{:S(2)}) collective-permute-start(bf16[2,16,3584]{2,1,0:T(8,128)(2,1)S(1)} %fusion.21), channel_id=1, source_target_pairs={{0,2},{2,0},{1,3},{3,1},{4,6},{6,4},{5,7},{7,5},{8,10},{10,8},{9,1... | collective-permute-start | bytes 688136 | tf_op jit(solution)/shard_map/ppermute | solution.py:17
  73.8 3.1 %collective-permute-start.26 = (bf16[2,16,3584]{2,1,0:T(8,128)(2,1)S(1)}, bf16[2,16,3584]{2,1,0:T(8,128)(2,1)S(1)}, u32[]{:S(2)}, u32[]{:S(2)}) collective-permute-start(bf16[2,16,3584]{2,1,0:T(8,128)(2,1)S(1)} %fusion.22), channel_id=1, source_target_pairs={{0,2},{2,0},{1,3},{3,1},{4,6},{6,4},{5,7},{7,5},{8,10},{10,8},{9,1... | collective-permute-start | bytes 688136 | tf_op jit(solution)/shard_map/ppermute | solution.py:17
  84.2 8.8 %collective-permute-done.28 = f32[2,128,512]{2,1,0:T(8,128)S(1)} collective-permute-done((f32[2,128,512]{2,1,0:T(8,128)S(1)}, f32[2,128,512]{2,1,0:T(8,128)S(1)}, u32[]{:S(2)}, u32[]{:S(2)}) %collective-permute-start.28) | collective-permute-done | bytes 524320 | tf_op jit(solution)/shard_map/ppermute | solution.py:17
  93.9 4.6 %collective-permute-done.25 = bf16[2,4,16,3584]{3,2,0,1:T(8,128)(2,1)S(1)} collective-permute-done((bf16[2,4,16,3584]{3,2,0,1:T(8,128)(2,1)S(1)}, bf16[2,4,16,3584]{3,2,0,1:T(8,128)(2,1)S(1)}, u32[]{:S(2)}, u32[]{:S(2)}) %collective-permute-start.25) | collective-permute-done | bytes 917536 | tf_op jit(solution)/shard_map/ppermute | solution.py:29
  99.2 2.3 %collective-permute-start.36 = (bf16[2,2,128,512]{3,2,1,0:T(8,128)(2,1)S(1)}, bf16[2,2,128,512]{3,2,1,0:T(8,128)(2,1)S(1)}, u32[]{:S(2)}, u32[]{:S(2)}) collective-permute-start(bf16[2,2,128,512]{3,2,1,0:T(8,128)(2,1)S(1)} %pad_maximum_fusion.9), channel_id=1, source_target_pairs={{0,32},{1,97},{32,0},{33,65},{64,96},{65,33},{96,64},{97,1},{2,34}... | collective-permute-start | bytes 1572872 | tf_op jit(solution)/shard_map/ppermute | solution.py:29
  101.6 2.0 %collective-permute-done.31 = bf16[2,2,16,3584]{3,2,0,1:T(8,128)(2,1)S(1)} collective-permute-done((bf16[2,2,16,3584]{3,2,0,1:T(8,128)(2,1)S(1)}, bf16[2,2,16,3584]{3,2,0,1:T(8,128)(2,1)S(1)}, u32[]{:S(2)}, u32[]{:S(2)}) %collective-permute-start.31) | collective-permute-done | bytes 458784 | tf_op jit(solution)/shard_map/ppermute | solution.py:29
  104.3 4.0 %collective-permute-done.34 = bf16[2,2,16,3584]{3,2,0,1:T(8,128)(2,1)S(1)} collective-permute-done((bf16[2,2,16,3584]{3,2,0,1:T(8,128)(2,1)S(1)}, bf16[2,2,16,3584]{3,2,0,1:T(8,128)(2,1)S(1)}, u32[]{:S(2)}, u32[]{:S(2)}) %collective-permute-start.34) | collective-permute-done | bytes 458784 | tf_op jit(solution)/shard_map/ppermute | solution.py:29
  108.9 2.3 %collective-permute-done.35.refs_5_ = bf16[2,64,3584]{2,1,0:T(8,128)(2,1)S(1)} collective-permute-done((bf16[2,64,3584]{2,1,0:T(8,128)(2,1)S(1)}, bf16[2,64,3584]{2,1,0:T(8,128)(2,1)S(1)}, u32[]{:S(2)}, u32[]{:S(2)}) %collective-permute-start.35) | collective-permute-done | bytes 917536 | tf_op jit(solution)/shard_map/ppermute | solution.py:17
  111.2 10.4 %shard_map.52 = f32[3584,512]{1,0:T(8,128)} custom-call(bf16[4,64,3584]{2,1,0:T(8,128)(2,1)S(1)} %bitcast.136, bf16[4,64,3584]{2,1,0:T(8,128)(2,1)S(1)} %collective-permute-done.30.refs_1_, bf16[2,64,3584]{2,1,0:T(8,128)(2,1)S(1)} %bitcast.141, bf16[2,64,3584]{2,1,0:T(8,128)(2,1)S(1)} %collective-permute-done.33.refs_3_, bf16[2,64,3584]{2,1,0:T(8,128)(2,1)S(1)} %bitcast.143, ...), custom_call_target="tpu_custom_call" | custom-call | flops 3758096384 | bytes 7340032 | tf_op jit(solution)/shard_map/pallas_call | solution.py:306
  (130 shorter events, 34.6 us)
Async XLA Ops:
  1.5 15.5 %collective-permute-start = (bf16[128,1792]{1,0:T(8,128)(2,1)S(1)}, bf16[128,1792]{1,0:T(8,128)(2,1)S(1)}, u32[]{:S(2)}, u32[]{:S(2)}) collective-permute-start(bf16[128,1792]{1,0:T(8,128)(2,1)S(1)} %convolution_convert_fusion.rows), channel_id=1, source_target_pairs={{0,16},{16,0},{1,17},{17,1},{2,18},{18,2},{3,19},{19,3},{4,20},{20... | collective-permute-start | bytes 1376264 | tf_op jit(solution)/shard_map/ppermute | solution.py:17
  4.0 13.9 %collective-permute-start.3 = (bf16[128,1792]{1,0:T(8,128)(2,1)S(1)}, bf16[128,1792]{1,0:T(8,128)(2,1)S(1)}, u32[]{:S(2)}, u32[]{:S(2)}) collective-permute-start(bf16[128,1792]{1,0:T(8,128)(2,1)S(1)} %convolution_convert_fusion.rows), channel_id=1, source_target_pairs={{0,96},{1,33},{32,64},{33,1},{64,32},{65,97},{96,0},{97,65},{2,98}... | collective-permute-start | bytes 1376264 | tf_op jit(solution)/shard_map/ppermute | solution.py:29
  5.2 13.5 %collective-permute-start.2 = (bf16[128,1792]{1,0:T(8,128)(2,1)S(1)}, bf16[128,1792]{1,0:T(8,128)(2,1)S(1)}, u32[]{:S(2)}, u32[]{:S(2)}) collective-permute-start(bf16[128,1792]{1,0:T(8,128)(2,1)S(1)} %convolution_convert_fusion.rows), channel_id=1, source_target_pairs={{0,32},{1,97},{32,0},{33,65},{64,96},{65,33},{96,64},{97,1},{2,34}... | collective-permute-start | bytes 1376264 | tf_op jit(solution)/shard_map/ppermute | solution.py:29
  15.0 10.6 %collective-permute-start.5 = (bf16[2,64,1024]{2,1,0:T(8,128)(2,1)S(1)}, bf16[2,64,1024]{2,1,0:T(8,128)(2,1)S(1)}, u32[]{:S(2)}, u32[]{:S(2)}) collective-permute-start(bf16[2,64,1024]{2,1,0:T(8,128)(2,1)S(1)} %pad_maximum_fusion.14), channel_id=1, source_target_pairs={{0,4},{1,13},{4,0},{5,9},{8,12},{9,5},{12,8},{13,1},{2,6},{3,15},{... | collective-permute-start | bytes 786440 | tf_op jit(solution)/shard_map/ppermute | solution.py:29
  17.0 14.8 %collective-permute-start.9 = (bf16[128,1792]{1,0:T(8,128)(2,1)S(1)}, bf16[128,1792]{1,0:T(8,128)(2,1)S(1)}, u32[]{:S(2)}, u32[]{:S(2)}) collective-permute-start(bf16[128,1792]{1,0:T(8,128)(2,1)S(1)} %collective-permute-done), channel_id=1, source_target_pairs={{0,96},{1,33},{32,64},{33,1},{64,32},{65,97},{96,0},{97,65},{2,98}... | collective-permute-start | bytes 1376264 | tf_op jit(solution)/shard_map/ppermute | solution.py:29
  17.3 16.5 %collective-permute-start.8 = (bf16[128,1792]{1,0:T(8,128)(2,1)S(1)}, bf16[128,1792]{1,0:T(8,128)(2,1)S(1)}, u32[]{:S(2)}, u32[]{:S(2)}) collective-permute-start(bf16[128,1792]{1,0:T(8,128)(2,1)S(1)} %collective-permute-done), channel_id=1, source_target_pairs={{0,32},{1,97},{32,0},{33,65},{64,96},{65,33},{96,64},{97,1},{2,34}... | collective-permute-start | bytes 1376264 | tf_op jit(solution)/shard_map/ppermute | solution.py:29
  25.7 15.7 %collective-permute-start.7 = (bf16[4,64,1024]{2,1,0:T(8,128)(2,1)S(1)}, bf16[4,64,1024]{2,1,0:T(8,128)(2,1)S(1)}, u32[]{:S(2)}, u32[]{:S(2)}) collective-permute-start(bf16[4,64,1024]{2,1,0:T(8,128)(2,1)S(1)} %get-tuple-element.116), channel_id=1, source_target_pairs={{0,2},{2,0},{1,3},{3,1},{4,6},{6,4},{5,7},{7,5},{8,10},{10,8},{9,1... | collective-permute-start | bytes 1572872 | tf_op jit(solution)/shard_map/ppermute | solution.py:17
  29.8 13.8 %collective-permute-start.6 = (bf16[2,4,16,3584]{3,2,1,0:T(8,128)(2,1)S(1)}, bf16[2,4,16,3584]{3,2,1,0:T(8,128)(2,1)S(1)}, u32[]{:S(2)}, u32[]{:S(2)}) collective-permute-start(bf16[2,4,16,3584]{3,2,1,0:T(8,128)(2,1)S(1)} %get-tuple-element.101), channel_id=1, source_target_pairs={{0,4},{1,13},{4,0},{5,9},{8,12},{9,5},{12,8},{13,1},{2,6},{3,15},{... | collective-permute-start | bytes 2752520 | tf_op jit(solution)/shard_map/ppermute | solution.py:29
  31.9 18.9 %collective-permute-start.12 = (bf16[2,64,1792]{2,1,0:T(8,128)(2,1)S(1)}, bf16[2,64,1792]{2,1,0:T(8,128)(2,1)S(1)}, u32[]{:S(2)}, u32[]{:S(2)}) collective-permute-start(bf16[2,64,1792]{2,1,0:T(8,128)(2,1)S(1)} %pad_maximum_fusion.10), channel_id=1, source_target_pairs={{0,32},{1,97},{32,0},{33,65},{64,96},{65,33},{96,64},{97,1},{2,34}... | collective-permute-start | bytes 1376264 | tf_op jit(solution)/shard_map/ppermute | solution.py:29
  33.9 16.9 %collective-permute-start.11 = (bf16[2,64,1792]{2,1,0:T(8,128)(2,1)S(1)}, bf16[2,64,1792]{2,1,0:T(8,128)(2,1)S(1)}, u32[]{:S(2)}, u32[]{:S(2)}) collective-permute-start(bf16[2,64,1792]{2,1,0:T(8,128)(2,1)S(1)} %pad_maximum_fusion.11), channel_id=1, source_target_pairs={{0,96},{1,33},{32,64},{33,1},{64,32},{65,97},{96,0},{97,65},{2,98}... | collective-permute-start | bytes 1376264 | tf_op jit(solution)/shard_map/ppermute | solution.py:29
  43.7 11.4 %collective-permute-start.10 = (bf16[4,16,3584]{2,1,0:T(8,128)(2,1)S(1)}, bf16[4,16,3584]{2,1,0:T(8,128)(2,1)S(1)}, u32[]{:S(2)}, u32[]{:S(2)}) collective-permute-start(bf16[4,16,3584]{2,1,0:T(8,128)(2,1)S(1)} %fusion.6), channel_id=1, source_target_pairs={{0,12},{1,5},{4,8},{5,1},{8,4},{9,13},{12,0},{13,9},{2,14},{3,7},{... | collective-permute-start | bytes 1376264 | tf_op jit(solution)/shard_map/ppermute | solution.py:29
  44.0 16.1 %collective-permute-start.16 = (bf16[2,2,16,3584]{3,2,1,0:T(8,128)(2,1)S(1)}, bf16[2,2,16,3584]{3,2,1,0:T(8,128)(2,1)S(1)}, u32[]{:S(2)}, u32[]{:S(2)}) collective-permute-start(bf16[2,2,16,3584]{3,2,1,0:T(8,128)(2,1)S(1)} %get-tuple-element.106), channel_id=1, source_target_pairs={{0,4},{1,13},{4,0},{5,9},{8,12},{9,5},{12,8},{13,1},{2,6},{3,15},{... | collective-permute-start | bytes 1376264 | tf_op jit(solution)/shard_map/ppermute | solution.py:29
  47.4 14.9 %collective-permute-start.20 = (f32[2,2,128,512]{3,2,1,0:T(8,128)S(1)}, f32[2,2,128,512]{3,2,1,0:T(8,128)S(1)}, u32[]{:S(2)}, u32[]{:S(2)}) collective-permute-start(f32[2,2,128,512]{3,2,1,0:T(8,128)S(1)} %shard_map.49), channel_id=1, source_target_pairs={{0,32},{1,97},{32,0},{33,65},{64,96},{65,33},{96,64},{97,1},{2,34}... | collective-permute-start | bytes 3145736 | tf_op jit(solution)/shard_map/ppermute | solution.py:29
  55.3 16.7 %collective-permute-start.15 = (bf16[4,16,3584]{2,1,0:T(8,128)(2,1)S(1)}, bf16[4,16,3584]{2,1,0:T(8,128)(2,1)S(1)}, u32[]{:S(2)}, u32[]{:S(2)}) collective-permute-start(bf16[4,16,3584]{2,1,0:T(8,128)(2,1)S(1)} %fusion.16), channel_id=1, source_target_pairs={{0,2},{2,0},{1,3},{3,1},{4,6},{6,4},{5,7},{7,5},{8,10},{10,8},{9,1... | collective-permute-start | bytes 1376264 | tf_op jit(solution)/shard_map/ppermute | solution.py:17
  58.5 9.6 %collective-permute-start.19 = (bf16[2,2,16,3584]{3,2,1,0:T(8,128)(2,1)S(1)}, bf16[2,2,16,3584]{3,2,1,0:T(8,128)(2,1)S(1)}, u32[]{:S(2)}, u32[]{:S(2)}) collective-permute-start(bf16[2,2,16,3584]{3,2,1,0:T(8,128)(2,1)S(1)} %get-tuple-element.104), channel_id=1, source_target_pairs={{0,4},{1,13},{4,0},{5,9},{8,12},{9,5},{12,8},{13,1},{2,6},{3,15},{... | collective-permute-start | bytes 1376264 | tf_op jit(solution)/shard_map/ppermute | solution.py:29
  62.5 14.4 %collective-permute-start.23 = (f32[2,128,512]{2,1,0:T(8,128)S(1)}, f32[2,128,512]{2,1,0:T(8,128)S(1)}, u32[]{:S(2)}, u32[]{:S(2)}) collective-permute-start(f32[2,128,512]{2,1,0:T(8,128)S(1)} %fusion.5), channel_id=1, source_target_pairs={{0,96},{1,33},{32,64},{33,1},{64,32},{65,97},{96,0},{97,65},{2,98}... | collective-permute-start | bytes 1572872 | tf_op jit(solution)/shard_map/ppermute | solution.py:29
  68.4 9.7 %collective-permute-start.22 = (bf16[2,16,3584]{2,1,0:T(8,128)(2,1)S(1)}, bf16[2,16,3584]{2,1,0:T(8,128)(2,1)S(1)}, u32[]{:S(2)}, u32[]{:S(2)}) collective-permute-start(bf16[2,16,3584]{2,1,0:T(8,128)(2,1)S(1)} %fusion.21), channel_id=1, source_target_pairs={{0,2},{2,0},{1,3},{3,1},{4,6},{6,4},{5,7},{7,5},{8,10},{10,8},{9,1... | collective-permute-start | bytes 688136 | tf_op jit(solution)/shard_map/ppermute | solution.py:17
  77.0 16.0 %collective-permute-start.28 = (f32[2,128,512]{2,1,0:T(8,128)S(1)}, f32[2,128,512]{2,1,0:T(8,128)S(1)}, u32[]{:S(2)}, u32[]{:S(2)}) collective-permute-start(f32[2,128,512]{2,1,0:T(8,128)S(1)} %fusion.4), channel_id=1, source_target_pairs={{0,16},{16,0},{1,17},{17,1},{2,18},{18,2},{3,19},{19,3},{4,20},{20... | collective-permute-start | bytes 1572872 | tf_op jit(solution)/shard_map/ppermute | solution.py:17
  79.9 18.6 %collective-permute-start.25 = (bf16[2,4,16,3584]{3,2,0,1:T(8,128)(2,1)S(1)}, bf16[2,4,16,3584]{3,2,0,1:T(8,128)(2,1)S(1)}, u32[]{:S(2)}, u32[]{:S(2)}) collective-permute-start(bf16[2,4,16,3584]{3,2,0,1:T(8,128)(2,1)S(1)} %pad_maximum_fusion.5), channel_id=1, source_target_pairs={{0,4},{1,13},{4,0},{5,9},{8,12},{9,5},{12,8},{13,1},{2,6},{3,15},{... | collective-permute-start | bytes 2752520 | tf_op jit(solution)/shard_map/ppermute | solution.py:29
  82.3 11.4 %collective-permute-start.27 = (bf16[2,16,3584]{2,1,0:T(8,128)(2,1)S(1)}, bf16[2,16,3584]{2,1,0:T(8,128)(2,1)S(1)}, u32[]{:S(2)}, u32[]{:S(2)}) collective-permute-start(bf16[2,16,3584]{2,1,0:T(8,128)(2,1)S(1)} %add_convert_fusion.5), channel_id=1, source_target_pairs={{0,12},{1,5},{4,8},{5,1},{8,4},{9,13},{12,0},{13,9},{2,14},{3,7},{... | collective-permute-start | bytes 688136 | tf_op jit(solution)/shard_map/ppermute | solution.py:29
  83.5 20.1 %collective-permute-start.31 = (bf16[2,2,16,3584]{3,2,0,1:T(8,128)(2,1)S(1)}, bf16[2,2,16,3584]{3,2,0,1:T(8,128)(2,1)S(1)}, u32[]{:S(2)}, u32[]{:S(2)}) collective-permute-start(bf16[2,2,16,3584]{3,2,0,1:T(8,128)(2,1)S(1)} %pad_maximum_fusion.12), channel_id=1, source_target_pairs={{0,4},{1,13},{4,0},{5,9},{8,12},{9,5},{12,8},{13,1},{2,6},{3,15},{... | collective-permute-start | bytes 1376264 | tf_op jit(solution)/shard_map/ppermute | solution.py:29
  93.7 14.6 %collective-permute-start.34 = (bf16[2,2,16,3584]{3,2,0,1:T(8,128)(2,1)S(1)}, bf16[2,2,16,3584]{3,2,0,1:T(8,128)(2,1)S(1)}, u32[]{:S(2)}, u32[]{:S(2)}) collective-permute-start(bf16[2,2,16,3584]{3,2,0,1:T(8,128)(2,1)S(1)} %pad_maximum_fusion.13), channel_id=1, source_target_pairs={{0,4},{1,13},{4,0},{5,9},{8,12},{9,5},{12,8},{13,1},{2,6},{3,15},{... | collective-permute-start | bytes 1376264 | tf_op jit(solution)/shard_map/ppermute | solution.py:29
  98.7 12.5 %collective-permute-start.30 = (bf16[4,64,3584]{2,1,0:T(8,128)(2,1)S(1)}, bf16[4,64,3584]{2,1,0:T(8,128)(2,1)S(1)}, u32[]{:S(2)}, u32[]{:S(2)}) collective-permute-start(bf16[4,64,3584]{2,1,0:T(8,128)(2,1)S(1)} %bitcast.135), channel_id=1, source_target_pairs={{0,1},{1,0},{2,3},{3,2},{4,5},{5,4},{6,7},{7,6},{8,9},{9,8},{10,11... | collective-permute-start | bytes 5505032 | tf_op jit(solution)/shard_map/ppermute | solution.py:17
  99.2 9.5 %collective-permute-start.36 = (bf16[2,2,128,512]{3,2,1,0:T(8,128)(2,1)S(1)}, bf16[2,2,128,512]{3,2,1,0:T(8,128)(2,1)S(1)}, u32[]{:S(2)}, u32[]{:S(2)}) collective-permute-start(bf16[2,2,128,512]{3,2,1,0:T(8,128)(2,1)S(1)} %pad_maximum_fusion.9), channel_id=1, source_target_pairs={{0,32},{1,97},{32,0},{33,65},{64,96},{65,33},{96,64},{97,1},{2,34}... | collective-permute-start | bytes 1572872 | tf_op jit(solution)/shard_map/ppermute | solution.py:29
  (19 other events, 104.8 us)

commit v5 on v4

--- a/solution.py
+++ b/solution.py
@@ -1,3 +1,5 @@
+import functools
+
 import jax
 import jax.numpy as jnp
 from jax import lax
@@ -89,32 +91,32 @@
 SPANS = 7
 
 
-def rotate_kernel(rows, basis, *refs):
-    have, outs = refs[:-2], refs[-2:]
-    span, half = basis.shape[1] // SPANS, rows.shape[0] // 2
+def rotate_kernel(count, rows, basis, *refs):
+    have, outs = refs[:-count], refs[-count:]
+    span, height = basis.shape[1] // SPANS, rows.shape[0] // len(outs)
     for i in range(SPANS):
         at = pl.ds(i * span, span)
         part = jnp.dot(rows[...], basis[:, at], preferred_element_type=F32)
         for h, out in enumerate(outs):
-            mine = part[h * half : (h + 1) * half].astype(out.dtype)
+            mine = part[h * height : (h + 1) * height].astype(out.dtype)
             if not have:
                 out[:, at] = mine
                 continue
-            old, new, both = (v // NY for v in (have[h].shape[0], half, out.shape[0]))
+            old, new, both = (v // NY for v in (have[h].shape[0], height, out.shape[0]))
             for t in range(NY):
                 out[pl.ds(t * both, old), at] = have[h][pl.ds(t * old, old), at]
                 out[pl.ds(t * both + old, new), at] = mine[t * new : (t + 1) * new]
 
 
-def rotated(rows, basis, have=()):
+def rotated(rows, basis, types, have=()):
     (m, k), n = rows.shape, basis.shape[1]
-    height = m // 2 + (have[0].shape[0] if have else 0)
+    height = m // len(types) + (have[0].shape[0] if have else 0)
     vmem = pl.BlockSpec(memory_space=pltpu.VMEM)
     return pl.pallas_call(
-        rotate_kernel,
+        functools.partial(rotate_kernel, len(types)),
         in_specs=[vmem] * (2 + len(have)),
-        out_specs=[vmem] * 2,
-        out_shape=[jax.ShapeDtypeStruct((height, n), t) for t in (BF, F32)],
+        out_specs=[vmem] * len(types),
+        out_shape=[jax.ShapeDtypeStruct((height, n), t) for t in types],
         compiler_params=pltpu.CompilerParams(vmem_limit_bytes=8 * 1024 * 1024),
     )(rows, basis, *have)
 
@@ -128,16 +130,20 @@
 
     def multiply_own(self, rows):
         rows = to_blocks([rows]).reshape(-1, rows.shape[-1])
-        self.have = self.line.run(lambda v: rotated(v, self.basis), rows)
+        self.have = self.line.run(lambda v: rotated(v, self.basis, (BF, F32)), rows)
 
     def multiply(self, join, *received):
-        def step(*received):
+        def first(*received):
             rows = to_blocks(join(*received))
-            send, mine = rotated(rows.reshape(-1, rows.shape[-1]), self.basis, self.have)
-            return self.shape(send), self.shape(mine)
-
-        send, self.mine = self.line.run(step, received)
+            return self.shape(rotated(rows[0], self.basis, (BF,), self.have[:1])[0]), rows[1]
+
+        send, rows = self.line.run(first, received)
         self.r = swap(send, "core")
+        last = self.line.last
+        self.mine = self.line.run(
+            lambda v: self.shape(rotated(v, self.basis, (F32,), self.have[1:])[0]), rows
+        )
+        self.line.last = last
 
     def blocks(self):
         def step(r, mine):
@@ -345,8 +351,8 @@
     two.blocks()
     inputs.multiply()
     three.multiply(lambda v, u: list(jnp.concatenate([u, v], axis=1)), high, low)
+    three.blocks()
     one.exchange()
-    three.blocks()
     two.reduce()
     inputs.reduce()
     three.reduce()

time: 123 us -> 121 us (0.984)
  starting transfers between devices: 46 us -> 39.5 us
  waiting for transfers between devices: 37.2 us -> 41.7 us
    ppermute x13, starting transfers between devices: 22.1 us -> 14.5 us  [swap(): return lax.ppermute(v, axis, [(0, 1), (1, 0)])]
    ppermute x24, waiting for transfers between devices: 23 us -> 29 us  [trade(): return lax.ppermute(v, (axis, 'core'), pairs)]
    ppermute x13, waiting for transfers between devices: 14.2 us -> 12.8 us  [swap(): return lax.ppermute(v, axis, [(0, 1), (1, 0)])]
    pallas_call x4 -> x7, Pallas kernels: 13.9 us -> 14.4 us  [rotated(): pl.pallas_call(functools.partial(rotate_kernel, len(types)), in_specs=[vm...]
  transfers between devices with their start and end apart: 37 -> 37, of which waited for: 14 -> 16; matrix products, arithmetic and copies ran while one was open for 4% -> 4% of each run, Pallas kernels for 14% -> 14%
where the time goes in v5:
time: 121 us; the launch traced here: 120 us
  waiting for transfers between devices  41.7 us (34%)
  starting transfers between devices  39.5 us (33%)
  Pallas kernels  27.7 us (23%)
  local copies, waits for them, and re-layouts  6.51 us (5%)
  other arithmetic  3.5 us (3%)
    ppermute x24, waiting for transfers between devices, trade(): return lax.ppermute(v, (axis, 'core'), pairs)  29 us
    ppermute x24, starting transfers between devices, trade(): return lax.ppermute(v, (axis, 'core'), pairs)  25 us
    ppermute x13, starting transfers between devices, swap(): return lax.ppermute(v, axis, [(0, 1), (1, 0)])  14.5 us
    pallas_call x7, Pallas kernels, rotated(): pl.pallas_call(functools.partial(rotate_kernel, len(types)), in_specs=[vm...  14.4 us
    ppermute x13, waiting for transfers between devices, swap(): return lax.ppermute(v, axis, [(0, 1), (1, 0)])  12.8 us
    pallas_call x1, Pallas kernels, square_sum(): pl.pallas_call(lambda *refs: square_kernel(sizes, *refs), grid=(rows // t...  10.4 us
    unnamed x20, local copies, waits for them, and re-layouts  5.73 us
    pallas_call x2, Pallas kernels, part_sums(): pl.pallas_call(part_kernel, grid_spec=pltpu.PrefetchScalarGridSpec(num_sc...  2.88 us
  transfers between devices with their start and end apart: 37, of which 16 were waited for; matrix products, arithmetic and copies ran while one was open for 4% of the time, Pallas kernels for 14%

profile of v5, /device:TPU:1, one launch (start us, length us, event | category | flops | bytes accessed | tf_op | source)
XLA Modules:
  0.0 120.4 jit_solution(317818897892467676)
XLA Ops:
  1.5 2.5 %collective-permute-start = (bf16[128,1792]{1,0:T(8,128)(2,1)S(1)}, bf16[128,1792]{1,0:T(8,128)(2,1)S(1)}, u32[]{:S(2)}, u32[]{:S(2)}) collective-permute-start(bf16[128,1792]{1,0:T(8,128)(2,1)S(1)} %convolution_convert_fusion.rows), channel_id=1, source_target_pairs={{0,16},{16,0},{1,17},{17,1},{2,18},{18,2},{3,19},{19,3},{4,20},{20... | collective-permute-start | bytes 1376264 | tf_op jit(solution)/shard_map/ppermute | solution.py:19
  8.4 4.6 %copy-done.2 = bf16[1792,3584]{1,0:T(8,128)(2,1)S(1)} copy-done((bf16[1792,3584]{1,0:T(8,128)(2,1)S(1)}, bf16[1792,3584]{1,0:T(8,128)(2,1)}, u32[]{:S(2)}) %copy-start.2) | copy-done | bytes 12845080
  15.0 2.0 %collective-permute-start.5 = (bf16[2,64,1024]{2,1,0:T(8,128)(2,1)S(1)}, bf16[2,64,1024]{2,1,0:T(8,128)(2,1)S(1)}, u32[]{:S(2)}, u32[]{:S(2)}) collective-permute-start(bf16[2,64,1024]{2,1,0:T(8,128)(2,1)S(1)} %pad_maximum_fusion.14), channel_id=1, source_target_pairs={{0,4},{1,13},{4,0},{5,9},{8,12},{9,5},{12,8},{13,1},{2,6},{3,15},{... | collective-permute-start | bytes 786440 | tf_op jit(solution)/shard_map/ppermute | solution.py:31
  19.1 2.7 %shard_map.47 = bf16[256,3584]{1,0:T(8,128)(2,1)S(1)} custom-call(bf16[192,1792]{1,0:T(8,128)(2,1)S(1)} %bitcast.145, bf16[1792,3584]{1,0:T(8,128)(2,1)S(1)} %copy-done.3, bf16[64,3584]{1,0:T(8,128)(2,1)S(1)} %get-tuple-element.47.refs_0_), custom_call_target="tpu_custom_call" | custom-call | tf_op jit(solution)/shard_map/pallas_call | solution.py:115
  23.2 3.4 %collective-permute-start.7 = (bf16[4,64,1024]{2,1,0:T(8,128)(2,1)S(1)}, bf16[4,64,1024]{2,1,0:T(8,128)(2,1)S(1)}, u32[]{:S(2)}, u32[]{:S(2)}) collective-permute-start(bf16[4,64,1024]{2,1,0:T(8,128)(2,1)S(1)} %get-tuple-element.116), channel_id=1, source_target_pairs={{0,2},{2,0},{1,3},{3,1},{4,6},{6,4},{5,7},{7,5},{8,10},{10,8},{9,1... | collective-permute-start | bytes 1572872 | tf_op jit(solution)/shard_map/ppermute | solution.py:19
  26.6 2.6 %shard_map.48 = f32[256,3584]{1,0:T(8,128)S(1)} custom-call(bf16[192,1792]{1,0:T(8,128)(2,1)S(1)} %bitcast.144, bf16[1792,3584]{1,0:T(8,128)(2,1)S(1)} %copy-done.3, f32[64,3584]{1,0:T(8,128)S(1)} %get-tuple-element.53.refs_0_), custom_call_target="tpu_custom_call" | custom-call | tf_op jit(solution)/shard_map/pallas_call | solution.py:115
  30.0 2.1 %collective-permute-start.6 = (bf16[2,4,16,3584]{3,2,1,0:T(8,128)(2,1)S(1)}, bf16[2,4,16,3584]{3,2,1,0:T(8,128)(2,1)S(1)}, u32[]{:S(2)}, u32[]{:S(2)}) collective-permute-start(bf16[2,4,16,3584]{3,2,1,0:T(8,128)(2,1)S(1)} %get-tuple-element.95), channel_id=1, source_target_pairs={{0,4},{1,13},{4,0},{5,9},{8,12},{9,5},{12,8},{13,1},{2,6},{3,15},{... | collective-permute-start | bytes 2752520 | tf_op jit(solution)/shard_map/ppermute | solution.py:31
  32.2 1.9 %collective-permute-start.12 = (bf16[2,64,1792]{2,1,0:T(8,128)(2,1)S(1)}, bf16[2,64,1792]{2,1,0:T(8,128)(2,1)S(1)}, u32[]{:S(2)}, u32[]{:S(2)}) collective-permute-start(bf16[2,64,1792]{2,1,0:T(8,128)(2,1)S(1)} %pad_maximum_fusion.10), channel_id=1, source_target_pairs={{0,32},{1,97},{32,0},{33,65},{64,96},{65,33},{96,64},{97,1},{2,34}... | collective-permute-start | bytes 1376264 | tf_op jit(solution)/shard_map/ppermute | solution.py:31
  41.7 2.2 %collective-permute-done.6 = bf16[2,4,16,3584]{3,2,1,0:T(8,128)(2,1)S(1)} collective-permute-done((bf16[2,4,16,3584]{3,2,1,0:T(8,128)(2,1)S(1)}, bf16[2,4,16,3584]{3,2,1,0:T(8,128)(2,1)S(1)}, u32[]{:S(2)}, u32[]{:S(2)}) %collective-permute-start.6) | collective-permute-done | bytes 917536 | tf_op jit(solution)/shard_map/ppermute | solution.py:31
  44.2 2.1 %collective-permute-start.17 = (bf16[2,2,16,3584]{3,2,1,0:T(8,128)(2,1)S(1)}, bf16[2,2,16,3584]{3,2,1,0:T(8,128)(2,1)S(1)}, u32[]{:S(2)}, u32[]{:S(2)}) collective-permute-start(bf16[2,2,16,3584]{3,2,1,0:T(8,128)(2,1)S(1)} %get-tuple-element.102), channel_id=1, source_target_pairs={{0,4},{1,13},{4,0},{5,9},{8,12},{9,5},{12,8},{13,1},{2,6},{3,15},{... | collective-permute-start | bytes 1376264 | tf_op jit(solution)/shard_map/ppermute | solution.py:31
  47.7 1.9 %collective-permute-start.20 = (f32[2,2,128,512]{3,2,1,0:T(8,128)S(1)}, f32[2,2,128,512]{3,2,1,0:T(8,128)S(1)}, u32[]{:S(2)}, u32[]{:S(2)}) collective-permute-start(f32[2,2,128,512]{3,2,1,0:T(8,128)S(1)} %shard_map.51), channel_id=1, source_target_pairs={{0,32},{1,97},{32,0},{33,65},{64,96},{65,33},{96,64},{97,1},{2,34}... | collective-permute-start | bytes 3145736 | tf_op jit(solution)/shard_map/ppermute | solution.py:31
  51.3 1.8 %shard_map.53 = bf16[128,3584]{1,0:T(8,128)(2,1)S(1)} custom-call(bf16[128,1792]{1,0:T(8,128)(2,1)S(1)} %bitcast.147, bf16[1792,3584]{1,0:T(8,128)(2,1)S(1)} %copy-done.3), custom_call_target="tpu_custom_call" | custom-call | tf_op jit(solution)/shard_map/pallas_call | solution.py:115
  55.9 2.4 %collective-permute-start.19 = (bf16[2,2,16,3584]{3,2,1,0:T(8,128)(2,1)S(1)}, bf16[2,2,16,3584]{3,2,1,0:T(8,128)(2,1)S(1)}, u32[]{:S(2)}, u32[]{:S(2)}) collective-permute-start(bf16[2,2,16,3584]{3,2,1,0:T(8,128)(2,1)S(1)} %get-tuple-element.100), channel_id=1, source_target_pairs={{0,4},{1,13},{4,0},{5,9},{8,12},{9,5},{12,8},{13,1},{2,6},{3,15},{... | collective-permute-start | bytes 1376264 | tf_op jit(solution)/shard_map/ppermute | solution.py:31
  59.5 3.2 %collective-permute-done.20 = f32[2,2,128,512]{3,2,1,0:T(8,128)S(1)} collective-permute-done((f32[2,2,128,512]{3,2,1,0:T(8,128)S(1)}, f32[2,2,128,512]{3,2,1,0:T(8,128)S(1)}, u32[]{:S(2)}, u32[]{:S(2)}) %collective-permute-start.20) | collective-permute-done | bytes 1048608 | tf_op jit(solution)/shard_map/ppermute | solution.py:31
  62.9 3.2 %collective-permute-done.19 = bf16[2,2,16,3584]{3,2,1,0:T(8,128)(2,1)S(1)} collective-permute-done((bf16[2,2,16,3584]{3,2,1,0:T(8,128)(2,1)S(1)}, bf16[2,2,16,3584]{3,2,1,0:T(8,128)(2,1)S(1)}, u32[]{:S(2)}, u32[]{:S(2)}) %collective-permute-start.19) | collective-permute-done | bytes 458784 | tf_op jit(solution)/shard_map/ppermute | solution.py:31
  68.3 3.9 %collective-permute-done.16 = bf16[4,16,3584]{2,1,0:T(8,128)(2,1)S(1)} collective-permute-done((bf16[4,16,3584]{2,1,0:T(8,128)(2,1)S(1)}, bf16[4,16,3584]{2,1,0:T(8,128)(2,1)S(1)}, u32[]{:S(2)}, u32[]{:S(2)}) %collective-permute-start.16) | collective-permute-done | bytes 458784 | tf_op jit(solution)/shard_map/ppermute | solution.py:19
  75.6 4.5 %collective-permute-done.21 = bf16[4,16,3584]{2,1,0:T(8,128)(2,1)S(1)} collective-permute-done((bf16[4,16,3584]{2,1,0:T(8,128)(2,1)S(1)}, bf16[4,16,3584]{2,1,0:T(8,128)(2,1)S(1)}, u32[]{:S(2)}, u32[]{:S(2)}) %collective-permute-start.21) | collective-permute-done | bytes 458784 | tf_op jit(solution)/shard_map/ppermute | solution.py:31
  83.5 4.7 %collective-permute-done.28 = f32[2,128,512]{2,1,0:T(8,128)S(1)} collective-permute-done((f32[2,128,512]{2,1,0:T(8,128)S(1)}, f32[2,128,512]{2,1,0:T(8,128)S(1)}, u32[]{:S(2)}, u32[]{:S(2)}) %collective-permute-start.28) | collective-permute-done | bytes 524320 | tf_op jit(solution)/shard_map/ppermute | solution.py:19
  88.9 2.6 %collective-permute-start.34 = (bf16[2,2,16,3584]{3,2,0,1:T(8,128)(2,1)S(1)}, bf16[2,2,16,3584]{3,2,0,1:T(8,128)(2,1)S(1)}, u32[]{:S(2)}, u32[]{:S(2)}) collective-permute-start(bf16[2,2,16,3584]{3,2,0,1:T(8,128)(2,1)S(1)} %pad_maximum_fusion.13), channel_id=1, source_target_pairs={{0,4},{1,13},{4,0},{5,9},{8,12},{9,5},{12,8},{13,1},{2,6},{3,15},{... | collective-permute-start | bytes 1376264 | tf_op jit(solution)/shard_map/ppermute | solution.py:31
  91.6 6.2 %collective-permute-done.25 = bf16[2,4,16,3584]{3,2,0,1:T(8,128)(2,1)S(1)} collective-permute-done((bf16[2,4,16,3584]{3,2,0,1:T(8,128)(2,1)S(1)}, bf16[2,4,16,3584]{3,2,0,1:T(8,128)(2,1)S(1)}, u32[]{:S(2)}, u32[]{:S(2)}) %collective-permute-start.25) | collective-permute-done | bytes 917536 | tf_op jit(solution)/shard_map/ppermute | solution.py:31
  99.0 3.4 %collective-permute-done.31 = bf16[2,2,16,3584]{3,2,0,1:T(8,128)(2,1)S(1)} collective-permute-done((bf16[2,2,16,3584]{3,2,0,1:T(8,128)(2,1)S(1)}, bf16[2,2,16,3584]{3,2,0,1:T(8,128)(2,1)S(1)}, u32[]{:S(2)}, u32[]{:S(2)}) %collective-permute-start.31) | collective-permute-done | bytes 458784 | tf_op jit(solution)/shard_map/ppermute | solution.py:31
  102.6 4.7 %collective-permute-done.34 = bf16[2,2,16,3584]{3,2,0,1:T(8,128)(2,1)S(1)} collective-permute-done((bf16[2,2,16,3584]{3,2,0,1:T(8,128)(2,1)S(1)}, bf16[2,2,16,3584]{3,2,0,1:T(8,128)(2,1)S(1)}, u32[]{:S(2)}, u32[]{:S(2)}) %collective-permute-start.34) | collective-permute-done | bytes 458784 | tf_op jit(solution)/shard_map/ppermute | solution.py:31
  107.7 2.3 %collective-permute-done.35.refs_5_ = bf16[2,64,3584]{2,1,0:T(8,128)(2,1)S(1)} collective-permute-done((bf16[2,64,3584]{2,1,0:T(8,128)(2,1)S(1)}, bf16[2,64,3584]{2,1,0:T(8,128)(2,1)S(1)}, u32[]{:S(2)}, u32[]{:S(2)}) %collective-permute-start.35) | collective-permute-done | bytes 917536 | tf_op jit(solution)/shard_map/ppermute | solution.py:19
  110.0 10.4 %shard_map.55 = f32[3584,512]{1,0:T(8,128)} custom-call(bf16[4,64,3584]{2,1,0:T(8,128)(2,1)S(1)} %bitcast.139, bf16[4,64,3584]{2,1,0:T(8,128)(2,1)S(1)} %collective-permute-done.30.refs_1_, bf16[2,64,3584]{2,1,0:T(8,128)(2,1)S(1)} %bitcast.141, bf16[2,64,3584]{2,1,0:T(8,128)(2,1)S(1)} %collective-permute-done.33.refs_3_, bf16[2,64,3584]{2,1,0:T(8,128)(2,1)S(1)} %bitcast.143, ...), custom_call_target="tpu_custom_call" | custom-call | flops 3758096384 | bytes 7340032 | tf_op jit(solution)/shard_map/pallas_call | solution.py:312
  (134 shorter events, 38.5 us)
Async XLA Ops:
  1.5 15.5 %collective-permute-start = (bf16[128,1792]{1,0:T(8,128)(2,1)S(1)}, bf16[128,1792]{1,0:T(8,128)(2,1)S(1)}, u32[]{:S(2)}, u32[]{:S(2)}) collective-permute-start(bf16[128,1792]{1,0:T(8,128)(2,1)S(1)} %convolution_convert_fusion.rows), channel_id=1, source_target_pairs={{0,16},{16,0},{1,17},{17,1},{2,18},{18,2},{3,19},{19,3},{4,20},{20... | collective-permute-start | bytes 1376264 | tf_op jit(solution)/shard_map/ppermute | solution.py:19
  4.0 13.9 %collective-permute-start.3 = (bf16[128,1792]{1,0:T(8,128)(2,1)S(1)}, bf16[128,1792]{1,0:T(8,128)(2,1)S(1)}, u32[]{:S(2)}, u32[]{:S(2)}) collective-permute-start(bf16[128,1792]{1,0:T(8,128)(2,1)S(1)} %convolution_convert_fusion.rows), channel_id=1, source_target_pairs={{0,96},{1,33},{32,64},{33,1},{64,32},{65,97},{96,0},{97,65},{2,98}... | collective-permute-start | bytes 1376264 | tf_op jit(solution)/shard_map/ppermute | solution.py:31
  5.2 13.5 %collective-permute-start.2 = (bf16[128,1792]{1,0:T(8,128)(2,1)S(1)}, bf16[128,1792]{1,0:T(8,128)(2,1)S(1)}, u32[]{:S(2)}, u32[]{:S(2)}) collective-permute-start(bf16[128,1792]{1,0:T(8,128)(2,1)S(1)} %convolution_convert_fusion.rows), channel_id=1, source_target_pairs={{0,32},{1,97},{32,0},{33,65},{64,96},{65,33},{96,64},{97,1},{2,34}... | collective-permute-start | bytes 1376264 | tf_op jit(solution)/shard_map/ppermute | solution.py:31
  17.0 15.1 %collective-permute-start.9 = (bf16[128,1792]{1,0:T(8,128)(2,1)S(1)}, bf16[128,1792]{1,0:T(8,128)(2,1)S(1)}, u32[]{:S(2)}, u32[]{:S(2)}) collective-permute-start(bf16[128,1792]{1,0:T(8,128)(2,1)S(1)} %collective-permute-done), channel_id=1, source_target_pairs={{0,96},{1,33},{32,64},{33,1},{64,32},{65,97},{96,0},{97,65},{2,98}... | collective-permute-start | bytes 1376264 | tf_op jit(solution)/shard_map/ppermute | solution.py:31
  17.3 16.8 %collective-permute-start.8 = (bf16[128,1792]{1,0:T(8,128)(2,1)S(1)}, bf16[128,1792]{1,0:T(8,128)(2,1)S(1)}, u32[]{:S(2)}, u32[]{:S(2)}) collective-permute-start(bf16[128,1792]{1,0:T(8,128)(2,1)S(1)} %collective-permute-done), channel_id=1, source_target_pairs={{0,32},{1,97},{32,0},{33,65},{64,96},{65,33},{96,64},{97,1},{2,34}... | collective-permute-start | bytes 1376264 | tf_op jit(solution)/shard_map/ppermute | solution.py:31
  23.2 14.7 %collective-permute-start.7 = (bf16[4,64,1024]{2,1,0:T(8,128)(2,1)S(1)}, bf16[4,64,1024]{2,1,0:T(8,128)(2,1)S(1)}, u32[]{:S(2)}, u32[]{:S(2)}) collective-permute-start(bf16[4,64,1024]{2,1,0:T(8,128)(2,1)S(1)} %get-tuple-element.116), channel_id=1, source_target_pairs={{0,2},{2,0},{1,3},{3,1},{4,6},{6,4},{5,7},{7,5},{8,10},{10,8},{9,1... | collective-permute-start | bytes 1572872 | tf_op jit(solution)/shard_map/ppermute | solution.py:19
  30.0 13.8 %collective-permute-start.6 = (bf16[2,4,16,3584]{3,2,1,0:T(8,128)(2,1)S(1)}, bf16[2,4,16,3584]{3,2,1,0:T(8,128)(2,1)S(1)}, u32[]{:S(2)}, u32[]{:S(2)}) collective-permute-start(bf16[2,4,16,3584]{3,2,1,0:T(8,128)(2,1)S(1)} %get-tuple-element.95), channel_id=1, source_target_pairs={{0,4},{1,13},{4,0},{5,9},{8,12},{9,5},{12,8},{13,1},{2,6},{3,15},{... | collective-permute-start | bytes 2752520 | tf_op jit(solution)/shard_map/ppermute | solution.py:31
  32.2 18.9 %collective-permute-start.12 = (bf16[2,64,1792]{2,1,0:T(8,128)(2,1)S(1)}, bf16[2,64,1792]{2,1,0:T(8,128)(2,1)S(1)}, u32[]{:S(2)}, u32[]{:S(2)}) collective-permute-start(bf16[2,64,1792]{2,1,0:T(8,128)(2,1)S(1)} %pad_maximum_fusion.10), channel_id=1, source_target_pairs={{0,32},{1,97},{32,0},{33,65},{64,96},{65,33},{96,64},{97,1},{2,34}... | collective-permute-start | bytes 1376264 | tf_op jit(solution)/shard_map/ppermute | solution.py:31
  34.2 16.9 %collective-permute-start.11 = (bf16[2,64,1792]{2,1,0:T(8,128)(2,1)S(1)}, bf16[2,64,1792]{2,1,0:T(8,128)(2,1)S(1)}, u32[]{:S(2)}, u32[]{:S(2)}) collective-permute-start(bf16[2,64,1792]{2,1,0:T(8,128)(2,1)S(1)} %pad_maximum_fusion.11), channel_id=1, source_target_pairs={{0,96},{1,33},{32,64},{33,1},{64,32},{65,97},{96,0},{97,65},{2,98}... | collective-permute-start | bytes 1376264 | tf_op jit(solution)/shard_map/ppermute | solution.py:31
  38.1 8.2 %collective-permute-start.13 = (bf16[4,2,64,1024]{3,2,1,0:T(8,128)(2,1)S(1)}, bf16[4,2,64,1024]{3,2,1,0:T(8,128)(2,1)S(1)}, u32[]{:S(2)}, u32[]{:S(2)}) collective-permute-start(bf16[4,2,64,1024]{3,2,1,0:T(8,128)(2,1)S(1)} %pad_maximum_fusion.2.own), channel_id=1, source_target_pairs={{0,1},{1,0},{2,3},{3,2},{4,5},{5,4},{6,7},{7,6},{8,9},{9,8},{10,11... | collective-permute-start | bytes 3145736 | tf_op jit(solution)/shard_map/ppermute | solution.py:19
  43.9 14.4 %collective-permute-start.10 = (bf16[4,16,3584]{2,1,0:T(8,128)(2,1)S(1)}, bf16[4,16,3584]{2,1,0:T(8,128)(2,1)S(1)}, u32[]{:S(2)}, u32[]{:S(2)}) collective-permute-start(bf16[4,16,3584]{2,1,0:T(8,128)(2,1)S(1)} %fusion.8), channel_id=1, source_target_pairs={{0,12},{1,5},{4,8},{5,1},{8,4},{9,13},{12,0},{13,9},{2,14},{3,7},{... | collective-permute-start | bytes 1376264 | tf_op jit(solution)/shard_map/ppermute | solution.py:31
  44.2 15.2 %collective-permute-start.17 = (bf16[2,2,16,3584]{3,2,1,0:T(8,128)(2,1)S(1)}, bf16[2,2,16,3584]{3,2,1,0:T(8,128)(2,1)S(1)}, u32[]{:S(2)}, u32[]{:S(2)}) collective-permute-start(bf16[2,2,16,3584]{3,2,1,0:T(8,128)(2,1)S(1)} %get-tuple-element.102), channel_id=1, source_target_pairs={{0,4},{1,13},{4,0},{5,9},{8,12},{9,5},{12,8},{13,1},{2,6},{3,15},{... | collective-permute-start | bytes 1376264 | tf_op jit(solution)/shard_map/ppermute | solution.py:31
  47.7 14.9 %collective-permute-start.20 = (f32[2,2,128,512]{3,2,1,0:T(8,128)S(1)}, f32[2,2,128,512]{3,2,1,0:T(8,128)S(1)}, u32[]{:S(2)}, u32[]{:S(2)}) collective-permute-start(f32[2,2,128,512]{3,2,1,0:T(8,128)S(1)} %shard_map.51), channel_id=1, source_target_pairs={{0,32},{1,97},{32,0},{33,65},{64,96},{65,33},{96,64},{97,1},{2,34}... | collective-permute-start | bytes 3145736 | tf_op jit(solution)/shard_map/ppermute | solution.py:31
  55.9 10.2 %collective-permute-start.19 = (bf16[2,2,16,3584]{3,2,1,0:T(8,128)(2,1)S(1)}, bf16[2,2,16,3584]{3,2,1,0:T(8,128)(2,1)S(1)}, u32[]{:S(2)}, u32[]{:S(2)}) collective-permute-start(bf16[2,2,16,3584]{3,2,1,0:T(8,128)(2,1)S(1)} %get-tuple-element.100), channel_id=1, source_target_pairs={{0,4},{1,13},{4,0},{5,9},{8,12},{9,5},{12,8},{13,1},{2,6},{3,15},{... | collective-permute-start | bytes 1376264 | tf_op jit(solution)/shard_map/ppermute | solution.py:31
  58.5 13.7 %collective-permute-start.16 = (bf16[4,16,3584]{2,1,0:T(8,128)(2,1)S(1)}, bf16[4,16,3584]{2,1,0:T(8,128)(2,1)S(1)}, u32[]{:S(2)}, u32[]{:S(2)}) collective-permute-start(bf16[4,16,3584]{2,1,0:T(8,128)(2,1)S(1)} %fusion.18), channel_id=1, source_target_pairs={{0,2},{2,0},{1,3},{3,1},{4,6},{6,4},{5,7},{7,5},{8,10},{10,8},{9,1... | collective-permute-start | bytes 1376264 | tf_op jit(solution)/shard_map/ppermute | solution.py:19
  62.8 10.9 %collective-permute-start.23 = (f32[2,128,512]{2,1,0:T(8,128)S(1)}, f32[2,128,512]{2,1,0:T(8,128)S(1)}, u32[]{:S(2)}, u32[]{:S(2)}) collective-permute-start(f32[2,128,512]{2,1,0:T(8,128)S(1)} %fusion.5), channel_id=1, source_target_pairs={{0,96},{1,33},{32,64},{33,1},{64,32},{65,97},{96,0},{97,65},{2,98}... | collective-permute-start | bytes 1572872 | tf_op jit(solution)/shard_map/ppermute | solution.py:31
  67.0 8.2 %collective-permute-start.22 = (bf16[2,16,3584]{2,1,0:T(8,128)(2,1)S(1)}, bf16[2,16,3584]{2,1,0:T(8,128)(2,1)S(1)}, u32[]{:S(2)}, u32[]{:S(2)}) collective-permute-start(bf16[2,16,3584]{2,1,0:T(8,128)(2,1)S(1)} %fusion.23), channel_id=1, source_target_pairs={{0,2},{2,0},{1,3},{3,1},{4,6},{6,4},{5,7},{7,5},{8,10},{10,8},{9,1... | collective-permute-start | bytes 688136 | tf_op jit(solution)/shard_map/ppermute | solution.py:19
  73.9 14.3 %collective-permute-start.28 = (f32[2,128,512]{2,1,0:T(8,128)S(1)}, f32[2,128,512]{2,1,0:T(8,128)S(1)}, u32[]{:S(2)}, u32[]{:S(2)}) collective-permute-start(f32[2,128,512]{2,1,0:T(8,128)S(1)} %fusion.4), channel_id=1, source_target_pairs={{0,16},{16,0},{1,17},{17,1},{2,18},{18,2},{3,19},{19,3},{4,20},{20... | collective-permute-start | bytes 1572872 | tf_op jit(solution)/shard_map/ppermute | solution.py:19
  80.2 17.6 %collective-permute-start.25 = (bf16[2,4,16,3584]{3,2,0,1:T(8,128)(2,1)S(1)}, bf16[2,4,16,3584]{3,2,0,1:T(8,128)(2,1)S(1)}, u32[]{:S(2)}, u32[]{:S(2)}) collective-permute-start(bf16[2,4,16,3584]{3,2,0,1:T(8,128)(2,1)S(1)} %pad_maximum_fusion.3), channel_id=1, source_target_pairs={{0,4},{1,13},{4,0},{5,9},{8,12},{9,5},{12,8},{13,1},{2,6},{3,15},{... | collective-permute-start | bytes 2752520 | tf_op jit(solution)/shard_map/ppermute | solution.py:31
  82.7 19.7 %collective-permute-start.31 = (bf16[2,2,16,3584]{3,2,0,1:T(8,128)(2,1)S(1)}, bf16[2,2,16,3584]{3,2,0,1:T(8,128)(2,1)S(1)}, u32[]{:S(2)}, u32[]{:S(2)}) collective-permute-start(bf16[2,2,16,3584]{3,2,0,1:T(8,128)(2,1)S(1)} %pad_maximum_fusion.12), channel_id=1, source_target_pairs={{0,4},{1,13},{4,0},{5,9},{8,12},{9,5},{12,8},{13,1},{2,6},{3,15},{... | collective-permute-start | bytes 1376264 | tf_op jit(solution)/shard_map/ppermute | solution.py:31
  88.7 9.4 %collective-permute-start.32 = (bf16[2,128,512]{2,1,0:T(8,128)(2,1)S(1)}, bf16[2,128,512]{2,1,0:T(8,128)(2,1)S(1)}, u32[]{:S(2)}, u32[]{:S(2)}) collective-permute-start(bf16[2,128,512]{2,1,0:T(8,128)(2,1)S(1)} %bitcast.173), channel_id=1, source_target_pairs={{0,96},{1,33},{32,64},{33,1},{64,32},{65,97},{96,0},{97,65},{2,98}... | collective-permute-start | bytes 786440 | tf_op jit(solution)/shard_map/ppermute | solution.py:31
  88.9 18.4 %collective-permute-start.34 = (bf16[2,2,16,3584]{3,2,0,1:T(8,128)(2,1)S(1)}, bf16[2,2,16,3584]{3,2,0,1:T(8,128)(2,1)S(1)}, u32[]{:S(2)}, u32[]{:S(2)}) collective-permute-start(bf16[2,2,16,3584]{3,2,0,1:T(8,128)(2,1)S(1)} %pad_maximum_fusion.13), channel_id=1, source_target_pairs={{0,4},{1,13},{4,0},{5,9},{8,12},{9,5},{12,8},{13,1},{2,6},{3,15},{... | collective-permute-start | bytes 1376264 | tf_op jit(solution)/shard_map/ppermute | solution.py:31
  98.0 12.0 %collective-permute-start.30 = (bf16[4,64,3584]{2,1,0:T(8,128)(2,1)S(1)}, bf16[4,64,3584]{2,1,0:T(8,128)(2,1)S(1)}, u32[]{:S(2)}, u32[]{:S(2)}) collective-permute-start(bf16[4,64,3584]{2,1,0:T(8,128)(2,1)S(1)} %bitcast.138), channel_id=1, source_target_pairs={{0,1},{1,0},{2,3},{3,2},{4,5},{5,4},{6,7},{7,6},{8,9},{9,8},{10,11... | collective-permute-start | bytes 5505032 | tf_op jit(solution)/shard_map/ppermute | solution.py:19
  98.1 9.4 %collective-permute-start.36 = (bf16[2,2,128,512]{3,2,1,0:T(8,128)(2,1)S(1)}, bf16[2,2,128,512]{3,2,1,0:T(8,128)(2,1)S(1)}, u32[]{:S(2)}, u32[]{:S(2)}) collective-permute-start(bf16[2,2,128,512]{3,2,1,0:T(8,128)(2,1)S(1)} %pad_maximum_fusion.7), channel_id=1, source_target_pairs={{0,32},{1,97},{32,0},{33,65},{64,96},{65,33},{96,64},{97,1},{2,34}... | collective-permute-start | bytes 1572872 | tf_op jit(solution)/shard_map/ppermute | solution.py:31
  (19 other events, 115.7 us)

commit v6 on v5

--- a/solution.py
+++ b/solution.py
@@ -347,9 +347,9 @@
     high = trade(line.run(lambda v, u: jnp.stack([u[half:], v[half:]]), first_n, first), "x", other=True)
     two.multiply(by_bit, first_n, second_n)
     inputs.rows_cross()
-    one.reduce()
     two.blocks()
     inputs.multiply()
+    one.reduce()
     three.multiply(lambda v, u: list(jnp.concatenate([u, v], axis=1)), high, low)
     three.blocks()
     one.exchange()

time: 121 us -> 120 us (level)
  waiting for transfers between devices: 41.7 us -> 31.1 us
  starting transfers between devices: 39.5 us -> 49.1 us
    ppermute x24, waiting for transfers between devices: 29 us -> 21 us  [trade(): return lax.ppermute(v, (axis, 'core'), pairs)]
    ppermute x13, starting transfers between devices: 14.5 us -> 19.9 us  [swap(): return lax.ppermute(v, axis, [(0, 1), (1, 0)])]
    ppermute x24, starting transfers between devices: 25 us -> 29.1 us  [trade(): return lax.ppermute(v, (axis, 'core'), pairs)]
    ppermute x13, waiting for transfers between devices: 12.8 us -> 10.1 us  [swap(): return lax.ppermute(v, axis, [(0, 1), (1, 0)])]
  transfers between devices with their start and end apart: 37 -> 37, of which waited for: 16 -> 14; matrix products, arithmetic and copies ran while one was open for 4% -> 4% of each run, Pallas kernels for 14% -> 15%
where the time goes in v6:
time: 120 us; the launch traced here: 119 us
  starting transfers between devices  49.1 us (41%)
  waiting for transfers between devices  31.1 us (26%)
  Pallas kernels  27.7 us (23%)
  local copies, waits for them, and re-layouts  6.51 us (5%)
  other arithmetic  3.51 us (3%)
    ppermute x24, starting transfers between devices, trade(): return lax.ppermute(v, (axis, 'core'), pairs)  29.1 us
    ppermute x24, waiting for transfers between devices, trade(): return lax.ppermute(v, (axis, 'core'), pairs)  21 us
    ppermute x13, starting transfers between devices, swap(): return lax.ppermute(v, axis, [(0, 1), (1, 0)])  19.9 us
    pallas_call x7, Pallas kernels, rotated(): pl.pallas_call(functools.partial(rotate_kernel, len(types)), in_specs=[vm...  14.4 us
    pallas_call x1, Pallas kernels, square_sum(): pl.pallas_call(lambda *refs: square_kernel(sizes, *refs), grid=(rows // t...  10.4 us
    ppermute x13, waiting for transfers between devices, swap(): return lax.ppermute(v, axis, [(0, 1), (1, 0)])  10.1 us
    unnamed x20, local copies, waits for them, and re-layouts  5.72 us
    pallas_call x2, Pallas kernels, part_sums(): pl.pallas_call(part_kernel, grid_spec=pltpu.PrefetchScalarGridSpec(num_sc...  2.88 us
  transfers between devices with their start and end apart: 37, of which 14 were waited for; matrix products, arithmetic and copies ran while one was open for 4% of the time, Pallas kernels for 15%

profile of v6, /device:TPU:1, one launch (start us, length us, event | category | flops | bytes accessed | tf_op | source)
XLA Modules:
  0.0 119.4 jit_solution(5208211087700216498)
XLA Ops:
  1.5 2.5 %collective-permute-start = (bf16[128,1792]{1,0:T(8,128)(2,1)S(1)}, bf16[128,1792]{1,0:T(8,128)(2,1)S(1)}, u32[]{:S(2)}, u32[]{:S(2)}) collective-permute-start(bf16[128,1792]{1,0:T(8,128)(2,1)S(1)} %convolution_convert_fusion.rows), channel_id=1, source_target_pairs={{0,16},{16,0},{1,17},{17,1},{2,18},{18,2},{3,19},{19,3},{4,20},{20... | collective-permute-start | bytes 1376264 | tf_op jit(solution)/shard_map/ppermute | solution.py:19
  8.4 4.6 %copy-done.2 = bf16[1792,3584]{1,0:T(8,128)(2,1)S(1)} copy-done((bf16[1792,3584]{1,0:T(8,128)(2,1)S(1)}, bf16[1792,3584]{1,0:T(8,128)(2,1)}, u32[]{:S(2)}) %copy-start.2) | copy-done | bytes 12845080
  13.1 1.8 %shard_map.46 = (bf16[64,3584]{1,0:T(8,128)(2,1)S(1)}, f32[64,3584]{1,0:T(8,128)S(1)}) custom-call(bf16[128,1792]{1,0:T(8,128)(2,1)S(1)} %convolution_convert_fusion.rows, bf16[1792,3584]{1,0:T(8,128)(2,1)S(1)} %copy-done.2), custom_call_target="tpu_custom_call" | custom-call | tf_op jit(solution)/shard_map/pallas_call | solution.py:115
  15.0 2.0 %collective-permute-start.5 = (bf16[2,64,1024]{2,1,0:T(8,128)(2,1)S(1)}, bf16[2,64,1024]{2,1,0:T(8,128)(2,1)S(1)}, u32[]{:S(2)}, u32[]{:S(2)}) collective-permute-start(bf16[2,64,1024]{2,1,0:T(8,128)(2,1)S(1)} %pad_maximum_fusion.14), channel_id=1, source_target_pairs={{0,4},{1,13},{4,0},{5,9},{8,12},{9,5},{12,8},{13,1},{2,6},{3,15},{... | collective-permute-start | bytes 786440 | tf_op jit(solution)/shard_map/ppermute | solution.py:31
  19.1 2.7 %shard_map.47 = bf16[256,3584]{1,0:T(8,128)(2,1)S(1)} custom-call(bf16[192,1792]{1,0:T(8,128)(2,1)S(1)} %bitcast.145, bf16[1792,3584]{1,0:T(8,128)(2,1)S(1)} %copy-done.3, bf16[64,3584]{1,0:T(8,128)(2,1)S(1)} %get-tuple-element.47.refs_0_), custom_call_target="tpu_custom_call" | custom-call | tf_op jit(solution)/shard_map/pallas_call | solution.py:115
  23.2 3.4 %collective-permute-start.7 = (bf16[4,64,1024]{2,1,0:T(8,128)(2,1)S(1)}, bf16[4,64,1024]{2,1,0:T(8,128)(2,1)S(1)}, u32[]{:S(2)}, u32[]{:S(2)}) collective-permute-start(bf16[4,64,1024]{2,1,0:T(8,128)(2,1)S(1)} %get-tuple-element.116), channel_id=1, source_target_pairs={{0,2},{2,0},{1,3},{3,1},{4,6},{6,4},{5,7},{7,5},{8,10},{10,8},{9,1... | collective-permute-start | bytes 1572872 | tf_op jit(solution)/shard_map/ppermute | solution.py:19
  26.6 2.6 %shard_map.48 = f32[256,3584]{1,0:T(8,128)S(1)} custom-call(bf16[192,1792]{1,0:T(8,128)(2,1)S(1)} %bitcast.144, bf16[1792,3584]{1,0:T(8,128)(2,1)S(1)} %copy-done.3, f32[64,3584]{1,0:T(8,128)S(1)} %get-tuple-element.53.refs_0_), custom_call_target="tpu_custom_call" | custom-call | tf_op jit(solution)/shard_map/pallas_call | solution.py:115
  30.0 2.1 %collective-permute-start.6 = (bf16[2,4,16,3584]{3,2,1,0:T(8,128)(2,1)S(1)}, bf16[2,4,16,3584]{3,2,1,0:T(8,128)(2,1)S(1)}, u32[]{:S(2)}, u32[]{:S(2)}) collective-permute-start(bf16[2,4,16,3584]{3,2,1,0:T(8,128)(2,1)S(1)} %get-tuple-element.95), channel_id=1, source_target_pairs={{0,4},{1,13},{4,0},{5,9},{8,12},{9,5},{12,8},{13,1},{2,6},{3,15},{... | collective-permute-start | bytes 2752520 | tf_op jit(solution)/shard_map/ppermute | solution.py:31
  32.2 1.9 %collective-permute-start.14 = (bf16[2,64,1792]{2,1,0:T(8,128)(2,1)S(1)}, bf16[2,64,1792]{2,1,0:T(8,128)(2,1)S(1)}, u32[]{:S(2)}, u32[]{:S(2)}) collective-permute-start(bf16[2,64,1792]{2,1,0:T(8,128)(2,1)S(1)} %pad_maximum_fusion.10), channel_id=1, source_target_pairs={{0,32},{1,97},{32,0},{33,65},{64,96},{65,33},{96,64},{97,1},{2,34}... | collective-permute-start | bytes 1376264 | tf_op jit(solution)/shard_map/ppermute | solution.py:31
  41.8 2.1 %collective-permute-start.17 = (bf16[2,2,16,3584]{3,2,1,0:T(8,128)(2,1)S(1)}, bf16[2,2,16,3584]{3,2,1,0:T(8,128)(2,1)S(1)}, u32[]{:S(2)}, u32[]{:S(2)}) collective-permute-start(bf16[2,2,16,3584]{3,2,1,0:T(8,128)(2,1)S(1)} %get-tuple-element.102), channel_id=1, source_target_pairs={{0,4},{1,13},{4,0},{5,9},{8,12},{9,5},{12,8},{13,1},{2,6},{3,15},{... | collective-permute-start | bytes 1376264 | tf_op jit(solution)/shard_map/ppermute | solution.py:31
  45.4 1.9 %collective-permute-start.20 = (f32[2,2,128,512]{3,2,1,0:T(8,128)S(1)}, f32[2,2,128,512]{3,2,1,0:T(8,128)S(1)}, u32[]{:S(2)}, u32[]{:S(2)}) collective-permute-start(f32[2,2,128,512]{3,2,1,0:T(8,128)S(1)} %shard_map.51), channel_id=1, source_target_pairs={{0,32},{1,97},{32,0},{33,65},{64,96},{65,33},{96,64},{97,1},{2,34}... | collective-permute-start | bytes 3145736 | tf_op jit(solution)/shard_map/ppermute | solution.py:31
  49.8 1.8 %shard_map.53 = bf16[128,3584]{1,0:T(8,128)(2,1)S(1)} custom-call(bf16[128,1792]{1,0:T(8,128)(2,1)S(1)} %bitcast.147, bf16[1792,3584]{1,0:T(8,128)(2,1)S(1)} %copy-done.3), custom_call_target="tpu_custom_call" | custom-call | tf_op jit(solution)/shard_map/pallas_call | solution.py:115
  56.7 3.1 %collective-permute-start.16 = (bf16[4,16,3584]{2,1,0:T(8,128)(2,1)S(1)}, bf16[4,16,3584]{2,1,0:T(8,128)(2,1)S(1)}, u32[]{:S(2)}, u32[]{:S(2)}) collective-permute-start(bf16[4,16,3584]{2,1,0:T(8,128)(2,1)S(1)} %fusion.18), channel_id=1, source_target_pairs={{0,2},{2,0},{1,3},{3,1},{4,6},{6,4},{5,7},{7,5},{8,10},{10,8},{9,1... | collective-permute-start | bytes 1376264 | tf_op jit(solution)/shard_map/ppermute | solution.py:19
  60.7 2.6 %collective-permute-done.19 = bf16[2,2,16,3584]{3,2,1,0:T(8,128)(2,1)S(1)} collective-permute-done((bf16[2,2,16,3584]{3,2,1,0:T(8,128)(2,1)S(1)}, bf16[2,2,16,3584]{3,2,1,0:T(8,128)(2,1)S(1)}, u32[]{:S(2)}, u32[]{:S(2)}) %collective-permute-start.19) | collective-permute-done | bytes 458784 | tf_op jit(solution)/shard_map/ppermute | solution.py:31
  65.2 2.7 %collective-permute-start.22 = (bf16[2,16,3584]{2,1,0:T(8,128)(2,1)S(1)}, bf16[2,16,3584]{2,1,0:T(8,128)(2,1)S(1)}, u32[]{:S(2)}, u32[]{:S(2)}) collective-permute-start(bf16[2,16,3584]{2,1,0:T(8,128)(2,1)S(1)} %fusion.23), channel_id=1, source_target_pairs={{0,2},{2,0},{1,3},{3,1},{4,6},{6,4},{5,7},{7,5},{8,10},{10,8},{9,1... | collective-permute-start | bytes 688136 | tf_op jit(solution)/shard_map/ppermute | solution.py:19
  69.4 2.0 %collective-permute-start.21 = (bf16[4,16,3584]{2,1,0:T(8,128)(2,1)S(1)}, bf16[4,16,3584]{2,1,0:T(8,128)(2,1)S(1)}, u32[]{:S(2)}, u32[]{:S(2)}) collective-permute-start(bf16[4,16,3584]{2,1,0:T(8,128)(2,1)S(1)} %add_convert_fusion.1), channel_id=1, source_target_pairs={{0,12},{1,5},{4,8},{5,1},{8,4},{9,13},{12,0},{13,9},{2,14},{3,7},{... | collective-permute-start | bytes 1376264 | tf_op jit(solution)/shard_map/ppermute | solution.py:31
  71.5 3.1 %collective-permute-start.26 = (bf16[2,16,3584]{2,1,0:T(8,128)(2,1)S(1)}, bf16[2,16,3584]{2,1,0:T(8,128)(2,1)S(1)}, u32[]{:S(2)}, u32[]{:S(2)}) collective-permute-start(bf16[2,16,3584]{2,1,0:T(8,128)(2,1)S(1)} %fusion.24), channel_id=1, source_target_pairs={{0,2},{2,0},{1,3},{3,1},{4,6},{6,4},{5,7},{7,5},{8,10},{10,8},{9,1... | collective-permute-start | bytes 688136 | tf_op jit(solution)/shard_map/ppermute | solution.py:19
  81.9 6.0 %collective-permute-done.28 = f32[2,128,512]{2,1,0:T(8,128)S(1)} collective-permute-done((f32[2,128,512]{2,1,0:T(8,128)S(1)}, f32[2,128,512]{2,1,0:T(8,128)S(1)}, u32[]{:S(2)}, u32[]{:S(2)}) %collective-permute-start.28) | collective-permute-done | bytes 524320 | tf_op jit(solution)/shard_map/ppermute | solution.py:19
  88.5 3.1 %collective-permute-start.34 = (bf16[2,2,16,3584]{3,2,0,1:T(8,128)(2,1)S(1)}, bf16[2,2,16,3584]{3,2,0,1:T(8,128)(2,1)S(1)}, u32[]{:S(2)}, u32[]{:S(2)}) collective-permute-start(bf16[2,2,16,3584]{3,2,0,1:T(8,128)(2,1)S(1)} %pad_maximum_fusion.13), channel_id=1, source_target_pairs={{0,4},{1,13},{4,0},{5,9},{8,12},{9,5},{12,8},{13,1},{2,6},{3,15},{... | collective-permute-start | bytes 1376264 | tf_op jit(solution)/shard_map/ppermute | solution.py:31
  91.6 4.8 %collective-permute-done.25 = bf16[2,4,16,3584]{3,2,0,1:T(8,128)(2,1)S(1)} collective-permute-done((bf16[2,4,16,3584]{3,2,0,1:T(8,128)(2,1)S(1)}, bf16[2,4,16,3584]{3,2,0,1:T(8,128)(2,1)S(1)}, u32[]{:S(2)}, u32[]{:S(2)}) %collective-permute-start.25) | collective-permute-done | bytes 917536 | tf_op jit(solution)/shard_map/ppermute | solution.py:31
  97.8 3.5 %collective-permute-done.31 = bf16[2,2,16,3584]{3,2,0,1:T(8,128)(2,1)S(1)} collective-permute-done((bf16[2,2,16,3584]{3,2,0,1:T(8,128)(2,1)S(1)}, bf16[2,2,16,3584]{3,2,0,1:T(8,128)(2,1)S(1)}, u32[]{:S(2)}, u32[]{:S(2)}) %collective-permute-start.31) | collective-permute-done | bytes 458784 | tf_op jit(solution)/shard_map/ppermute | solution.py:31
  101.6 4.7 %collective-permute-done.34 = bf16[2,2,16,3584]{3,2,0,1:T(8,128)(2,1)S(1)} collective-permute-done((bf16[2,2,16,3584]{3,2,0,1:T(8,128)(2,1)S(1)}, bf16[2,2,16,3584]{3,2,0,1:T(8,128)(2,1)S(1)}, u32[]{:S(2)}, u32[]{:S(2)}) %collective-permute-start.34) | collective-permute-done | bytes 458784 | tf_op jit(solution)/shard_map/ppermute | solution.py:31
  106.7 2.3 %collective-permute-done.35.refs_5_ = bf16[2,64,3584]{2,1,0:T(8,128)(2,1)S(1)} collective-permute-done((bf16[2,64,3584]{2,1,0:T(8,128)(2,1)S(1)}, bf16[2,64,3584]{2,1,0:T(8,128)(2,1)S(1)}, u32[]{:S(2)}, u32[]{:S(2)}) %collective-permute-start.35) | collective-permute-done | bytes 917536 | tf_op jit(solution)/shard_map/ppermute | solution.py:19
  109.0 10.4 %shard_map.55 = f32[3584,512]{1,0:T(8,128)} custom-call(bf16[4,64,3584]{2,1,0:T(8,128)(2,1)S(1)} %bitcast.139, bf16[4,64,3584]{2,1,0:T(8,128)(2,1)S(1)} %collective-permute-done.30.refs_1_, bf16[2,64,3584]{2,1,0:T(8,128)(2,1)S(1)} %bitcast.141, bf16[2,64,3584]{2,1,0:T(8,128)(2,1)S(1)} %collective-permute-done.33.refs_3_, bf16[2,64,3584]{2,1,0:T(8,128)(2,1)S(1)} %bitcast.143, ...), custom_call_target="tpu_custom_call" | custom-call | flops 3758096384 | bytes 7340032 | tf_op jit(solution)/shard_map/pallas_call | solution.py:312
  (134 shorter events, 40.9 us)
Async XLA Ops:
  1.5 15.5 %collective-permute-start = (bf16[128,1792]{1,0:T(8,128)(2,1)S(1)}, bf16[128,1792]{1,0:T(8,128)(2,1)S(1)}, u32[]{:S(2)}, u32[]{:S(2)}) collective-permute-start(bf16[128,1792]{1,0:T(8,128)(2,1)S(1)} %convolution_convert_fusion.rows), channel_id=1, source_target_pairs={{0,16},{16,0},{1,17},{17,1},{2,18},{18,2},{3,19},{19,3},{4,20},{20... | collective-permute-start | bytes 1376264 | tf_op jit(solution)/shard_map/ppermute | solution.py:19
  4.0 13.9 %collective-permute-start.3 = (bf16[128,1792]{1,0:T(8,128)(2,1)S(1)}, bf16[128,1792]{1,0:T(8,128)(2,1)S(1)}, u32[]{:S(2)}, u32[]{:S(2)}) collective-permute-start(bf16[128,1792]{1,0:T(8,128)(2,1)S(1)} %convolution_convert_fusion.rows), channel_id=1, source_target_pairs={{0,96},{1,33},{32,64},{33,1},{64,32},{65,97},{96,0},{97,65},{2,98}... | collective-permute-start | bytes 1376264 | tf_op jit(solution)/shard_map/ppermute | solution.py:31
  5.2 13.5 %collective-permute-start.2 = (bf16[128,1792]{1,0:T(8,128)(2,1)S(1)}, bf16[128,1792]{1,0:T(8,128)(2,1)S(1)}, u32[]{:S(2)}, u32[]{:S(2)}) collective-permute-start(bf16[128,1792]{1,0:T(8,128)(2,1)S(1)} %convolution_convert_fusion.rows), channel_id=1, source_target_pairs={{0,32},{1,97},{32,0},{33,65},{64,96},{65,33},{96,64},{97,1},{2,34}... | collective-permute-start | bytes 1376264 | tf_op jit(solution)/shard_map/ppermute | solution.py:31
  17.0 15.1 %collective-permute-start.9 = (bf16[128,1792]{1,0:T(8,128)(2,1)S(1)}, bf16[128,1792]{1,0:T(8,128)(2,1)S(1)}, u32[]{:S(2)}, u32[]{:S(2)}) collective-permute-start(bf16[128,1792]{1,0:T(8,128)(2,1)S(1)} %collective-permute-done), channel_id=1, source_target_pairs={{0,96},{1,33},{32,64},{33,1},{64,32},{65,97},{96,0},{97,65},{2,98}... | collective-permute-start | bytes 1376264 | tf_op jit(solution)/shard_map/ppermute | solution.py:31
  17.3 16.8 %collective-permute-start.8 = (bf16[128,1792]{1,0:T(8,128)(2,1)S(1)}, bf16[128,1792]{1,0:T(8,128)(2,1)S(1)}, u32[]{:S(2)}, u32[]{:S(2)}) collective-permute-start(bf16[128,1792]{1,0:T(8,128)(2,1)S(1)} %collective-permute-done), channel_id=1, source_target_pairs={{0,32},{1,97},{32,0},{33,65},{64,96},{65,33},{96,64},{97,1},{2,34}... | collective-permute-start | bytes 1376264 | tf_op jit(solution)/shard_map/ppermute | solution.py:31
  23.2 14.7 %collective-permute-start.7 = (bf16[4,64,1024]{2,1,0:T(8,128)(2,1)S(1)}, bf16[4,64,1024]{2,1,0:T(8,128)(2,1)S(1)}, u32[]{:S(2)}, u32[]{:S(2)}) collective-permute-start(bf16[4,64,1024]{2,1,0:T(8,128)(2,1)S(1)} %get-tuple-element.116), channel_id=1, source_target_pairs={{0,2},{2,0},{1,3},{3,1},{4,6},{6,4},{5,7},{7,5},{8,10},{10,8},{9,1... | collective-permute-start | bytes 1572872 | tf_op jit(solution)/shard_map/ppermute | solution.py:19
  30.0 18.7 %collective-permute-start.6 = (bf16[2,4,16,3584]{3,2,1,0:T(8,128)(2,1)S(1)}, bf16[2,4,16,3584]{3,2,1,0:T(8,128)(2,1)S(1)}, u32[]{:S(2)}, u32[]{:S(2)}) collective-permute-start(bf16[2,4,16,3584]{3,2,1,0:T(8,128)(2,1)S(1)} %get-tuple-element.95), channel_id=1, source_target_pairs={{0,4},{1,13},{4,0},{5,9},{8,12},{9,5},{12,8},{13,1},{2,6},{3,15},{... | collective-permute-start | bytes 2752520 | tf_op jit(solution)/shard_map/ppermute | solution.py:31
  32.2 17.4 %collective-permute-start.14 = (bf16[2,64,1792]{2,1,0:T(8,128)(2,1)S(1)}, bf16[2,64,1792]{2,1,0:T(8,128)(2,1)S(1)}, u32[]{:S(2)}, u32[]{:S(2)}) collective-permute-start(bf16[2,64,1792]{2,1,0:T(8,128)(2,1)S(1)} %pad_maximum_fusion.10), channel_id=1, source_target_pairs={{0,32},{1,97},{32,0},{33,65},{64,96},{65,33},{96,64},{97,1},{2,34}... | collective-permute-start | bytes 1376264 | tf_op jit(solution)/shard_map/ppermute | solution.py:31
  34.2 15.4 %collective-permute-start.13 = (bf16[2,64,1792]{2,1,0:T(8,128)(2,1)S(1)}, bf16[2,64,1792]{2,1,0:T(8,128)(2,1)S(1)}, u32[]{:S(2)}, u32[]{:S(2)}) collective-permute-start(bf16[2,64,1792]{2,1,0:T(8,128)(2,1)S(1)} %pad_maximum_fusion.11), channel_id=1, source_target_pairs={{0,96},{1,33},{32,64},{33,1},{64,32},{65,97},{96,0},{97,65},{2,98}... | collective-permute-start | bytes 1376264 | tf_op jit(solution)/shard_map/ppermute | solution.py:31
  41.8 17.9 %collective-permute-start.17 = (bf16[2,2,16,3584]{3,2,1,0:T(8,128)(2,1)S(1)}, bf16[2,2,16,3584]{3,2,1,0:T(8,128)(2,1)S(1)}, u32[]{:S(2)}, u32[]{:S(2)}) collective-permute-start(bf16[2,2,16,3584]{3,2,1,0:T(8,128)(2,1)S(1)} %get-tuple-element.102), channel_id=1, source_target_pairs={{0,4},{1,13},{4,0},{5,9},{8,12},{9,5},{12,8},{13,1},{2,6},{3,15},{... | collective-permute-start | bytes 1376264 | tf_op jit(solution)/shard_map/ppermute | solution.py:31
  45.4 15.2 %collective-permute-start.20 = (f32[2,2,128,512]{3,2,1,0:T(8,128)S(1)}, f32[2,2,128,512]{3,2,1,0:T(8,128)S(1)}, u32[]{:S(2)}, u32[]{:S(2)}) collective-permute-start(f32[2,2,128,512]{3,2,1,0:T(8,128)S(1)} %shard_map.51), channel_id=1, source_target_pairs={{0,32},{1,97},{32,0},{33,65},{64,96},{65,33},{96,64},{97,1},{2,34}... | collective-permute-start | bytes 3145736 | tf_op jit(solution)/shard_map/ppermute | solution.py:31
  54.4 8.9 %collective-permute-start.19 = (bf16[2,2,16,3584]{3,2,1,0:T(8,128)(2,1)S(1)}, bf16[2,2,16,3584]{3,2,1,0:T(8,128)(2,1)S(1)}, u32[]{:S(2)}, u32[]{:S(2)}) collective-permute-start(bf16[2,2,16,3584]{3,2,1,0:T(8,128)(2,1)S(1)} %get-tuple-element.100), channel_id=1, source_target_pairs={{0,4},{1,13},{4,0},{5,9},{8,12},{9,5},{12,8},{13,1},{2,6},{3,15},{... | collective-permute-start | bytes 1376264 | tf_op jit(solution)/shard_map/ppermute | solution.py:31
  56.7 12.5 %collective-permute-start.16 = (bf16[4,16,3584]{2,1,0:T(8,128)(2,1)S(1)}, bf16[4,16,3584]{2,1,0:T(8,128)(2,1)S(1)}, u32[]{:S(2)}, u32[]{:S(2)}) collective-permute-start(bf16[4,16,3584]{2,1,0:T(8,128)(2,1)S(1)} %fusion.18), channel_id=1, source_target_pairs={{0,2},{2,0},{1,3},{3,1},{4,6},{6,4},{5,7},{7,5},{8,10},{10,8},{9,1... | collective-permute-start | bytes 1376264 | tf_op jit(solution)/shard_map/ppermute | solution.py:19
  60.7 14.0 %collective-permute-start.23 = (f32[2,128,512]{2,1,0:T(8,128)S(1)}, f32[2,128,512]{2,1,0:T(8,128)S(1)}, u32[]{:S(2)}, u32[]{:S(2)}) collective-permute-start(f32[2,128,512]{2,1,0:T(8,128)S(1)} %fusion.5), channel_id=1, source_target_pairs={{0,96},{1,33},{32,64},{33,1},{64,32},{65,97},{96,0},{97,65},{2,98}... | collective-permute-start | bytes 1572872 | tf_op jit(solution)/shard_map/ppermute | solution.py:31
  65.2 9.7 %collective-permute-start.22 = (bf16[2,16,3584]{2,1,0:T(8,128)(2,1)S(1)}, bf16[2,16,3584]{2,1,0:T(8,128)(2,1)S(1)}, u32[]{:S(2)}, u32[]{:S(2)}) collective-permute-start(bf16[2,16,3584]{2,1,0:T(8,128)(2,1)S(1)} %fusion.23), channel_id=1, source_target_pairs={{0,2},{2,0},{1,3},{3,1},{4,6},{6,4},{5,7},{7,5},{8,10},{10,8},{9,1... | collective-permute-start | bytes 688136 | tf_op jit(solution)/shard_map/ppermute | solution.py:19
  69.4 8.2 %collective-permute-start.21 = (bf16[4,16,3584]{2,1,0:T(8,128)(2,1)S(1)}, bf16[4,16,3584]{2,1,0:T(8,128)(2,1)S(1)}, u32[]{:S(2)}, u32[]{:S(2)}) collective-permute-start(bf16[4,16,3584]{2,1,0:T(8,128)(2,1)S(1)} %add_convert_fusion.1), channel_id=1, source_target_pairs={{0,12},{1,5},{4,8},{5,1},{8,4},{9,13},{12,0},{13,9},{2,14},{3,7},{... | collective-permute-start | bytes 1376264 | tf_op jit(solution)/shard_map/ppermute | solution.py:31
  74.8 13.0 %collective-permute-start.28 = (f32[2,128,512]{2,1,0:T(8,128)S(1)}, f32[2,128,512]{2,1,0:T(8,128)S(1)}, u32[]{:S(2)}, u32[]{:S(2)}) collective-permute-start(f32[2,128,512]{2,1,0:T(8,128)S(1)} %fusion.4), channel_id=1, source_target_pairs={{0,16},{16,0},{1,17},{17,1},{2,18},{18,2},{3,19},{19,3},{4,20},{20... | collective-permute-start | bytes 1572872 | tf_op jit(solution)/shard_map/ppermute | solution.py:19
  77.7 18.8 %collective-permute-start.25 = (bf16[2,4,16,3584]{3,2,0,1:T(8,128)(2,1)S(1)}, bf16[2,4,16,3584]{3,2,0,1:T(8,128)(2,1)S(1)}, u32[]{:S(2)}, u32[]{:S(2)}) collective-permute-start(bf16[2,4,16,3584]{3,2,0,1:T(8,128)(2,1)S(1)} %pad_maximum_fusion.3), channel_id=1, source_target_pairs={{0,4},{1,13},{4,0},{5,9},{8,12},{9,5},{12,8},{13,1},{2,6},{3,15},{... | collective-permute-start | bytes 2752520 | tf_op jit(solution)/shard_map/ppermute | solution.py:31
  78.9 9.6 %collective-permute-start.27 = (bf16[2,16,3584]{2,1,0:T(8,128)(2,1)S(1)}, bf16[2,16,3584]{2,1,0:T(8,128)(2,1)S(1)}, u32[]{:S(2)}, u32[]{:S(2)}) collective-permute-start(bf16[2,16,3584]{2,1,0:T(8,128)(2,1)S(1)} %add_convert_fusion.5), channel_id=1, source_target_pairs={{0,12},{1,5},{4,8},{5,1},{8,4},{9,13},{12,0},{13,9},{2,14},{3,7},{... | collective-permute-start | bytes 688136 | tf_op jit(solution)/shard_map/ppermute | solution.py:31
  80.4 21.0 %collective-permute-start.31 = (bf16[2,2,16,3584]{3,2,0,1:T(8,128)(2,1)S(1)}, bf16[2,2,16,3584]{3,2,0,1:T(8,128)(2,1)S(1)}, u32[]{:S(2)}, u32[]{:S(2)}) collective-permute-start(bf16[2,2,16,3584]{3,2,0,1:T(8,128)(2,1)S(1)} %pad_maximum_fusion.12), channel_id=1, source_target_pairs={{0,4},{1,13},{4,0},{5,9},{8,12},{9,5},{12,8},{13,1},{2,6},{3,15},{... | collective-permute-start | bytes 1376264 | tf_op jit(solution)/shard_map/ppermute | solution.py:31
  88.4 8.4 %collective-permute-start.32 = (bf16[2,128,512]{2,1,0:T(8,128)(2,1)S(1)}, bf16[2,128,512]{2,1,0:T(8,128)(2,1)S(1)}, u32[]{:S(2)}, u32[]{:S(2)}) collective-permute-start(bf16[2,128,512]{2,1,0:T(8,128)(2,1)S(1)} %bitcast.173), channel_id=1, source_target_pairs={{0,96},{1,33},{32,64},{33,1},{64,32},{65,97},{96,0},{97,65},{2,98}... | collective-permute-start | bytes 786440 | tf_op jit(solution)/shard_map/ppermute | solution.py:31
  88.5 17.8 %collective-permute-start.34 = (bf16[2,2,16,3584]{3,2,0,1:T(8,128)(2,1)S(1)}, bf16[2,2,16,3584]{3,2,0,1:T(8,128)(2,1)S(1)}, u32[]{:S(2)}, u32[]{:S(2)}) collective-permute-start(bf16[2,2,16,3584]{3,2,0,1:T(8,128)(2,1)S(1)} %pad_maximum_fusion.13), channel_id=1, source_target_pairs={{0,4},{1,13},{4,0},{5,9},{8,12},{9,5},{12,8},{13,1},{2,6},{3,15},{... | collective-permute-start | bytes 1376264 | tf_op jit(solution)/shard_map/ppermute | solution.py:31
  96.7 12.3 %collective-permute-start.30 = (bf16[4,64,3584]{2,1,0:T(8,128)(2,1)S(1)}, bf16[4,64,3584]{2,1,0:T(8,128)(2,1)S(1)}, u32[]{:S(2)}, u32[]{:S(2)}) collective-permute-start(bf16[4,64,3584]{2,1,0:T(8,128)(2,1)S(1)} %bitcast.138), channel_id=1, source_target_pairs={{0,1},{1,0},{2,3},{3,2},{4,5},{5,4},{6,7},{7,6},{8,9},{9,8},{10,11... | collective-permute-start | bytes 5505032 | tf_op jit(solution)/shard_map/ppermute | solution.py:19
  96.8 9.7 %collective-permute-start.36 = (bf16[2,2,128,512]{3,2,1,0:T(8,128)(2,1)S(1)}, bf16[2,2,128,512]{3,2,1,0:T(8,128)(2,1)S(1)}, u32[]{:S(2)}, u32[]{:S(2)}) collective-permute-start(bf16[2,2,128,512]{3,2,1,0:T(8,128)(2,1)S(1)} %pad_maximum_fusion.7), channel_id=1, source_target_pairs={{0,32},{1,97},{32,0},{33,65},{64,96},{65,33},{96,64},{97,1},{2,34}... | collective-permute-start | bytes 1572872 | tf_op jit(solution)/shard_map/ppermute | solution.py:31
  (19 other events, 107.7 us)
